TPU v7x, 32 devices: a whole 2x2x4 slice. The times are simulated.
32 devices in a mesh: seq: 8 (over y, x, core), head: 4 (over z).
Axes of the slice: x: 2, y: 2, z: 4, core: 2. Of those that a mesh axis runs over, the one named last changes fastest.
Arguments:
- tokens: bfloat16 [32768, 768], P(('seq', 'head')), may hold values from -6 to 6
- lengths: int32 [8, 32], P('seq'), may hold values from 1 to 512, 4096 in all within a row
- cotangent: bfloat16 [32768, 768], P(('seq', 'head')), may hold values from -12 to 12
- w_query: bfloat16 [768, 768], replicated, may hold values from -0.21875 to 0.21875
- w_key: bfloat16 [768, 768], replicated, may hold values from -0.21875 to 0.21875
- w_value: bfloat16 [768, 768], replicated, may hold values from -0.21875 to 0.21875
- w_output: bfloat16 [768, 768], replicated, may hold values from -1.25 to 1.25
- vera_down: bfloat16 [768, 1024], replicated, may hold values from -0.21875 to 0.21875
- vera_up: bfloat16 [1024, 768], replicated, may hold values from -0.1875 to 0.1875
- query_scale: float32 [1024], replicated, may hold values from 0.5 to 1.5
- query_bias: float32 [768], replicated, may hold values from -4 to 4
- value_scale: float32 [1024], replicated, may hold values from 0.5 to 1.5
- value_bias: float32 [768], replicated, may hold values from -4 to 4
- hidden_in: bfloat16 [768, 3072], P(None, ('seq', 'head')), may hold values from -0.21875 to 0.21875
- hidden_out: bfloat16 [768, 3072], P(None, ('seq', 'head')), may hold values from -0.109375 to 0.109375
Outputs:
- layer_output: bfloat16 [32768, 768], P(('seq', 'head'))
- token_grad: bfloat16 [32768, 768], P(('seq', 'head'))
- query_scale_grad: float32 [1024], replicated
- query_bias_grad: float32 [768], replicated
- value_scale_grad: float32 [1024], replicated
- value_bias_grad: float32 [768], replicated
Inputs may be any that keep to these rules, and one draw needn't show every extreme that they name: `lengths`: each row sums to 4096, and its longest sequence has exactly 512 tokens.
All inputs are finite; a program needn't handle non-finite values.
Results may differ from a plain program's by a relative error of at most 0.015.
Values may be sent and summed in bfloat16 or wider, within the bound.
A program may use at most 192 MiB of HBM per device.

v0:
```python
import jax
import jax.numpy as jnp
from jax import lax
from jax.sharding import PartitionSpec as P

HEAD_DIM = 64
SEQ_MOST = 512


EPSILON = 1e-05
MASKED = -1000000000.0
CONTRACT_LAST = (((1,), (1,)), ((), ()))


def gelu_exact(values):
    return jax.nn.gelu(values, approximate=False)


def gelu_back(preact, upstream):
    unused, pullback = jax.vjp(gelu_exact, preact)
    return pullback(upstream)[0]


def layer_norm(values):
    center = values - jnp.mean(values, axis=-1, keepdims=True)
    variance = jnp.mean(center * center, axis=-1, keepdims=True)
    inverse = lax.rsqrt(variance + EPSILON)
    return (center * inverse, inverse)


def norm_back(gradient, normed, inverse):
    centered = gradient - jnp.mean(gradient, axis=-1, keepdims=True)
    return inverse * (centered - normed * jnp.mean(gradient * normed, axis=-1, keepdims=True))


def segment_ids(lengths, group_rows):
    seq_ends = jnp.cumsum(lengths)
    positions = jnp.arange(group_rows, dtype=jnp.int32)
    return jnp.sum((positions[:, None] >= seq_ends[None, :]).astype(jnp.int32), axis=1)


def block_scores(queries, key_pad, segment, segment_pad, offset, block, head_count):
    window = block + 2 * SEQ_MOST
    query_block = lax.dynamic_slice_in_dim(queries, offset, block, 0).reshape(
        block, head_count, HEAD_DIM
    )
    key_block = lax.dynamic_slice_in_dim(key_pad, offset, window, 0).reshape(
        window, head_count, HEAD_DIM
    )
    scores = jnp.einsum(
        "qhd,khd->hqk", query_block, key_block, preferred_element_type=jnp.float32
    ) * HEAD_DIM ** (-0.5)
    own_segment = lax.dynamic_slice_in_dim(segment, offset, block, 0)
    key_segment = lax.dynamic_slice_in_dim(segment_pad, offset, window, 0)
    allowed = own_segment[:, None] == key_segment[None, :]
    return (query_block, key_block, jnp.where(allowed[None], scores, MASKED))


def attention_forward(queries, key_pad, value_pad, segment, segment_pad, block):
    row_count, columns = queries.shape
    head_count = columns // HEAD_DIM
    window = block + 2 * SEQ_MOST

    def one_block(block_index):
        offset = block_index * block
        query_block, key_block, scores = block_scores(
            queries, key_pad, segment, segment_pad, offset, block, head_count
        )
        value_block = lax.dynamic_slice_in_dim(value_pad, offset, window, 0).reshape(
            window, head_count, HEAD_DIM
        )
        highest = jnp.max(scores, axis=-1, keepdims=True)
        exponent = jnp.exp(scores - highest)
        totals = jnp.sum(exponent, axis=-1, keepdims=True)
        weights = (exponent / totals).astype(jnp.bfloat16)
        context = jnp.einsum(
            "hqk,khd->qhd", weights, value_block, preferred_element_type=jnp.float32
        )
        return (
            context.reshape(block, columns).astype(jnp.bfloat16),
            (highest + jnp.log(totals))[..., 0],
        )

    context, logsum = lax.map(one_block, jnp.arange(row_count // block, dtype=jnp.int32))
    return (context.reshape(row_count, columns), logsum)


def attention_backward(
    queries, key_pad, value_pad, segment, segment_pad, logsum, grad_context, block
):
    row_count, columns = queries.shape
    head_count = columns // HEAD_DIM
    window = block + 2 * SEQ_MOST
    accumulate = jnp.zeros((row_count + 2 * SEQ_MOST, columns), jnp.float32)
    score_scale = HEAD_DIM ** (-0.5)

    def one_block(running, block_index):
        key_grads, value_grads = running
        offset = block_index * block
        query_block, key_block, scores = block_scores(
            queries, key_pad, segment, segment_pad, offset, block, head_count
        )
        value_block = lax.dynamic_slice_in_dim(value_pad, offset, window, 0).reshape(
            window, head_count, HEAD_DIM
        )
        probabilities = jnp.exp(scores - logsum[block_index][..., None])
        grad_block = lax.dynamic_slice_in_dim(grad_context, offset, block, 0).reshape(
            block, head_count, HEAD_DIM
        )
        grad_probs = jnp.einsum(
            "qhd,khd->hqk", grad_block, value_block, preferred_element_type=jnp.float32
        )
        delta_rows = jnp.sum(probabilities * grad_probs, axis=-1, keepdims=True)
        grad_scores = (probabilities * (grad_probs - delta_rows)).astype(jnp.bfloat16)
        grad_query = (
            jnp.einsum("hqk,khd->qhd", grad_scores, key_block, preferred_element_type=jnp.float32)
            * score_scale
        )
        grad_key = (
            jnp.einsum("hqk,qhd->khd", grad_scores, query_block, preferred_element_type=jnp.float32)
            * score_scale
        )
        grad_value = jnp.einsum(
            "hqk,qhd->khd",
            probabilities.astype(jnp.bfloat16),
            grad_block,
            preferred_element_type=jnp.float32,
        )
        key_window = lax.dynamic_slice_in_dim(key_grads, offset, window, 0) + grad_key.reshape(
            window, columns
        )
        value_window = lax.dynamic_slice_in_dim(
            value_grads, offset, window, 0
        ) + grad_value.reshape(window, columns)
        key_grads = lax.dynamic_update_slice_in_dim(key_grads, key_window, offset, 0)
        value_grads = lax.dynamic_update_slice_in_dim(value_grads, value_window, offset, 0)
        return ((key_grads, value_grads), grad_query.reshape(block, columns).astype(jnp.bfloat16))

    (key_grads, value_grads), query_grads = lax.scan(
        one_block, (accumulate, accumulate), jnp.arange(row_count // block, dtype=jnp.int32)
    )
    return (query_grads.reshape(row_count, columns), key_grads, value_grads)


def body(
    tokens,
    lengths,
    cotangent,
    w_query,
    w_key,
    w_value,
    w_output,
    vera_down,
    vera_up,
    query_scale,
    query_bias,
    value_scale,
    value_bias,
    hidden_in,
    hidden_out,
):
    padding = ((SEQ_MOST, SEQ_MOST), (0, 0))
    shared_code = jnp.dot(tokens, vera_down, preferred_element_type=jnp.float32)
    code_query = (shared_code * query_scale).astype(jnp.bfloat16)
    code_value = (shared_code * value_scale).astype(jnp.bfloat16)
    side_query = jnp.dot(code_query, vera_up, preferred_element_type=jnp.float32)
    side_value = jnp.dot(code_value, vera_up, preferred_element_type=jnp.float32)
    queries = (
        jnp.dot(tokens, w_query, preferred_element_type=jnp.float32) + side_query * query_bias
    ).astype(jnp.bfloat16)
    key_rows = jnp.dot(tokens, w_key, preferred_element_type=jnp.float32).astype(jnp.bfloat16)
    value_rows = (
        jnp.dot(tokens, w_value, preferred_element_type=jnp.float32) + side_value * value_bias
    ).astype(jnp.bfloat16)
    attn_queries, head_keys, head_values = (
        lax.all_to_all(queries, "head", split_axis=1, concat_axis=0, tiled=True),
        lax.all_to_all(key_rows, "head", split_axis=1, concat_axis=0, tiled=True),
        lax.all_to_all(value_rows, "head", split_axis=1, concat_axis=0, tiled=True),
    )
    group_rows = attn_queries.shape[0]
    segment = segment_ids(lengths[0], group_rows)
    key_pad = jnp.pad(head_keys, padding)
    value_pad = jnp.pad(head_values, padding)
    segment_pad = jnp.pad(segment, (SEQ_MOST, SEQ_MOST), constant_values=-1)
    block = SEQ_MOST
    head_context, logsum = attention_forward(
        attn_queries, key_pad, value_pad, segment, segment_pad, block
    )
    context = lax.all_to_all(head_context, "head", split_axis=0, concat_axis=1, tiled=True)
    attended = jnp.dot(context, w_output, preferred_element_type=jnp.float32)
    normed, inverse_first = layer_norm(tokens.astype(jnp.float32) + attended)
    normed_low = normed.astype(jnp.bfloat16)
    pieces = (
        lax.all_gather(hidden_in, ("seq", "head"), axis=1, tiled=True),
        lax.all_gather(hidden_out, ("seq", "head"), axis=1, tiled=True),
    )
    piece_pre = jnp.dot(normed_low, pieces[0], preferred_element_type=jnp.float32)
    piece_act = gelu_exact(piece_pre).astype(jnp.bfloat16)
    forward_out = lax.dot_general(
        piece_act, pieces[1], CONTRACT_LAST, preferred_element_type=jnp.float32
    )
    layer_out, inverse_second = layer_norm(normed + forward_out)
    grad_combined = norm_back(cotangent.astype(jnp.float32), layer_out, inverse_second)
    grad_forward = grad_combined.astype(jnp.bfloat16)
    pieces = (
        lax.all_gather(hidden_in, ("seq", "head"), axis=1, tiled=True),
        lax.all_gather(hidden_out, ("seq", "head"), axis=1, tiled=True),
    )
    piece_pre = jnp.dot(normed_low, pieces[0], preferred_element_type=jnp.float32)
    piece_up = jnp.dot(grad_forward, pieces[1], preferred_element_type=jnp.float32)
    piece_grad = gelu_back(piece_pre, piece_up).astype(jnp.bfloat16)
    grad_normed = grad_combined + lax.dot_general(
        piece_grad, pieces[0], CONTRACT_LAST, preferred_element_type=jnp.float32
    )
    grad_first = norm_back(grad_normed, normed, inverse_first)
    grad_attended = grad_first.astype(jnp.bfloat16)
    grad_context = lax.dot_general(
        grad_attended, w_output, CONTRACT_LAST, preferred_element_type=jnp.float32
    ).astype(jnp.bfloat16)
    head_grad_context = lax.all_to_all(
        grad_context, "head", split_axis=1, concat_axis=0, tiled=True
    )
    head_query_grad, key_grad_pad, value_grad_pad = attention_backward(
        attn_queries, key_pad, value_pad, segment, segment_pad, logsum, head_grad_context, block
    )
    head_key_grad = key_grad_pad[SEQ_MOST : SEQ_MOST + group_rows].astype(jnp.bfloat16)
    head_value_grad = value_grad_pad[SEQ_MOST : SEQ_MOST + group_rows].astype(jnp.bfloat16)
    grad_queries, grad_keys, grad_values = (
        lax.all_to_all(head_query_grad, "head", split_axis=0, concat_axis=1, tiled=True),
        lax.all_to_all(head_key_grad, "head", split_axis=0, concat_axis=1, tiled=True),
        lax.all_to_all(head_value_grad, "head", split_axis=0, concat_axis=1, tiled=True),
    )
    query_bias_grad = jnp.sum(grad_queries.astype(jnp.float32) * side_query, axis=0)
    value_bias_grad = jnp.sum(grad_values.astype(jnp.float32) * side_value, axis=0)
    grad_code_query = lax.dot_general(
        (grad_queries * query_bias).astype(jnp.bfloat16),
        vera_up,
        CONTRACT_LAST,
        preferred_element_type=jnp.float32,
    )
    grad_code_value = lax.dot_general(
        (grad_values * value_bias).astype(jnp.bfloat16),
        vera_up,
        CONTRACT_LAST,
        preferred_element_type=jnp.float32,
    )
    query_scale_grad = jnp.sum(grad_code_query * shared_code, axis=0)
    value_scale_grad = jnp.sum(grad_code_value * shared_code, axis=0)
    grad_code = (grad_code_query * query_scale + grad_code_value * value_scale).astype(jnp.bfloat16)
    token_grad = grad_first + lax.dot_general(
        grad_queries, w_query, CONTRACT_LAST, preferred_element_type=jnp.float32
    )
    token_grad = token_grad + lax.dot_general(
        grad_keys, w_key, CONTRACT_LAST, preferred_element_type=jnp.float32
    )
    token_grad = token_grad + lax.dot_general(
        grad_values, w_value, CONTRACT_LAST, preferred_element_type=jnp.float32
    )
    token_grad = token_grad + lax.dot_general(
        grad_code, vera_down, CONTRACT_LAST, preferred_element_type=jnp.float32
    )
    totals = lax.psum(
        (query_scale_grad, query_bias_grad, value_scale_grad, value_bias_grad), ("seq", "head")
    )
    return (
        layer_out.astype(jnp.bfloat16),
        token_grad.astype(jnp.bfloat16),
        totals[0],
        totals[1],
        totals[2],
        totals[3],
    )


def solution(mesh):
    return jax.shard_map(
        body,
        mesh=mesh,
        in_specs=(
            P(("seq", "head"), None),
            P("seq", None),
            P(("seq", "head"), None),
            P(),
            P(),
            P(),
            P(),
            P(),
            P(),
            P(),
            P(),
            P(),
            P(),
            P(None, ("seq", "head")),
            P(None, ("seq", "head")),
        ),
        out_specs=(P(("seq", "head"), None), P(("seq", "head"), None), P(), P(), P(), P()),
        check_vma=False,
    )
```

profile of v0, /device:TPU:0, one launch (start us, length us, event | category | flops | bytes accessed | tf_op | source)
XLA Modules:
  0.0 1031.7 jit_solution(921197608585857721)
XLA Ops:
  7.2 3.8 fusion.64
  16.9 6.4 all-to-all-start
  23.3 4.2 fusion.27
  31.8 28.5 %all-to-all-done = bf16[1024,4,192]{0,2,1:T(8,128)(2,1)S(1)} async-done(((bf16[1024,4,192]{0,2,1:T(8,128)(2,1)}), bf16[1024,4,192]{0,2,1:T(8,128)(2,1)S(1)}, u32[]{:S(2)}, u32[]{:S(2)}) %all-to-all-start) | async-done | bytes 1572896 | tf_op jit(solution)/shard_map/all_to_all | solution.py:178
  60.3 4.3 all-to-all-start.1
  64.6 4.3 convolution_convert_fusion.1
  69.0 32.2 %all-to-all-done.1 = bf16[1024,4,192]{0,2,1:T(8,128)(2,1)} async-done(((bf16[1024,4,192]{0,2,1:T(8,128)(2,1)}), bf16[1024,4,192]{0,2,1:T(8,128)(2,1)}, u32[]{:S(2)}, u32[]{:S(2)}) %all-to-all-start.1) | async-done | bytes 1572896 | tf_op jit(solution)/shard_map/all_to_all | solution.py:176
  101.2 4.4 all-to-all-start.2
  111.9 33.3 %all-to-all-done.2 = bf16[1024,4,192]{0,2,1:T(8,128)(2,1)} async-done(((bf16[1024,4,192]{0,2,1:T(8,128)(2,1)}), bf16[1024,4,192]{0,2,1:T(8,128)(2,1)}, u32[]{:S(2)}, u32[]{:S(2)}) %all-to-all-start.2) | async-done | bytes 1572896 | tf_op jit(solution)/shard_map/all_to_all | solution.py:177
  151.1 120.4 %while.26 = (s32[]{:T(128)}, bf16[8,512,192]{1,2,0:T(8,128)(2,1)}, f32[8,3,512]{2,1,0:T(4,128)}, s32[8]{0:T(128)S(1)}, bf16[5120,192]{0,1:T(8,128)(2,1)S(1)}, /*...) while((s32[]{:T(128)}, bf16[8,512,192]{1,2,0:T(8,128)(2,1)}, ...), condition=%wide.region_5.6_spmd, body=%wide.region_2.5_spmd.sunk | while | flops 633174528 | bytes 36252904 | solution.py:84
  207.1 3.5 fusion.129
  271.5 4.1 copy.96
  275.7 3.7 all_to_all.124
  282.4 4.5 all-to-all-start.3
  292.1 34.6 %all-to-all-done.3 = bf16[4,1024,192]{1,2,0:T(8,128)(2,1)} async-done(((bf16[4,1024,192]{1,2,0:T(8,128)(2,1)}), bf16[4,1024,192]{1,2,0:T(8,128)(2,1)}, u32[]{:S(2)}, u32[]{:S(2)}) %all-to-all-start.3) | async-done | bytes 1572896 | tf_op jit(solution)/shard_map/all_to_all | solution.py:189
  332.1 34.6 %fusion.9 = (f32[1024,3072]{1,0:T(8,128)}, f32[1024,3072]{1,0:T(8,128)}) fusion(bf16[768,3072]{0,1:T(8,128)(2,1)} %all-gather.3.cloned.1.call-done, f32[1024,768]{0,1:T(8,128)} %copy-done.4, f32[1024]{0:T(1024)S(1)} %add_rsqrt_fusion.1, f32[1024]{0:T(1024)S(1)} %broadcast_multiply_fusion.5), kind=kOutput, calls=%fused_computation.35 | convolution fusion | flops 5029232640 | bytes 33038336 | tf_op jit(solution)/shard_map/dot_general | solution.py:197
  366.7 15.8 %fusion.60 = (f32[1024]{0:T(1024)S(1)}, f32[1024,768]{0,1:T(8,128)S(1)}) fusion(bf16[768,3072]{0,1:T(8,128)(2,1)} %all-gather.5.cloned.1.call-done, f32[1024,3072]{1,0:T(8,128)} %get-tuple-element.216, f32[1024,3072]{1,0:T(8,128)} %get-tuple-element.217, f32[1024]{0:T(1024)S(1)} %add_rsqrt_fusion.1, f32[1024,768]{0,1:T(8,128)} %copy-done.4, ...), kind=kOutput, calls=%fused_computation.126 | convolution fusion | flops 4844420096 | bytes 36188160 | tf_op jit(solution)/shard_map/dot_general | solution.py:199
  387.0 25.1 %fusion.58 = (f32[1024]{0:T(1024)S(1)}, f32[1024]{0:T(1024)S(1)}, f32[1024,768]{0,1:T(8,128)}) fusion(f32[1024]{0:T(1024)S(1)} %add_rsqrt_fusion.1, f32[1024,768]{0,1:T(8,128)} %copy-done.4, f32[1024]{0:T(1024)S(1)} %broadcast_multiply_fusion.5, bf16[768,3072]{0,1:T(8,128)(2,1)} %all-gather.3.cloned.1.call-done, f32[1024,3072]{1,0:T(8,128)} %get-tuple-element.216, ...), kind=kOutput, calls=%fused_computation.124 | convolution fusion | flops 9724229632 | bytes 45645824 | tf_op jit(solution)/shard_map/dot_general | solution.py:212
  412.2 5.5 convolution_convert_fusion
  417.7 3.8 all-to-all-start.4
  421.4 36.5 %all-to-all-done.4 = bf16[1024,4,192]{0,2,1:T(8,128)(2,1)S(1)} async-done(((bf16[1024,4,192]{0,2,1:T(8,128)(2,1)}), bf16[1024,4,192]{0,2,1:T(8,128)(2,1)S(1)}, u32[]{:S(2)}, u32[]{:S(2)}) %all-to-all-start.4) | async-done | bytes 1572896 | tf_op jit(solution)/shard_map/all_to_all | solution.py:220
  465.4 374.2 %while.27 = (s32[]{:T(128)}, f32[5120,192]{0,1:T(8,128)}, f32[5120,192]{0,1:T(8,128)}, bf16[8,512,192]{1,2,0:T(8,128)(2,1)}, s32[8]{0:T(128)S(1)}, /*index=5*/bf...) while((s32[]{:T(128)}, f32[5120,192]{0,1:T(8,128)}, ...), condition=%wide.region_16.17_spmd, body=%wide.region_14.16_spmd.sunk | while | flops 1533049344 | bytes 102292328 | solution.py:139
  468.9 5.1 fusion.140
  480.8 8.2 multiply_reduce_fusion.7
  489.0 9.5 multiply_convert_fusion.10
  501.9 4.7 fusion.141
  515.6 5.1 fusion.140
  527.6 8.2 multiply_reduce_fusion.7
  535.8 9.5 multiply_convert_fusion.10
  548.7 4.7 fusion.141
  562.4 5.1 fusion.140
  574.4 8.2 multiply_reduce_fusion.7
  582.5 9.5 multiply_convert_fusion.10
  595.4 4.7 fusion.141
  609.2 5.1 fusion.140
  621.2 8.2 multiply_reduce_fusion.7
  629.4 9.5 multiply_convert_fusion.10
  642.3 4.7 fusion.141
  656.0 5.1 fusion.140
  668.0 8.2 multiply_reduce_fusion.7
  676.2 9.5 multiply_convert_fusion.10
  689.1 4.7 fusion.141
  702.8 5.1 fusion.140
  714.8 8.2 multiply_reduce_fusion.7
  723.0 9.5 multiply_convert_fusion.10
  735.9 4.7 fusion.141
  749.6 5.1 fusion.140
  761.6 8.2 multiply_reduce_fusion.7
  769.8 9.5 multiply_convert_fusion.10
  782.6 4.7 fusion.141
  796.3 5.1 fusion.140
  808.3 8.2 multiply_reduce_fusion.7
  816.5 9.5 multiply_convert_fusion.10
  829.4 4.7 fusion.141
  847.2 3.6 all-to-all-start.5
  854.1 33.1 %all-to-all-done.5 = bf16[4,1024,192]{1,2,0:T(8,128)(2,1)S(1)} async-done(((bf16[4,1024,192]{1,2,0:T(8,128)(2,1)}), bf16[4,1024,192]{1,2,0:T(8,128)(2,1)S(1)}, u32[]{:S(2)}, u32[]{:S(2)}) %all-to-all-start.5) | async-done | bytes 1572896 | tf_op jit(solution)/shard_map/all_to_all | solution.py:229
  888.4 3.6 all-to-all-start.7
  895.3 33.1 %all-to-all-done.7 = bf16[4,1024,192]{1,2,0:T(8,128)(2,1)S(1)} async-done(((bf16[4,1024,192]{1,2,0:T(8,128)(2,1)}), bf16[4,1024,192]{1,2,0:T(8,128)(2,1)S(1)}, u32[]{:S(2)}, u32[]{:S(2)}) %all-to-all-start.7) | async-done | bytes 1572896 | tf_op jit(solution)/shard_map/all_to_all | solution.py:231
  928.3 4.6 all-to-all-start.6
  935.6 4.9 fusion.65
  945.0 3.6 fusion.28
  948.5 21.0 %all-to-all-done.6 = bf16[4,1024,192]{1,2,0:T(8,128)(2,1)} async-done(((bf16[4,1024,192]{1,2,0:T(8,128)(2,1)}), bf16[4,1024,192]{1,2,0:T(8,128)(2,1)}, u32[]{:S(2)}, u32[]{:S(2)}) %all-to-all-start.6) | async-done | bytes 1572896 | tf_op jit(solution)/shard_map/all_to_all | solution.py:230
  974.1 5.7 add_convert_fusion.3
  986.2 38.2 %all-reduce.3 = (f32[1024]{0:T(1024)}, f32[768]{0:T(1024)}, f32[1024]{0:T(1024)}, f32[768]{0:T(1024)}) all-reduce(f32[1024]{0:T(1024)S(1)} %get-tuple-element.154, f32[768]{0:T(1024)S(1)} %fusion.19, f32[1024]{0:T(1024)S(1)} %get-tuple-element.153, f32[768]{0:T(1024)S(1)} %fusion.21), channel_id=1, replica_groups=mesh['seq'=8,'head'=4] {'seq','head'}, use_global_device_ids=true, to_apply=%region_18.19 | all-reduce | flops 3584 | bytes 28672 | tf_op jit(solution)/shard_map/psum | solution.py:262
  (368 shorter events, 324.9 us)
Async XLA Ops:
  7.2 3.8 copy-start
  7.2 3.8 copy-start.24
  11.0 2.1 copy-start.9
  11.0 2.6 copy-start.16
  11.0 3.2 copy-start.20
  11.0 3.2 copy-start.34
  14.3 2.6 copy-start.11
  16.9 6.5 copy-start.26
  16.9 43.4 %all-to-all-start = ((bf16[1024,4,192]{0,2,1:T(8,128)(2,1)}), bf16[1024,4,192]{0,2,1:T(8,128)(2,1)S(1)}, u32[]{:S(2)}, u32[]{:S(2)}) async-start(bf16[1024,4,192]{0,2,1:T(8,128)(2,1)} %bitcast.188), calls=%async_computation | async-start | bytes 3145728 | tf_op jit(solution)/shard_map/all_to_all | solution.py:178
  23.3 5.9 copy-start.17
  23.3 5.9 copy-start.38
  23.3 5.9 copy-start.39
  60.3 40.9 %all-to-all-start.1 = ((bf16[1024,4,192]{0,2,1:T(8,128)(2,1)}), bf16[1024,4,192]{0,2,1:T(8,128)(2,1)}, u32[]{:S(2)}, u32[]{:S(2)}) async-start(bf16[1024,4,192]{0,2,1:T(8,128)(2,1)} %bitcast.187), calls=%async_computation.1 | async-start | bytes 3145728 | tf_op jit(solution)/shard_map/all_to_all | solution.py:176
  69.0 37.3 %copy-start.36 = (s32[1,32]{1,0:T(1,128)S(1)}, s32[1,32]{1,0:T(1,128)}, u32[]{:S(2)}) copy-start(s32[1,32]{1,0:T(1,128)} %param.20) | copy-start | bytes 388
  101.2 44.0 %all-to-all-start.2 = ((bf16[1024,4,192]{0,2,1:T(8,128)(2,1)}), bf16[1024,4,192]{0,2,1:T(8,128)(2,1)}, u32[]{:S(2)}, u32[]{:S(2)}) async-start(bf16[1024,4,192]{0,2,1:T(8,128)(2,1)} %bitcast.186), calls=%async_computation.2 | async-start | bytes 3145728 | tf_op jit(solution)/shard_map/all_to_all | solution.py:177
  105.5 226.6 %all-gather.3.cloned.1.call-start = ((), (), s32[]{:S(2)}) async-start(), calls=%async_computation.8 | async-start | bytes 4866048 | tf_op jit(solution)/shard_map/all_gather | solution.py:194
  271.5 7.9 copy-start.1
  282.4 5.3 copy-start.18
  282.4 44.3 %all-to-all-start.3 = ((bf16[4,1024,192]{1,2,0:T(8,128)(2,1)}), bf16[4,1024,192]{1,2,0:T(8,128)(2,1)}, u32[]{:S(2)}, u32[]{:S(2)}) async-start(bf16[4,1024,192]{1,2,0:T(8,128)(2,1)} %copy.97), calls=%async_computation.3 | async-start | bytes 3145728 | tf_op jit(solution)/shard_map/all_to_all | solution.py:189
  286.9 79.7 %all-gather.5.cloned.1.call-start = ((), (), s32[]{:S(2)}) async-start(), calls=%async_computation.9 | async-start | bytes 4866048 | tf_op jit(solution)/shard_map/all_gather | solution.py:195
  289.4 37.3 %copy-start.19 = (bf16[1024,768]{0,1:T(8,128)(2,1)S(1)}, bf16[1024,768]{0,1:T(8,128)(2,1)}, u32[]{:S(2)}) copy-start(bf16[1024,768]{0,1:T(8,128)(2,1)} %copy.91) | copy-start | bytes 4718596
  330.0 1.7 copy-start.4
  330.0 82.1 %copy-start.22 = (f32[1024]{0:T(1024)}, f32[1024]{0:T(1024)S(1)}, u32[]{:S(2)}) copy-start(f32[1024]{0:T(1024)S(1)} %broadcast_multiply_fusion.5) | copy-start | bytes 12292
  332.1 80.1 %copy-start.28 = (f32[1024]{0:T(1024)}, f32[1024]{0:T(1024)S(1)}, u32[]{:S(2)}) copy-start(f32[1024]{0:T(1024)S(1)} %add_rsqrt_fusion.1) | copy-start | bytes 12292
  382.5 4.5 copy-start.3
  382.5 2.5 copy-start.8
  387.0 25.1 %copy-start.37 = (bf16[768,768]{1,0:T(8,128)(2,1)S(1)}, bf16[768,768]{1,0:T(8,128)(2,1)}, u32[]{:S(2)}) copy-start(bf16[768,768]{1,0:T(8,128)(2,1)} %param.25) | copy-start | bytes 3538948
  412.1 5.6 copy-start.30
  412.1 5.5 copy-start.32
  417.7 40.3 %all-to-all-start.4 = ((bf16[1024,4,192]{0,2,1:T(8,128)(2,1)}), bf16[1024,4,192]{0,2,1:T(8,128)(2,1)S(1)}, u32[]{:S(2)}, u32[]{:S(2)}) async-start(bf16[1024,4,192]{0,2,1:T(8,128)(2,1)} %bitcast.189), calls=%async_computation.4 | async-start | bytes 3145728 | tf_op jit(solution)/shard_map/all_to_all | solution.py:220
  498.5 11.5 %slice-start = ((s8[4718592]{0:T(1024)(128)(4,1)}), s8[4194304]{0:T(1024)(128)(4,1)S(1)}, s32[]{:S(2)}) async-start(s8[4718592]{0:T(1024)(128)(4,1)} %bitcast.158), calls=%async_computation.10 | async-start | bytes 8388608 | tf_op jit(solution)/shard_map/while
  501.9 8.0 slice-start.1
  545.2 11.5 %slice-start = ((s8[4718592]{0:T(1024)(128)(4,1)}), s8[4194304]{0:T(1024)(128)(4,1)S(1)}, s32[]{:S(2)}) async-start(s8[4718592]{0:T(1024)(128)(4,1)} %bitcast.158), calls=%async_computation.10 | async-start | bytes 8388608 | tf_op jit(solution)/shard_map/while
  548.6 8.1 slice-start.1
  592.0 11.5 %slice-start = ((s8[4718592]{0:T(1024)(128)(4,1)}), s8[4194304]{0:T(1024)(128)(4,1)S(1)}, s32[]{:S(2)}) async-start(s8[4718592]{0:T(1024)(128)(4,1)} %bitcast.158), calls=%async_computation.10 | async-start | bytes 8388608 | tf_op jit(solution)/shard_map/while
  595.4 8.1 slice-start.1
  638.8 11.5 %slice-start = ((s8[4718592]{0:T(1024)(128)(4,1)}), s8[4194304]{0:T(1024)(128)(4,1)S(1)}, s32[]{:S(2)}) async-start(s8[4718592]{0:T(1024)(128)(4,1)} %bitcast.158), calls=%async_computation.10 | async-start | bytes 8388608 | tf_op jit(solution)/shard_map/while
  642.2 8.1 slice-start.1
  685.7 11.5 %slice-start = ((s8[4718592]{0:T(1024)(128)(4,1)}), s8[4194304]{0:T(1024)(128)(4,1)S(1)}, s32[]{:S(2)}) async-start(s8[4718592]{0:T(1024)(128)(4,1)} %bitcast.158), calls=%async_computation.10 | async-start | bytes 8388608 | tf_op jit(solution)/shard_map/while
  689.1 8.1 slice-start.1
  732.5 11.5 %slice-start = ((s8[4718592]{0:T(1024)(128)(4,1)}), s8[4194304]{0:T(1024)(128)(4,1)S(1)}, s32[]{:S(2)}) async-start(s8[4718592]{0:T(1024)(128)(4,1)} %bitcast.158), calls=%async_computation.10 | async-start | bytes 8388608 | tf_op jit(solution)/shard_map/while
  735.9 8.1 slice-start.1
  779.2 11.4 %slice-start = ((s8[4718592]{0:T(1024)(128)(4,1)}), s8[4194304]{0:T(1024)(128)(4,1)S(1)}, s32[]{:S(2)}) async-start(s8[4718592]{0:T(1024)(128)(4,1)} %bitcast.158), calls=%async_computation.10 | async-start | bytes 8388608 | tf_op jit(solution)/shard_map/while
  782.6 8.0 slice-start.1
  826.0 11.4 %slice-start = ((s8[4718592]{0:T(1024)(128)(4,1)}), s8[4194304]{0:T(1024)(128)(4,1)S(1)}, s32[]{:S(2)}) async-start(s8[4718592]{0:T(1024)(128)(4,1)} %bitcast.158), calls=%async_computation.10 | async-start | bytes 8388608 | tf_op jit(solution)/shard_map/while
  829.4 8.0 slice-start.1
  847.2 40.0 %all-to-all-start.5 = ((bf16[4,1024,192]{1,2,0:T(8,128)(2,1)}), bf16[4,1024,192]{1,2,0:T(8,128)(2,1)S(1)}, u32[]{:S(2)}, u32[]{:S(2)}) async-start(bf16[4,1024,192]{1,2,0:T(8,128)(2,1)} %copy.101), calls=%async_computation.5 | async-start | bytes 3145728 | tf_op jit(solution)/shard_map/all_to_all | solution.py:229
  888.4 40.0 %all-to-all-start.7 = ((bf16[4,1024,192]{1,2,0:T(8,128)(2,1)}), bf16[4,1024,192]{1,2,0:T(8,128)(2,1)S(1)}, u32[]{:S(2)}, u32[]{:S(2)}) async-start(bf16[4,1024,192]{1,2,0:T(8,128)(2,1)} %bitcast.176), calls=%async_computation.7 | async-start | bytes 3145728 | tf_op jit(solution)/shard_map/all_to_all | solution.py:231
  928.3 41.1 %all-to-all-start.6 = ((bf16[4,1024,192]{1,2,0:T(8,128)(2,1)}), bf16[4,1024,192]{1,2,0:T(8,128)(2,1)}, u32[]{:S(2)}, u32[]{:S(2)}) async-start(bf16[4,1024,192]{1,2,0:T(8,128)(2,1)} %bitcast.175), calls=%async_computation.6 | async-start | bytes 3145728 | tf_op jit(solution)/shard_map/all_to_all | solution.py:230
  935.6 4.9 copy-start.7
  935.6 4.9 copy-start.40
  940.5 2.2 copy-start.10
  940.5 2.2 copy-start.35
  942.7 2.3 copy-start.15
  942.7 2.3 copy-start.25
  942.7 2.3 copy-start.27
  969.5 3.4 copy-start.2
  969.5 3.7 copy-start.5
  969.5 4.6 copy-start.14
  969.5 4.6 copy-start.23
  969.5 4.6 copy-start.29
  969.5 4.6 copy-start.31
  969.5 4.6 copy-start.33
  982.4 3.3 copy-start.12
  (3 other events, 3.4 us)
Sparse Core Ops, SparseCore 0:
  109.2 73.5 all-gather.2
  290.6 73.7 all-gather.4
where the time goes:
time: 1050 us; the launch traced here: 1030 us
  matrix products  353 us (34%)
  waiting for transfers between devices  253 us (24%)
  local copies, waits for them, and re-layouts  164 us (16%)
  other arithmetic  145 us (14%)
  blocking collectives  38.2 us (4%)
  starting transfers between devices  35.9 us (3%)
  loops' own time  28.1 us (3%)
  between operations  15 us (1%)
    dot_general x16, matrix products, block_scores(): jnp.einsum('qhd,khd->hqk', query_block, key_block, preferred_element_type...  81.6 us
    convert_element_type x8, other arithmetic, one_block(): (probabilities * (grad_probs - delta_rows)).astype(jnp.bfloat16)  75.7 us
    dot_general x8, matrix products, one_block(): jnp.einsum('qhd,khd->hqk', grad_block, value_block, preferred_element_typ...  40.9 us
    psum x1, blocking collectives, body(): lax.psum((query_scale_grad, query_bias_grad, value_scale_grad, value_bias...  38.2 us
    dot_general x8, matrix products, one_block(): jnp.einsum('hqk,qhd->khd', probabilities.astype(jnp.bfloat16), grad_block...  37.4 us
    all_to_all x1, waiting for transfers between devices, body(): lax.all_to_all(grad_context, 'head', split_axis=1, concat_axis=0, tiled=T...  36.5 us
    all_to_all x1, waiting for transfers between devices, body(): lax.all_to_all(head_context, 'head', split_axis=0, concat_axis=1, tiled=T...  34.6 us
    dot_general x1, matrix products, body(): jnp.dot(normed_low, pieces[0], preferred_element_type=jnp.float32)  34.6 us
  transfers between devices with their start and end apart: 10, of which 8 were waited for; matrix products, arithmetic and copies ran while one was open for 20% of the time, Pallas kernels for 0%

commit v1 on v0

v1 whole, which is shorter than its diff:
```python
import functools
import math

import jax
import jax.numpy as jnp
from jax import lax
from jax.experimental import pallas as pl
from jax.experimental.pallas import tpu as pltpu
from jax.sharding import PartitionSpec as P

HEAD_DIM = 64
SEQ_MOST = 512
EPSILON = 1e-05
HIDDEN = -1e30
LN2 = math.log(2.0)
QUERY_FOLD = HEAD_DIM ** (-0.5) / LN2
TILE_Q = 256
TILE_K = 256
LANES = 128
NN = (((1,), (0,)), ((), ()))
NT = (((1,), (1,)), ((), ()))
TN = (((0,), (0,)), ((), ()))
F32 = jnp.float32
BF16 = jnp.bfloat16
VMEM = pl.BlockSpec(memory_space=pltpu.VMEM)
SMEM = pl.BlockSpec(memory_space=pltpu.SMEM)
PARAMS = pltpu.CompilerParams(vmem_limit_bytes=58 << 20)


def dot(left, right, form):
    return lax.dot_general(left, right, form, preferred_element_type=F32)


def sds(shape, dtype):
    return jax.ShapeDtypeStruct(shape, dtype)


def span(index, size):
    return pl.ds(pl.multiple_of(index * size, size), size)


def project_kernel(
    x_ref, wq_ref, wk_ref, wv_ref, down_ref, up_ref, qs_ref, qb_ref, vs_ref, vb_ref,
    qt_ref, kt_ref, vt_ref, xt_ref, wqe_ref, wve_ref,
):
    rows, width = x_ref.shape

    def fold(index, carry):
        part = span(index, 256)
        down = down_ref[part, :].astype(F32)
        side_q = dot((down * qs_ref[...]).astype(BF16), up_ref[...], NN) * qb_ref[...]
        wqe_ref[part, :] = ((wq_ref[part, :].astype(F32) + side_q) * QUERY_FOLD).astype(BF16)
        side_v = dot((down * vs_ref[...]).astype(BF16), up_ref[...], NN) * vb_ref[...]
        wve_ref[part, :] = (wv_ref[part, :].astype(F32) + side_v).astype(BF16)
        return carry

    lax.fori_loop(0, width // 256, fold, 0)

    def flip(index, carry):
        part = span(index, 256)
        xt_ref[:, part] = x_ref[part, :].T
        return carry

    lax.fori_loop(0, rows // 256, flip, 0)

    def apply(index, carry):
        part = span(index, 256)
        qt_ref[part, :] = dot(wqe_ref[:, part], xt_ref[...], TN).astype(BF16)
        kt_ref[part, :] = dot(wk_ref[:, part], xt_ref[...], TN).astype(BF16)
        vt_ref[part, :] = dot(wve_ref[:, part], xt_ref[...], TN).astype(BF16)
        return carry

    lax.fori_loop(0, width // 256, apply, 0)


def bounds(len_ref, first, count):
    row = first + lax.broadcasted_iota(jnp.int32, (1, count), 1)
    last = first + count - 1
    low = jnp.zeros((1, count), jnp.int32)
    high = jnp.full((1, count), 1 << 30, jnp.int32)
    end, least, most = 0, 0, 1 << 30
    for i in range(len_ref.shape[1]):
        end = end + len_ref[0, i]
        low = jnp.where(row >= end, end, low)
        high = jnp.where(row < end, jnp.minimum(high, end), high)
        least = jnp.where(first >= end, end, least)
        most = jnp.where(last < end, jnp.minimum(most, end), most)
    return low, high, least, most


def key_range(least, most, shift, extent):
    start = (least - shift) // LANES
    tiles = (most - shift - start * LANES + TILE_K - 1) // TILE_K
    start = jnp.minimum(start, (extent - tiles * TILE_K) // LANES)
    return start, tiles


def attend_kernel(
    shift_ref, len_ref, qt_ref, kt_ref, vt_ref, xl_ref, xr_ref, wk_ref, wve_ref,
    ct_ref, ls_ref, ke_ref, ve_ref,
    flip_ref, acc_ref, high_ref, total_ref, bias_ref,
):
    width, rows = qt_ref.shape
    extent = ke_ref.shape[1]
    heads = width // HEAD_DIM
    shift = shift_ref[0]

    ke_ref[:, SEQ_MOST : SEQ_MOST + rows] = kt_ref[...]
    ve_ref[:, SEQ_MOST : SEQ_MOST + rows] = vt_ref[...]
    for side_ref, base in ((xl_ref, 0), (xr_ref, SEQ_MOST + rows)):
        flip_ref[...] = side_ref[...].T

        def edge(index, carry):
            part = span(index, 256)
            ke_ref[part, base : base + SEQ_MOST] = dot(
                wk_ref[:, part], flip_ref[...], TN
            ).astype(BF16)
            ve_ref[part, base : base + SEQ_MOST] = dot(
                wve_ref[:, part], flip_ref[...], TN
            ).astype(BF16)
            return carry

        lax.fori_loop(0, width // 256, edge, 0)

    def query_tile(tile, carry):
        first = shift + SEQ_MOST + tile * TILE_Q
        low, high, least, most = bounds(len_ref, first, TILE_Q)
        start, tiles = key_range(least, most, shift, extent)
        q_part = span(tile, TILE_Q)
        acc_ref[...] = jnp.zeros_like(acc_ref)
        high_ref[...] = jnp.full_like(high_ref, HIDDEN)
        total_ref[...] = jnp.zeros_like(total_ref)

        def key_tile(step, inner):
            base = pl.multiple_of((start + step * (TILE_K // LANES)) * LANES, LANES)
            k_part = pl.ds(base, TILE_K)
            key = shift + base + lax.broadcasted_iota(jnp.int32, (TILE_K, TILE_Q), 0)
            bias_ref[...] = jnp.where((key >= low) & (key < high), 0.0, HIDDEN)

            def group(index, deep):
                for sub in range(4):
                    head = index * 4 + sub
                    part = span(head, HEAD_DIM)
                    scores = dot(ke_ref[part, k_part], qt_ref[part, q_part], TN) + bias_ref[...]
                    before = high_ref[head]
                    best = jnp.maximum(before, jnp.max(scores, axis=0, keepdims=True))
                    fade = jnp.exp2(before - best)
                    probs = jnp.exp2(scores - best)
                    high_ref[head] = best
                    total_ref[head] = total_ref[head] * fade + jnp.sum(
                        probs, axis=0, keepdims=True
                    )
                    acc_ref[part, :] = acc_ref[part, :] * fade + dot(
                        ve_ref[part, k_part], probs.astype(BF16), NN
                    )
                return deep

            lax.fori_loop(0, heads // 4, group, 0)
            return inner

        lax.fori_loop(0, tiles, key_tile, 0)
        for head in range(heads):
            part = pl.ds(head * HEAD_DIM, HEAD_DIM)
            total = total_ref[head]
            ct_ref[part, q_part] = (acc_ref[part, :] / total).astype(BF16)
            ls_ref[head, :, q_part] = high_ref[head] + jnp.log2(total)
        return carry

    lax.fori_loop(0, rows // TILE_Q, query_tile, 0)


def attend_back_kernel(
    shift_ref, len_ref, qt_ref, ke_ref, ve_ref, ls_ref, gt_ref, dl_ref,
    dq_ref, dk_ref, dv_ref,
    dq_acc, dk_acc, dv_acc, bias_ref,
):
    width, rows = qt_ref.shape
    extent = ke_ref.shape[1]
    heads = width // HEAD_DIM
    shift = shift_ref[0]
    dk_acc[...] = jnp.zeros_like(dk_acc)
    dv_acc[...] = jnp.zeros_like(dv_acc)

    def query_tile(tile, carry):
        first = shift + SEQ_MOST + tile * TILE_Q
        low, high, least, most = bounds(len_ref, first, TILE_Q)
        start, tiles = key_range(least, most, shift, extent)
        q_part = span(tile, TILE_Q)
        dq_acc[...] = jnp.zeros_like(dq_acc)

        def key_tile(step, inner):
            base = pl.multiple_of((start + step * (TILE_K // LANES)) * LANES, LANES)
            k_part = pl.ds(base, TILE_K)
            key = shift + base + lax.broadcasted_iota(jnp.int32, (TILE_K, TILE_Q), 0)
            bias_ref[...] = jnp.where((key >= low) & (key < high), 0.0, HIDDEN)

            def group(index, deep):
                for sub in range(4):
                    head = index * 4 + sub
                    part = span(head, HEAD_DIM)
                    keys = ke_ref[part, k_part]
                    queries = qt_ref[part, q_part]
                    grads = gt_ref[part, q_part]
                    scores = dot(keys, queries, TN) + bias_ref[...]
                    probs = jnp.exp2(scores - ls_ref[head, :, q_part])
                    grad_probs = dot(ve_ref[part, k_part], grads, TN)
                    slopes = (probs * (grad_probs - dl_ref[head, :, q_part])).astype(BF16)
                    dv_acc[part, k_part] += dot(grads, probs.astype(BF16), NT)
                    dk_acc[part, k_part] += dot(queries, slopes, NT)
                    dq_acc[part, :] += dot(keys, slopes, NN)
                return deep

            lax.fori_loop(0, heads // 4, group, 0)
            return inner

        lax.fori_loop(0, tiles, key_tile, 0)
        dq_ref[:, q_part] = (dq_acc[...] * LN2).astype(BF16)
        return carry

    lax.fori_loop(0, rows // TILE_Q, query_tile, 0)
    dk_ref[...] = (dk_acc[...] * LN2).astype(BF16)
    dv_ref[...] = dv_acc[...].astype(BF16)


def norm(values):
    center = values - jnp.mean(values, axis=0, keepdims=True)
    inverse = lax.rsqrt(jnp.mean(center * center, axis=0, keepdims=True) + EPSILON)
    return center * inverse, inverse


def norm_back(gradient, normed, inverse):
    centered = gradient - jnp.mean(gradient, axis=0, keepdims=True)
    return inverse * (centered - normed * jnp.mean(gradient * normed, axis=0, keepdims=True))


def gelu_parts(x):
    bell = jnp.exp(-0.5 * (x * x))
    t = 1.0 / (1.0 + (0.3275911 * math.sqrt(0.5)) * jnp.abs(x))
    poly = t * (0.127414796 + t * (-0.142248368 + t * (0.710706870 + t * (-0.726576013 + t * 0.530702714))))
    tail = poly * bell
    normal = jnp.where(x >= 0, 1.0 - tail, tail)
    return x * normal, normal + x * (bell * (1.0 / math.sqrt(2.0 * math.pi)))


def feed_kernel(
    xt_ref, ct_ref, cot_ref, wo_ref, hi_ref, ho_ref,
    out_ref, gf_ref, gc_ref, dl_ref,
    normed_ref, low_ref, slope_ref, sum_ref,
):
    width = xt_ref.shape[0]
    hidden = hi_ref.shape[0]
    step = 768
    heads = width // HEAD_DIM
    attended = dot(wo_ref[...], ct_ref[...], TN)
    normed, inverse_first = norm(xt_ref[...].astype(F32) + attended)
    normed_ref[...] = normed
    low_ref[...] = normed.astype(BF16)
    sum_ref[...] = normed

    def forward(index, carry):
        part = span(index, step)
        act, slope = gelu_parts(dot(hi_ref[part, :], low_ref[...], NN))
        slope_ref[part, :] = slope
        sum_ref[...] += dot(ho_ref[part, :], act.astype(BF16), TN)
        return carry

    lax.fori_loop(0, hidden // step, forward, 0)
    layer_out, inverse_second = norm(sum_ref[...])
    out_ref[...] = layer_out.T.astype(BF16)
    grad = norm_back(cot_ref[...].astype(F32).T, layer_out, inverse_second)
    sum_ref[...] = grad
    low_ref[...] = grad.astype(BF16)

    def backward(index, carry):
        part = span(index, step)
        upstream = dot(ho_ref[part, :], low_ref[...], NN)
        grad_pre = (slope_ref[part, :] * upstream).astype(BF16)
        sum_ref[...] += dot(hi_ref[part, :], grad_pre, TN)
        return carry

    lax.fori_loop(0, hidden // step, backward, 0)
    grad_first = norm_back(sum_ref[...], normed_ref[...], inverse_first)
    gf_ref[...] = grad_first
    grad_context = dot(wo_ref[...], grad_first.astype(BF16), NN).astype(BF16)
    gc_ref[...] = grad_context
    product = grad_context.astype(F32) * ct_ref[...].astype(F32)
    for head in range(heads):
        dl_ref[head] = jnp.sum(
            product[head * HEAD_DIM : (head + 1) * HEAD_DIM], axis=0, keepdims=True
        )


def edge_kernel(dk_ref, dv_ref, wk_ref, wve_ref, left_ref, right_ref):
    extent = dk_ref.shape[1]
    width = wk_ref.shape[0]

    def part_of(index, carry):
        part = span(index, 256)
        for out_ref, base in ((left_ref, 0), (right_ref, extent - SEQ_MOST)):
            side = slice(base, base + SEQ_MOST)
            out_ref[part, :] = (
                dot(wk_ref[part, :], dk_ref[:, side], NN)
                + dot(wve_ref[part, :], dv_ref[:, side], NN)
            ).astype(BF16)
        return carry

    lax.fori_loop(0, width // 256, part_of, 0)


def grads_kernel(
    dq_ref, dk_ref, dv_ref, xt_ref, xl_ref, xr_ref, gf_ref, wqe_ref, wk_ref, wve_ref,
    down_ref, up_ref, qs_ref, qb_ref, vs_ref, vb_ref,
    own_ref, gqs_ref, gqb_ref, gvs_ref, gvb_ref,
    sum_ref,
):
    width, rows = dq_ref.shape
    rank = up_ref.shape[0]
    own = slice(SEQ_MOST, SEQ_MOST + rows)

    def tokens_part(index, carry):
        part = span(index, 256)
        own_ref[part, :] = (
            gf_ref[part, :]
            + dot(wqe_ref[part, :], dq_ref[...], NN)
            + dot(wk_ref[part, :], dk_ref[:, own], NN)
            + dot(wve_ref[part, :], dv_ref[:, own], NN)
        )
        return carry

    lax.fori_loop(0, width // 256, tokens_part, 0)

    for value in (False, True):
        scale_ref, bias_ref = (vs_ref, vb_ref) if value else (qs_ref, qb_ref)
        out_scale, out_bias = (gvs_ref, gvb_ref) if value else (gqs_ref, gqb_ref)
        factor = 1.0 if value else QUERY_FOLD

        def outer(index, carry):
            part = span(index, 256)
            if value:
                total = dot(xt_ref[part, :], dv_ref[:, own], NT)
                total += dot(xl_ref[:, part], dv_ref[:, :SEQ_MOST], (((0,), (1,)), ((), ())))
                total += dot(xr_ref[:, part], dv_ref[:, SEQ_MOST + rows :], (((0,), (1,)), ((), ())))
            else:
                total = dot(xt_ref[part, :], dq_ref[...], NT)
            sum_ref[part, :] = total.astype(BF16)
            return carry

        lax.fori_loop(0, width // 256, outer, 0)
        out_bias[...] = jnp.zeros_like(out_bias)

        def inner(index, carry):
            part = span(index, 256)
            mixed = dot(down_ref[:, part], sum_ref[...], TN) * up_ref[part, :].astype(F32) * factor
            out_bias[...] += dot_rows(scale_ref[:, part], mixed)
            weighted = mixed * bias_ref[...]
            folded = weighted[:, :LANES]
            for at in range(LANES, width, LANES):
                folded = folded + weighted[:, at : at + LANES]
            out_scale[:, part] = jnp.sum(folded.T, axis=0, keepdims=True)
            return carry

        lax.fori_loop(0, rank // 256, inner, 0)


def dot_rows(scale, mixed):
    return jnp.sum(mixed * jnp.broadcast_to(scale, (LANES, scale.shape[1])).T[:, :1], axis=0, keepdims=True)


def finish_kernel(own_ref, left_ref, right_ref, out_ref):
    rows = own_ref.shape[1]
    total = own_ref[...]
    out_ref[:SEQ_MOST, :] = (total[:, :SEQ_MOST] + left_ref[...].astype(F32)).T.astype(BF16)
    out_ref[rows - SEQ_MOST :, :] = (
        total[:, rows - SEQ_MOST :] + right_ref[...].astype(F32)
    ).T.astype(BF16)


def call(kernel, outs, count, scratch=(), **kw):
    return pl.pallas_call(
        kernel,
        out_shape=outs,
        in_specs=[VMEM] * count,
        out_specs=[VMEM] * len(outs),
        scratch_shapes=list(scratch),
        compiler_params=PARAMS,
        **kw,
    )


def body(n_head, *arrays):
    (
        tokens, lengths, cotangent, w_query, w_key, w_value, w_output, vera_down, vera_up,
        query_scale, query_bias, value_scale, value_bias, hidden_in, hidden_out,
    ) = arrays
    rows, width = tokens.shape
    rank = vera_up.shape[0]
    heads = width // HEAD_DIM
    extent = rows + 2 * SEQ_MOST
    up_z = [(i, i + 1) for i in range(n_head - 1)]
    down_z = [(i + 1, i) for i in range(n_head - 1)]
    from_left = lax.ppermute(tokens[rows - SEQ_MOST :], "head", up_z)
    from_right = lax.ppermute(tokens[:SEQ_MOST], "head", down_z)
    hidden_in_t = lax.all_gather(hidden_in.T, ("seq", "head"), axis=0, tiled=True)
    hidden_out_t = lax.all_gather(hidden_out.T, ("seq", "head"), axis=0, tiled=True)
    hidden = hidden_in_t.shape[0]
    shift = (lax.axis_index("head") * rows - SEQ_MOST).astype(jnp.int32).reshape(1)
    qs, qb = query_scale[None], query_bias[None]
    vs, vb = value_scale[None], value_bias[None]
    tall = sds((width, rows), BF16)
    wide = sds((width, extent), BF16)
    square = sds((width, width), BF16)

    qt, kt, vt, xt, wqe, wve = call(
        project_kernel, [tall, tall, tall, tall, square, square], 10
    )(tokens, w_query, w_key, w_value, vera_down, vera_up, qs, qb, vs, vb)

    stats = sds((heads, 1, rows), F32)
    ct, ls, ke, ve = pl.pallas_call(
        attend_kernel,
        out_shape=[tall, stats, wide, wide],
        in_specs=[SMEM, SMEM] + [VMEM] * 7,
        out_specs=[VMEM] * 4,
        scratch_shapes=[
            pltpu.VMEM((width, SEQ_MOST), BF16),
            pltpu.VMEM((width, TILE_Q), F32),
            pltpu.VMEM((heads, 1, TILE_Q), F32),
            pltpu.VMEM((heads, 1, TILE_Q), F32),
            pltpu.VMEM((TILE_K, TILE_Q), F32),
        ],
        compiler_params=PARAMS,
    )(shift, lengths, qt, kt, vt, from_left, from_right, w_key, wve)

    tile = 256
    column = pl.BlockSpec((width, tile), lambda i: (0, i))
    row = pl.BlockSpec((tile, width), lambda i: (i, 0))
    layer_out, gf, gc, dl = pl.pallas_call(
        feed_kernel,
        grid=(rows // tile,),
        out_shape=[sds((rows, width), BF16), sds((width, rows), F32), tall, stats],
        in_specs=[column, column, row, VMEM, VMEM, VMEM],
        out_specs=[row, column, column, pl.BlockSpec((heads, 1, tile), lambda i: (0, 0, i))],
        scratch_shapes=[
            pltpu.VMEM((width, tile), F32),
            pltpu.VMEM((width, tile), BF16),
            pltpu.VMEM((hidden, tile), F32),
            pltpu.VMEM((width, tile), F32),
        ],
        compiler_params=PARAMS,
    )(xt, ct, cotangent, w_output, hidden_in_t, hidden_out_t)

    dq, dk, dv = pl.pallas_call(
        attend_back_kernel,
        out_shape=[tall, wide, wide],
        in_specs=[SMEM, SMEM] + [VMEM] * 6,
        out_specs=[VMEM] * 3,
        scratch_shapes=[
            pltpu.VMEM((width, TILE_Q), F32),
            pltpu.VMEM((width, extent), F32),
            pltpu.VMEM((width, extent), F32),
            pltpu.VMEM((TILE_K, TILE_Q), F32),
        ],
        compiler_params=PARAMS,
    )(shift, lengths, qt, ke, ve, ls, gc, dl)

    half = sds((width, SEQ_MOST), BF16)
    to_left, to_right = call(edge_kernel, [half, half], 4)(dk, dv, w_key, wve)
    right_part = lax.ppermute(to_left, "head", down_z)
    left_part = lax.ppermute(to_right, "head", up_z)
    own, gqs, gqb, gvs, gvb = call(
        grads_kernel,
        [
            sds((width, rows), F32), sds((1, rank), F32), sds((1, width), F32),
            sds((1, rank), F32), sds((1, width), F32),
        ],
        16,
        [pltpu.VMEM((width, width), BF16)],
    )(dq, dk, dv, xt, from_left, from_right, gf, wqe, w_key, wve, vera_down, vera_up, qs, qb, vs, vb)
    totals = lax.psum((gqs[0], gqb[0], gvs[0], gvb[0]), ("seq", "head"))
    (token_grad,) = call(finish_kernel, [sds((rows, width), BF16)], 3)(own, left_part, right_part)
    return (layer_out, token_grad, *totals)


def solution(mesh):
    return jax.shard_map(
        functools.partial(body, mesh.shape["head"]),
        mesh=mesh,
        in_specs=(
            P(("seq", "head"), None),
            P("seq", None),
            P(("seq", "head"), None),
            P(), P(), P(), P(), P(), P(), P(), P(), P(), P(),
            P(None, ("seq", "head")),
            P(None, ("seq", "head")),
        ),
        out_specs=(P(("seq", "head"), None), P(("seq", "head"), None), P(), P(), P(), P()),
        check_vma=False,
    )
```

time: 1050 us -> 355 us (0.34); the launches traced: 1030 us -> 352 us
  matrix products: 353 us -> 0 us
  Pallas kernels: 0 us -> 217 us
  waiting for transfers between devices: 253 us -> 56.9 us
  local copies, waits for them, and re-layouts: 164 us -> 4.69 us
  other arithmetic: 145 us -> 1.38 us
  loops' own time: 28.1 us -> 0 us
  starting transfers between devices: 35.9 us -> 15.8 us
    dot_general x73 -> x0, matrix products: 353 us -> none  [the longest x16 81.6 us: block_scores(): jnp.einsum('qhd,khd->hqk', query_block, key_block, preferred_element_type...]
    all_to_all x8 -> x0, waiting for transfers between devices: 252 us -> none  [the longest x1 36.5 us: body(): lax.all_to_all(grad_context, 'head', split_axis=1, concat_axis=0, tiled=T...]
    pallas_call x0 -> x7, Pallas kernels: none -> 217 us  [the longest x1 63.1 us: body(): pl.pallas_call(feed_kernel, grid=(rows // tile,), out_shape=[sds((rows, w...]
    dynamic_slice x96 -> x0, local copies, waits for them, and re-layouts: 84.2 us -> none  [the longest x16 18.2 us: block_scores(): lax.dynamic_slice_in_dim(key_pad, offset, window, 0)]
    convert_element_type x8 -> x0, other arithmetic: 75.7 us -> none  [one_block(): (probabilities * (grad_probs - delta_rows)).astype(jnp.bfloat16)]
    all_gather x2, waiting for transfers between devices: 0.02 us -> 50.2 us  [the longest x1 50.2 us: body(): lax.all_gather(hidden_out.T, ('seq', 'head'), axis=0, tiled=True)]
    all_to_all x8 -> x0, starting transfers between devices: 35.2 us -> none  [the longest x1 6.45 us: body(): lax.all_to_all(value_rows, 'head', split_axis=1, concat_axis=0, tiled=True)]
    dynamic_update_slice x16 -> x0, other arithmetic: 32 us -> none  [the longest x8 27.1 us: one_block(): lax.dynamic_update_slice_in_dim(value_grads, value_window, offset, 0)]
  transfers between devices with their start and end apart: 10 -> 6, of which waited for: 8 -> 3; matrix products, arithmetic and copies ran while one was open for 20% -> 1% of each run, Pallas kernels for 0% -> 26%
where the time goes in v1:
time: 355 us; the launch traced here: 352 us
  Pallas kernels  217 us (61%)
  waiting for transfers between devices  56.9 us (16%)
  blocking collectives  42 us (12%)
  starting transfers between devices  15.8 us (4%)
  between operations  14.1 us (4%)
  local copies, waits for them, and re-layouts  4.69 us (1%)
    pallas_call x1, Pallas kernels, body(): pl.pallas_call(feed_kernel, grid=(rows // tile,), out_shape=[sds((rows, w...  63.1 us
    pallas_call x1, Pallas kernels, body(): pl.pallas_call(attend_kernel, out_shape=[tall, stats, wide, wide], in_spe...  55.9 us
    pallas_call x1, Pallas kernels, body(): pl.pallas_call(attend_back_kernel, out_shape=[tall, wide, wide], in_specs...  50.7 us
    all_gather x1, waiting for transfers between devices, body(): lax.all_gather(hidden_out.T, ('seq', 'head'), axis=0, tiled=True)  50.2 us
    psum x1, blocking collectives, body(): totals = lax.psum((gqs[0], gqb[0], gvs[0], gvb[0]), ('seq', 'head'))  42 us
    pallas_call x1, Pallas kernels, body(): call(grads_kernel, [sds((width, rows), F32), sds((1, rank), F32), sds((1,...  22.5 us
    pallas_call x1, Pallas kernels, body(): call(project_kernel, [tall, tall, tall, tall, square, square], 10)  13.4 us
    pallas_call x1, Pallas kernels, body(): to_left, to_right = call(edge_kernel, [half, half], 4)(dk, dv, w_key, wve)  7.34 us
  transfers between devices with their start and end apart: 6, of which 3 were waited for; matrix products, arithmetic and copies ran while one was open for 1% of the time, Pallas kernels for 26%

profile of v1, /device:TPU:0, one launch (start us, length us, event | category | flops | bytes accessed | tf_op | source)
XLA Modules:
  0.0 351.8 jit_solution(8335755649314403959)
XLA Ops:
  7.2 0.0 all-gather.3.cloned.1.call-start
  7.2 0.7 all-gather.3.cloned.1.call-update
  7.9 0.0 all-gather.5.cloned.1.call-start
  7.9 0.7 all-gather.5.cloned.1.call-update
  8.6 0.0 copy-start.4
  8.7 0.0 copy-start.5
  8.7 1.5 fusion
  10.2 1.3 collective-permute-start.1
  11.5 5.6 %collective-permute-start = (bf16[512,768]{1,0:T(8,128)(2,1)S(1)}, bf16[512,768]{1,0:T(8,128)(2,1)S(1)}, u32[]{:S(2)}, u32[]{:S(2)}) collective-permute-start(bf16[512,768]{1,0:T(8,128)(2,1)S(1)} %get-tuple-element.59), channel_id=1, source_target_pairs={{0,1},{1,2},{2,3},{4,5},{5,6},{6,7},{8,9},{9,10},{10,11},{12,13},{... | collective-permute-start | bytes 2359304 | tf_op jit(solution)/shard_map/ppermute | solution.py:401
  17.1 0.0 copy-done.4
  17.1 0.6 broadcast_in_dim.13.qb_ref
  17.7 0.0 copy-done.5
  17.7 0.6 broadcast_in_dim.15.vb_ref
  18.2 13.4 %shard_map.190 = (bf16[768,1024]{1,0:T(8,128)(2,1)}, bf16[768,1024]{1,0:T(8,128)(2,1)}, bf16[768,1024]{1,0:T(8,128)(2,1)}, bf16[768,1024]{1,0:T(8,128)(2,1)}, bf...) custom-call(bf16[1024,768]{1,0:T(8,128)(2,1)} %x_ref.1, bf16[768,768]{1,0:T(8,128)(2,1)} %wq_ref.1, ...), custom_call_target="tpu_custom_call" | custom-call | tf_op jit(solution)/shard_map/pallas_call | solution.py:413
  31.6 4.1 %collective-permute-done.1.xr_ref = bf16[512,768]{1,0:T(8,128)(2,1)S(1)} collective-permute-done((bf16[512,768]{1,0:T(8,128)(2,1)S(1)}, bf16[512,768]{1,0:T(8,128)(2,1)S(1)}, u32[]{:S(2)}, u32[]{:S(2)}) %collective-permute-start.1) | collective-permute-done | bytes 786464 | tf_op jit(solution)/shard_map/ppermute | solution.py:402
  35.8 0.0 copy-start
  35.8 1.2 collective-permute-done.xl_ref
  37.0 0.0 copy-start.1
  37.0 0.0 copy-done
  37.0 0.9 copy-done.1
  37.8 55.9 %shard_map.191 = (bf16[768,1024]{1,0:T(8,128)(2,1)}, f32[12,1,1024]{2,1,0:T(1,128)}, bf16[768,2048]{1,0:T(8,128)(2,1)}, bf16[768,2048]{1,0:T(8,128)(2,1)}) custom-call(s32[1]{0:T(128)} %bitcast.2.shift_ref, s32[1,32]{1,0:T(1,128)} %len_ref.3, bf16[768,1024]{1,0:T(8,128)(2,1)} %get-tuple-element.31.qt_ref, bf16[768,1024]{1,0:T(8,128)(2,1)} %get-tuple-element.32.kt_ref, ...), custom_call_target="tpu_custom_call" | custom-call | tf_op jit(solution)/shard_map/pallas_call | solution.py:418
  93.7 0.0 all-gather.3.cloned.1.call-done.hi_ref
  93.7 50.2 %all-gather.5.cloned.1.call-done.ho_ref = bf16[3072,768]{1,0:T(8,128)(2,1)} async-done(((bf16[96,768]{1,0:T(8,128)(2,1)}), bf16[3072,768]{1,0:T(8,128)(2,1)}) %all-gather.5.cloned.1.call-update) | async-done | bytes 4718608 | tf_op jit(solution)/shard_map/all_gather | solution.py:404
  144.0 63.1 %shard_map.192 = (bf16[1024,768]{1,0:T(8,128)(2,1)}, f32[768,1024]{1,0:T(8,128)}, bf16[768,1024]{1,0:T(8,128)(2,1)}, f32[12,1,1024]{2,1,0:T(1,128)}) custom-call(bf16[768,1024]{1,0:T(8,128)(2,1)} %get-tuple-element.30.xt_ref, bf16[768,1024]{1,0:T(8,128)(2,1)} %get-tuple-element.35.ct_ref, bf16[1024,768]{1,0:T(8,128)(2,1)} %cot_ref.1, ...), custom_call_target="tpu_custom_call" | custom-call | tf_op jit(solution)/shard_map/pallas_call | solution.py:436
  207.1 50.7 %shard_map.193 = (bf16[768,1024]{1,0:T(8,128)(2,1)}, bf16[768,2048]{1,0:T(8,128)(2,1)}, bf16[768,2048]{1,0:T(8,128)(2,1)}) custom-call(s32[1]{0:T(128)} %bitcast.2.shift_ref, s32[1,32]{1,0:T(1,128)} %len_ref.3, bf16[768,1024]{1,0:T(8,128)(2,1)} %get-tuple-element.31.qt_ref, bf16[768,2048]{1,0:T(8,128)(2,1)} %get-tuple-element.37.ke_ref, ...), custom_call_target="tpu_custom_call" | custom-call | tf_op jit(solution)/shard_map/pallas_call | solution.py:451
  257.8 7.3 %shard_map.195 = (bf16[768,512]{1,0:T(8,128)(2,1)}, bf16[768,512]{1,0:T(8,128)(2,1)}) custom-call(bf16[768,2048]{1,0:T(8,128)(2,1)} %get-tuple-element.43.dk_ref, bf16[768,2048]{1,0:T(8,128)(2,1)} %get-tuple-element.44.dv_ref, bf16[768,768]{1,0:T(8,128)(2,1)} %wk_ref.7, bf16[768,768]{1,0:T(8,128)(2,1)} %get-tuple-element.34.wve_ref), custom_call_target="tpu_custom_call" | custom-call | tf_op jit(solution)/shard_map/pallas_call | solution.py:466
  265.1 7.3 %collective-permute-start.2 = (bf16[768,512]{1,0:T(8,128)(2,1)}, bf16[768,512]{1,0:T(8,128)(2,1)S(1)}, u32[]{:S(2)}, u32[]{:S(2)}) collective-permute-start(bf16[768,512]{1,0:T(8,128)(2,1)} %get-tuple-element.48), channel_id=1, source_target_pairs={{0,1},{1,2},{2,3},{4,5},{5,6},{6,7},{8,9},{9,10},{10,11},{12,13},{... | collective-permute-start | bytes 2359304 | tf_op jit(solution)/shard_map/ppermute | solution.py:468
  272.5 1.5 collective-permute-start.3
  273.9 22.5 %shard_map.194 = (f32[768,1024]{1,0:T(8,128)}, f32[1,1024]{1,0:T(1,128)}, f32[1,768]{1,0:T(1,128)}, f32[1,1024]{1,0:T(1,128)}, f32[1,768]{1,0:T(1,128)}) custom-call(bf16[768,1024]{1,0:T(8,128)(2,1)} %get-tuple-element.42.dq_ref, bf16[768,2048]{1,0:T(8,128)(2,1)} %get-tuple-element.43.dk_ref, bf16[768,2048]{1,0:T(8,128)(2,1)} %get-tuple-element.44.dv_ref, ...), custom_call_target="tpu_custom_call" | custom-call | tf_op jit(solution)/shard_map/pallas_call | solution.py:469
  296.4 0.7 reduce
  297.1 0.7 reduce.1
  297.8 42.0 %all-reduce = (f32[1024]{0:T(1024)}, f32[768]{0:T(1024)}, f32[1024]{0:T(1024)}, f32[768]{0:T(1024)}) all-reduce(f32[1024]{0:T(1024)} %bitcast.13, f32[768]{0:T(1024)S(1)} %reduce, f32[1024]{0:T(1024)} %bitcast.14, f32[768]{0:T(1024)S(1)} %reduce.1), channel_id=1, replica_groups=mesh['seq'=8,'head'=4] {'seq','head'}, use_global_device_ids=true, to_apply=%region_0.0 | all-reduce | flops 3584 | bytes 28672 | tf_op jit(solution)/shard_map/psum | solution.py:478
  339.9 0.0 collective-permute-done.2.left_ref
  339.9 0.0 copy-start.2
  339.9 0.0 collective-permute-done.3.right_ref
  339.9 0.0 copy-start.3
  339.9 0.9 copy-done.2
  340.8 0.3 copy-done.3
  341.0 4.0 %shard_map.196 = bf16[1024,768]{1,0:T(8,128)(2,1)} custom-call(f32[768,1024]{1,0:T(8,128)} %get-tuple-element.47.own_ref, bf16[768,512]{1,0:T(8,128)(2,1)} %copy-done.2, bf16[768,512]{1,0:T(8,128)(2,1)} %copy-done.3), custom_call_target="tpu_custom_call" | custom-call | tf_op jit(solution)/shard_map/pallas_call | solution.py:479
Async XLA Ops:
  7.2 86.6 %all-gather.3.cloned.1.call-start = ((), (), s32[]{:S(2)}) async-start(), calls=%async_computation | async-start | bytes 4866048 | tf_op jit(solution)/shard_map/all_gather | solution.py:403
  7.9 136.1 %all-gather.5.cloned.1.call-start = ((), (), s32[]{:S(2)}) async-start(), calls=%async_computation.1 | async-start | bytes 4866048 | tf_op jit(solution)/shard_map/all_gather | solution.py:404
  8.6 8.4 %copy-start.4 = (f32[768]{0:T(1024)S(1)}, f32[768]{0:T(1024)}, u32[]{:S(2)}) copy-start(f32[768]{0:T(1024)} %param.25) | copy-start | bytes 9220
  8.7 9.0 %copy-start.5 = (f32[768]{0:T(1024)S(1)}, f32[768]{0:T(1024)}, u32[]{:S(2)}) copy-start(f32[768]{0:T(1024)} %param.27) | copy-start | bytes 9220
  10.2 25.6 %collective-permute-start.1 = (bf16[512,768]{1,0:T(8,128)(2,1)S(1)}, bf16[512,768]{1,0:T(8,128)(2,1)S(1)}, u32[]{:S(2)}, u32[]{:S(2)}) collective-permute-start(bf16[512,768]{1,0:T(8,128)(2,1)S(1)} %get-tuple-element.58), channel_id=1, source_target_pairs={{1,0},{2,1},{3,2},{5,4},{6,5},{7,6},{9,8},{10,9},{11,10},{13,12},{... | collective-permute-start | bytes 2359304 | tf_op jit(solution)/shard_map/ppermute | solution.py:402
  11.5 25.5 %collective-permute-start = (bf16[512,768]{1,0:T(8,128)(2,1)S(1)}, bf16[512,768]{1,0:T(8,128)(2,1)S(1)}, u32[]{:S(2)}, u32[]{:S(2)}) collective-permute-start(bf16[512,768]{1,0:T(8,128)(2,1)S(1)} %get-tuple-element.59), channel_id=1, source_target_pairs={{0,1},{1,2},{2,3},{4,5},{5,6},{6,7},{8,9},{9,10},{10,11},{12,13},{... | collective-permute-start | bytes 2359304 | tf_op jit(solution)/shard_map/ppermute | solution.py:401
  35.8 1.2 copy-start
  37.0 0.9 copy-start.1
  265.1 74.7 %collective-permute-start.2 = (bf16[768,512]{1,0:T(8,128)(2,1)}, bf16[768,512]{1,0:T(8,128)(2,1)S(1)}, u32[]{:S(2)}, u32[]{:S(2)}) collective-permute-start(bf16[768,512]{1,0:T(8,128)(2,1)} %get-tuple-element.48), channel_id=1, source_target_pairs={{0,1},{1,2},{2,3},{4,5},{5,6},{6,7},{8,9},{9,10},{10,11},{12,13},{... | collective-permute-start | bytes 2359304 | tf_op jit(solution)/shard_map/ppermute | solution.py:468
  272.5 67.4 %collective-permute-start.3 = (bf16[768,512]{1,0:T(8,128)(2,1)}, bf16[768,512]{1,0:T(8,128)(2,1)S(1)}, u32[]{:S(2)}, u32[]{:S(2)}) collective-permute-start(bf16[768,512]{1,0:T(8,128)(2,1)} %get-tuple-element.49), channel_id=1, source_target_pairs={{1,0},{2,1},{3,2},{5,4},{6,5},{7,6},{9,8},{10,9},{11,10},{13,12},{... | collective-permute-start | bytes 2359304 | tf_op jit(solution)/shard_map/ppermute | solution.py:467
  339.9 0.9 copy-start.2
  339.9 1.2 copy-start.3
Sparse Core Ops, SparseCore 0:
  10.8 67.6 all-gather.2
  81.3 62.6 all-gather.4

commit v2 on v1

v2 whole, which is shorter than its diff:
```python
import functools
import math

import jax
import jax.numpy as jnp
from jax import lax
from jax.experimental import pallas as pl
from jax.experimental.pallas import tpu as pltpu
from jax.sharding import PartitionSpec as P

HEAD_DIM = 64
SEQ_MOST = 512
EPSILON = 1e-05
HIDDEN = -1e30
LN2 = math.log(2.0)
QUERY_FOLD = HEAD_DIM ** (-0.5) / LN2
TILE_Q = 256
TILE_K = 256
LANES = 128
NN = (((1,), (0,)), ((), ()))
NT = (((1,), (1,)), ((), ()))
TN = (((0,), (0,)), ((), ()))
F32 = jnp.float32
BF16 = jnp.bfloat16
VMEM = pl.BlockSpec(memory_space=pltpu.VMEM)
SMEM = pl.BlockSpec(memory_space=pltpu.SMEM)
MESH = pl.DeviceIdType.MESH
ANY = pl.BlockSpec(memory_space=pl.ANY)
PARAMS = pltpu.CompilerParams(vmem_limit_bytes=58 << 20)


def dot(left, right, form):
    return lax.dot_general(left, right, form, preferred_element_type=F32)


def sds(shape, dtype):
    return jax.ShapeDtypeStruct(shape, dtype)


def span(index, size):
    if isinstance(index, int):
        return pl.ds(index * size, size)
    return pl.ds(pl.multiple_of(index * size, size), size)


def bounds(len_ref, first, count):
    row = first + lax.broadcasted_iota(jnp.int32, (1, count), 1)
    low = jnp.zeros((1, count), jnp.int32)
    high = jnp.full((1, count), 1 << 30, jnp.int32)
    end = 0
    for i in range(len_ref.shape[1]):
        end = end + len_ref[0, i]
        low = jnp.where(row >= end, end, low)
        high = jnp.where(row < end, jnp.minimum(high, end), high)
    return low, high


def reach(len_ref, first, count):
    last = first + count - 1
    end, least, most = 0, 0, 1 << 30
    for i in range(len_ref.shape[1]):
        end = end + len_ref[0, i]
        least = jnp.where(first >= end, end, least)
        most = jnp.where(last < end, jnp.minimum(most, end), most)
    return least, most


def key_range(least, most, shift, extent):
    start = (least - shift) // LANES
    tiles = (most - shift - start * LANES + TILE_K - 1) // TILE_K
    start = jnp.minimum(start, (extent - tiles * TILE_K) // LANES)
    return start, tiles


def other(index, bit):
    return index + bit - 2 * bit * ((index // bit) % 2)


def remote(src, dst, send, recv, seq, head):
    return pltpu.make_async_remote_copy(
        src_ref=src, dst_ref=dst, send_sem=send, recv_sem=recv, device_id=(seq, head), device_id_type=MESH
    )


class Gather:
    def __init__(self, own, full, sems, seq, head, n_head):
        self.own, self.full, self.sems = own, full, sems
        self.seq, self.head, self.n = seq, head, n_head
        self.shard = own.shape[1]
        self.near_x, self.near_y = other(seq, 2), other(seq, 4)
        self.far = other(self.near_x, 4)

    def rows(self, seq, k):
        origin = (self.head + self.n - k) % self.n
        return self.full.at[:, span(seq * self.n + origin, self.shard), :]

    def column(self, seq):
        return self.full.at[:, span(seq, self.n * self.shard), :]

    def pair(self, kind, k):
        return self.sems.at[2 * (4 * kind + k)], self.sems.at[2 * (4 * kind + k) + 1]

    def local(self):
        return pltpu.make_async_copy(self.own, self.rows(self.seq, 0), self.sems.at[0])

    def over_z(self, k):
        return remote(self.own, self.rows(self.seq, 0), *self.pair(0, k), self.seq, (self.head + k) % self.n)

    def over_x(self, k):
        src = self.own if k == 0 else self.rows(self.seq, k)
        return remote(src, self.rows(self.seq, k), *self.pair(1, k), self.near_x, self.head)

    def over_y(self, k):
        src = self.own if k == 0 else self.rows(self.seq, k)
        return remote(src, self.rows(self.seq, k), *self.pair(2, k), self.near_y, self.head)

    def onward(self, k):
        src, to = (self.near_x, self.near_y) if k < 2 else (self.near_y, self.near_x)
        return remote(self.rows(src, k), self.rows(src, k), *self.pair(3, k), to, self.head)

    def across(self, group):
        seq = (self.seq, self.near_x, self.near_y, self.far)[group]
        return remote(
            self.column(seq), self.column(seq), *self.pair(4, group), other(self.seq, 1), self.head
        )


def front_kernel(n_head, n_seq, gather, *refs):
    (
        len_ref, x_ref, wq_ref, wk_ref, wv_ref, down_ref, up_ref, qs_ref, qb_ref, vs_ref, vb_ref,
    ) = refs[:11]
    refs = refs[11:]
    if gather:
        (hi_ref, ho_ref), refs = refs[:2], refs[2:]
    (ct_ref, ls_ref, qt_ref, ke_ref, ve_ref, xt_ref, lt_ref, rt_ref, wqe_ref, wve_ref), refs = refs[:10], refs[10:]
    if gather:
        full_ref, refs = refs[0], refs[1:]
    (
        xl_ref, xr_ref, acc_ref, high_ref, total_ref, low_row, high_row, bias_ref, halo_sem,
    ), refs = refs[:9], refs[9:]
    rows, width = x_ref.shape
    heads = width // HEAD_DIM
    seq, head_at = lax.axis_index("seq"), lax.axis_index("head")
    shift = head_at * rows - SEQ_MOST
    first_z, last_z = head_at == 0, head_at == n_head - 1

    barrier = pltpu.get_barrier_semaphore()
    partners = [(seq, (head_at + k) % n_head) for k in range(1, n_head)]
    if gather:
        partners += [(other(seq, bit), head_at) for bit in (1, 2, 4)]
        own_ref, gather_sem = refs
        own_ref[0] = hi_ref[...].T
        own_ref[1] = ho_ref[...].T
    for partner in partners:
        pl.semaphore_signal(barrier, inc=1, device_id=partner, device_id_type=MESH)
    pl.semaphore_wait(barrier, len(partners))

    to_right = remote(
        x_ref.at[rows - SEQ_MOST :], xl_ref, halo_sem.at[0], halo_sem.at[1], seq, (head_at + 1) % n_head
    )
    to_left = remote(
        x_ref.at[:SEQ_MOST], xr_ref, halo_sem.at[2], halo_sem.at[3], seq, (head_at + n_head - 1) % n_head
    )
    if gather:
        g = Gather(own_ref, full_ref, gather_sem, seq, head_at, n_head)
        for k in (1, 3, 2):
            g.over_z(k).start()
        g.over_x(0).start()
        g.over_y(0).start()
        g.local().start()

    @pl.when(head_at < n_head - 1)
    def _():
        to_right.start()

    @pl.when(head_at > 0)
    def _():
        to_left.start()

    def fold(index, carry):
        part = span(index, 256)
        down = down_ref[part, :].astype(F32)
        side_q = dot((down * qs_ref[...]).astype(BF16), up_ref[...], NN) * qb_ref[...]
        wqe_ref[part, :] = ((wq_ref[part, :].astype(F32) + side_q) * QUERY_FOLD).astype(BF16)
        side_v = dot((down * vs_ref[...]).astype(BF16), up_ref[...], NN) * vb_ref[...]
        wve_ref[part, :] = (wv_ref[part, :].astype(F32) + side_v).astype(BF16)
        return carry

    lax.fori_loop(0, width // 256, fold, 0)

    def flip(index, carry):
        part = span(index, 256)
        xt_ref[:, part] = x_ref[part, :].T
        return carry

    lax.fori_loop(0, rows // 256, flip, 0)
    own = slice(SEQ_MOST, SEQ_MOST + rows)

    def apply(index, carry):
        part = span(index, 256)
        qt_ref[part, :] = dot(wqe_ref[:, part], xt_ref[...], TN).astype(BF16)
        ke_ref[part, own] = dot(wk_ref[:, part], xt_ref[...], TN).astype(BF16)
        ve_ref[part, own] = dot(wve_ref[:, part], xt_ref[...], TN).astype(BF16)
        return carry

    lax.fori_loop(0, width // 256, apply, 0)

    low, high = bounds(len_ref, shift + SEQ_MOST, rows)
    low_row[...] = low
    high_row[...] = high
    acc_ref[...] = jnp.zeros_like(acc_ref)
    high_ref[...] = jnp.full_like(high_ref, HIDDEN)
    total_ref[...] = jnp.zeros_like(total_ref)

    def block(tile, key_tile):
        q_part, k_part = span(tile, TILE_Q), span(key_tile, TILE_K)
        key = shift + key_tile * TILE_K + lax.broadcasted_iota(jnp.int32, (TILE_K, TILE_Q), 0)
        bias_ref[...] = jnp.where((key >= low_row[:, q_part]) & (key < high_row[:, q_part]), 0.0, HIDDEN)
        bias = bias_ref[...]
        parts = [span(head, HEAD_DIM) for head in range(heads)]
        before = [high_ref[head, :, q_part] for head in range(heads)]
        totals = [total_ref[head, :, q_part] for head in range(heads)]
        sums = [acc_ref[part, q_part] for part in parts]
        scores = [dot(ke_ref[part, k_part], qt_ref[part, q_part], TN) + bias for part in parts]
        best = [jnp.maximum(b, jnp.max(v, axis=0, keepdims=True)) for b, v in zip(before, scores)]
        probs = [jnp.exp2(v - b) for v, b in zip(scores, best)]
        fade = [jnp.exp2(a - b) for a, b in zip(before, best)]
        totals = [t * f + jnp.sum(p, axis=0, keepdims=True) for t, f, p in zip(totals, fade, probs)]
        sums = [
            a * f + dot(ve_ref[part, k_part], p.astype(BF16), NN)
            for a, f, p, part in zip(sums, fade, probs, parts)
        ]
        for head, part, b, t, a in zip(range(heads), parts, best, totals, sums):
            high_ref[head, :, q_part] = b
            total_ref[head, :, q_part] = t
            acc_ref[part, q_part] = a

    def own_block(index, carry):
        tile, at = (index + 1) // 4, (index + 1) % 4
        block(tile, at + 1 + (tile + 1) // 2)
        return carry

    def left_block(index, carry):
        block(index // 2, (index + 1) // 2)
        return carry

    def right_block(index, carry):
        block(2 + (index + 1) // 2, 6 + index // 2)
        return carry

    if gather:
        g.over_x(0).wait_recv()
        g.onward(0).start()
    lax.fori_loop(0, 3, own_block, 0)
    if gather:
        g.over_z(1).wait_recv()
        g.over_x(1).start()
        g.over_y(1).start()
    lax.fori_loop(3, 7, own_block, 0)
    if gather:
        g.over_z(3).wait_recv()
        g.over_x(3).start()
        g.over_y(3).start()
        g.over_x(1).wait_recv()
        g.onward(1).start()
    lax.fori_loop(7, 11, own_block, 0)
    if gather:
        g.over_z(2).wait_recv()
        g.over_x(2).start()
        g.over_y(2).start()
        g.local().wait()
        g.across(0).start()
    lax.fori_loop(11, 14, own_block, 0)

    for absent, copy, side_ref, flat_ref, base in (
        (first_z, to_right, xl_ref, lt_ref, 0),
        (last_z, to_left, xr_ref, rt_ref, SEQ_MOST + rows),
    ):

        @pl.when(absent)
        def _():
            side_ref[...] = jnp.zeros_like(side_ref)

        @pl.when(jnp.logical_not(absent))
        def _():
            copy.wait_recv()

        def edge_flip(index, carry):
            part = span(index, 256)
            flat_ref[:, part] = side_ref[part, :].T
            return carry

        lax.fori_loop(0, SEQ_MOST // 256, edge_flip, 0)

        def edge(index, carry):
            part = span(index, 256)
            ke_ref[part, base : base + SEQ_MOST] = dot(wk_ref[:, part], flat_ref[...], TN).astype(BF16)
            ve_ref[part, base : base + SEQ_MOST] = dot(wve_ref[:, part], flat_ref[...], TN).astype(BF16)
            return carry

        lax.fori_loop(0, width // 256, edge, 0)

    if gather:
        g.over_y(3).wait_recv()
        g.onward(3).start()
    lax.fori_loop(0, 3, left_block, 0)
    if gather:
        g.over_y(2).wait_recv()
        g.onward(2).start()
        for k in (2, 3):
            g.over_x(k).wait_recv()
        g.across(1).start()
        for k in (0, 1):
            g.over_y(k).wait_recv()
        g.across(2).start()
    lax.fori_loop(0, 3, right_block, 0)

    for head in range(heads):
        part = pl.ds(head * HEAD_DIM, HEAD_DIM)
        total = total_ref[head]
        ct_ref[part, :] = (acc_ref[part, :] / total).astype(BF16)
        ls_ref[head] = high_ref[head] + jnp.log2(total)

    @pl.when(head_at < n_head - 1)
    def _():
        to_right.wait_send()

    @pl.when(head_at > 0)
    def _():
        to_left.wait_send()

    if gather:
        for k in range(4):
            g.onward(k).wait_recv()
        g.across(3).start()
        for k in (1, 2, 3):
            g.over_z(k).wait_send()
        for k in range(4):
            g.over_x(k).wait_send()
            g.over_y(k).wait_send()
            g.onward(k).wait_send()
        for k, seq_at in enumerate((seq, g.near_x, g.near_y, g.far)):
            g.across(k).wait_send()
            came = g.column(other(seq_at, 1))
            remote(came, came, *g.pair(4, k), other(seq, 1), head_at).wait_recv()


def attend_back_kernel(
    shift_ref, len_ref, qt_ref, ke_ref, ve_ref, ls_ref, gt_ref, dl_ref,
    dq_ref, dk_ref, dv_ref,
    dq_acc, dk_acc, dv_acc, bias_ref,
):
    width, rows = qt_ref.shape
    extent = ke_ref.shape[1]
    heads = width // HEAD_DIM
    shift = shift_ref[0]
    dk_acc[...] = jnp.zeros_like(dk_acc)
    dv_acc[...] = jnp.zeros_like(dv_acc)

    def query_tile(tile, carry):
        first = shift + SEQ_MOST + tile * TILE_Q
        low, high = bounds(len_ref, first, TILE_Q)
        least, most = reach(len_ref, first, TILE_Q)
        start, tiles = key_range(least, most, shift, extent)
        q_part = span(tile, TILE_Q)
        dq_acc[...] = jnp.zeros_like(dq_acc)

        def key_tile(step, inner):
            base = pl.multiple_of((start + step * (TILE_K // LANES)) * LANES, LANES)
            k_part = pl.ds(base, TILE_K)
            key = shift + base + lax.broadcasted_iota(jnp.int32, (TILE_K, TILE_Q), 0)
            bias_ref[...] = jnp.where((key >= low) & (key < high), 0.0, HIDDEN)

            def group(index):
                heads_of = [index * 6 + sub for sub in range(6)]
                parts = [span(head, HEAD_DIM) for head in heads_of]
                bias = bias_ref[...]
                scores = [dot(ke_ref[part, k_part], qt_ref[part, q_part], TN) + bias for part in parts]
                grad_probs = [dot(ve_ref[part, k_part], gt_ref[part, q_part], TN) for part in parts]
                probs = [jnp.exp2(v - ls_ref[head, :, q_part]) for head, v in zip(heads_of, scores)]
                slopes = [
                    (p * (g - dl_ref[head, :, q_part])).astype(BF16)
                    for head, p, g in zip(heads_of, probs, grad_probs)
                ]
                for part, p, d in zip(parts, probs, slopes):
                    dv_acc[part, k_part] += dot(gt_ref[part, q_part], p.astype(BF16), NT)
                    dk_acc[part, k_part] += dot(qt_ref[part, q_part], d, NT)
                    dq_acc[part, :] += dot(ke_ref[part, k_part], d, NN)

            for index in range(heads // 6):
                group(index)
            return inner

        lax.fori_loop(0, tiles, key_tile, 0)
        dq_ref[:, q_part] = (dq_acc[...] * LN2).astype(BF16)
        return carry

    lax.fori_loop(0, rows // TILE_Q, query_tile, 0)
    dk_ref[...] = (dk_acc[...] * LN2).astype(BF16)
    dv_ref[...] = dv_acc[...].astype(BF16)


def norm(values):
    center = values - jnp.mean(values, axis=0, keepdims=True)
    inverse = lax.rsqrt(jnp.mean(center * center, axis=0, keepdims=True) + EPSILON)
    return center * inverse, inverse


def norm_back(gradient, normed, inverse):
    centered = gradient - jnp.mean(gradient, axis=0, keepdims=True)
    return inverse * (centered - normed * jnp.mean(gradient * normed, axis=0, keepdims=True))


def gelu_parts(x):
    bell = jnp.exp2((-0.5 / LN2) * (x * x))
    t = 1.0 / (1.0 + (0.3275911 * math.sqrt(0.5)) * jnp.abs(x))
    poly = t * (0.127414796 + t * (-0.142248368 + t * (0.710706870 + t * (-0.726576013 + t * 0.530702714))))
    tail = poly * bell
    normal = jnp.where(x >= 0, 1.0 - tail, tail)
    return x * normal, normal + x * (bell * (1.0 / math.sqrt(2.0 * math.pi)))


def feed_kernel(
    xt_ref, ct_ref, cot_ref, wo_ref, w_ref,
    out_ref, gf_ref, gc_ref, dl_ref,
    normed_ref, low_ref, slope_ref, sum_ref, act_ref, pre_ref,
):
    width = xt_ref.shape[0]
    hidden = w_ref.shape[1]
    step = act_ref.shape[1]
    heads = width // HEAD_DIM
    pieces = [pl.ds(at, step) for at in range(0, hidden, step)]

    def sweep(first, second, change):
        count = len(pieces)
        pre_ref[0] = dot(w_ref[first, pieces[0], :], low_ref[...], NN)
        for at in range(count):
            if at + 1 < count:
                pre_ref[(at + 1) % 2] = dot(w_ref[first, pieces[at + 1], :], low_ref[...], NN)
            act_ref[at % 2] = change(pieces[at], pre_ref[at % 2]).astype(BF16)
            if at > 0:
                sum_ref[...] += dot(w_ref[second, pieces[at - 1], :], act_ref[(at - 1) % 2], TN)
        sum_ref[...] += dot(w_ref[second, pieces[-1], :], act_ref[(count - 1) % 2], TN)

    def forward(piece, pre):
        act, slope = gelu_parts(pre)
        slope_ref[piece, :] = slope
        return act

    attended = dot(wo_ref[...], ct_ref[...], TN)
    normed, inverse_first = norm(xt_ref[...].astype(F32) + attended)
    normed_ref[...] = normed
    low_ref[...] = normed.astype(BF16)
    sum_ref[...] = normed
    sweep(0, 1, forward)
    layer_out, inverse_second = norm(sum_ref[...])
    out_ref[...] = layer_out.T.astype(BF16)
    grad = norm_back(cot_ref[...].astype(F32).T, layer_out, inverse_second)
    sum_ref[...] = grad
    low_ref[...] = grad.astype(BF16)
    sweep(1, 0, lambda piece, upstream: slope_ref[piece, :] * upstream)
    grad_first = norm_back(sum_ref[...], normed_ref[...], inverse_first)
    gf_ref[...] = grad_first
    grad_context = dot(wo_ref[...], grad_first.astype(BF16), NN).astype(BF16)
    gc_ref[...] = grad_context
    product = grad_context.astype(F32) * ct_ref[...].astype(F32)
    for head in range(heads):
        dl_ref[head] = jnp.sum(
            product[head * HEAD_DIM : (head + 1) * HEAD_DIM], axis=0, keepdims=True
        )


def edge_kernel(dk_ref, dv_ref, wk_ref, wve_ref, left_ref, right_ref):
    extent = dk_ref.shape[1]
    width = wk_ref.shape[0]

    def part_of(index, carry):
        part = span(index, 256)
        for out_ref, base in ((left_ref, 0), (right_ref, extent - SEQ_MOST)):
            side = slice(base, base + SEQ_MOST)
            out_ref[part, :] = (
                dot(wk_ref[part, :], dk_ref[:, side], NN)
                + dot(wve_ref[part, :], dv_ref[:, side], NN)
            ).astype(BF16)
        return carry

    lax.fori_loop(0, width // 256, part_of, 0)


def grads_kernel(
    dq_ref, dk_ref, dv_ref, xt_ref, xl_ref, xr_ref, gf_ref, wqe_ref, wk_ref, wve_ref,
    down_ref, up_ref, qs_ref, qb_ref, vs_ref, vb_ref,
    own_ref, gqs_ref, gqb_ref, gvs_ref, gvb_ref,
    sum_ref,
):
    width, rows = dq_ref.shape
    rank = up_ref.shape[0]
    own = slice(SEQ_MOST, SEQ_MOST + rows)

    def tokens_part(index, carry):
        part = span(index, 256)
        own_ref[part, :] = (
            gf_ref[part, :]
            + dot(wqe_ref[part, :], dq_ref[...], NN)
            + dot(wk_ref[part, :], dk_ref[:, own], NN)
            + dot(wve_ref[part, :], dv_ref[:, own], NN)
        )
        return carry

    lax.fori_loop(0, width // 256, tokens_part, 0)

    for value in (False, True):
        scale_ref, bias_ref = (vs_ref, vb_ref) if value else (qs_ref, qb_ref)
        out_scale, out_bias = (gvs_ref, gvb_ref) if value else (gqs_ref, gqb_ref)
        factor = 1.0 if value else QUERY_FOLD

        def outer(index, carry):
            part = span(index, 256)
            if value:
                total = dot(xt_ref[part, :], dv_ref[:, own], NT)
                total += dot(xl_ref[part, :], dv_ref[:, :SEQ_MOST], NT)
                total += dot(xr_ref[part, :], dv_ref[:, SEQ_MOST + rows :], NT)
            else:
                total = dot(xt_ref[part, :], dq_ref[...], NT)
            sum_ref[part, :] = total.astype(BF16)
            return carry

        lax.fori_loop(0, width // 256, outer, 0)
        out_bias[...] = jnp.zeros_like(out_bias)

        def inner(index, carry):
            part = span(index, 256)
            mixed = dot(down_ref[:, part], sum_ref[...], TN) * up_ref[part, :].astype(F32) * factor
            out_bias[...] += dot_rows(scale_ref[:, part], mixed)
            weighted = mixed * bias_ref[...]
            folded = weighted[:, :LANES]
            for at in range(LANES, width, LANES):
                folded = folded + weighted[:, at : at + LANES]
            out_scale[:, part] = jnp.sum(folded.T, axis=0, keepdims=True)
            return carry

        lax.fori_loop(0, rank // 256, inner, 0)


def dot_rows(scale, mixed):
    return jnp.sum(mixed * jnp.broadcast_to(scale, (LANES, scale.shape[1])).T[:, :1], axis=0, keepdims=True)


def finish_kernel(own_ref, left_ref, right_ref, out_ref):
    rows = own_ref.shape[1]
    total = own_ref[...]
    out_ref[:SEQ_MOST, :] = (total[:, :SEQ_MOST] + left_ref[...].astype(F32)).T.astype(BF16)
    out_ref[rows - SEQ_MOST :, :] = (
        total[:, rows - SEQ_MOST :] + right_ref[...].astype(F32)
    ).T.astype(BF16)


def call(kernel, outs, count, scratch=(), scalars=0):
    return pl.pallas_call(
        kernel,
        out_shape=outs,
        in_specs=[SMEM] * scalars + [VMEM] * count,
        out_specs=[VMEM] * len(outs),
        scratch_shapes=list(scratch),
        compiler_params=PARAMS,
    )


def front(n_head, n_seq, lengths, tokens, w_query, w_key, w_value, vera, shards):
    rows, width = tokens.shape
    heads = width // HEAD_DIM
    extent = rows + 2 * SEQ_MOST
    tall, wide = sds((width, rows), BF16), sds((width, extent), BF16)
    square, half = sds((width, width), BF16), sds((width, SEQ_MOST), BF16)
    outs = [tall, sds((heads, 1, rows), F32), tall, wide, wide, tall, half, half, square, square]
    scratch = [
        pltpu.VMEM((SEQ_MOST, width), BF16),
        pltpu.VMEM((SEQ_MOST, width), BF16),
        pltpu.VMEM((width, rows), F32),
        pltpu.VMEM((heads, 1, rows), F32),
        pltpu.VMEM((heads, 1, rows), F32),
        pltpu.VMEM((1, rows), jnp.int32),
        pltpu.VMEM((1, rows), jnp.int32),
        pltpu.VMEM((TILE_K, TILE_Q), F32),
        pltpu.SemaphoreType.DMA((4,)),
    ]
    gather = len(shards) > 0
    specs = [VMEM] * len(outs)
    if gather:
        shard = shards[0].shape[1]
        outs.append(sds((2, n_head * n_seq * shard, width), BF16))
        specs.append(ANY)
        scratch += [pltpu.VMEM((2, shard, width), BF16), pltpu.SemaphoreType.DMA((40,))]
    return pl.pallas_call(
        functools.partial(front_kernel, n_head, n_seq, gather),
        out_shape=outs,
        in_specs=[SMEM] + [VMEM] * (10 + len(shards)),
        out_specs=specs,
        scratch_shapes=scratch,
        compiler_params=pltpu.CompilerParams(
            vmem_limit_bytes=58 << 20, collective_id=0, has_side_effects=True
        ),
    )(lengths, tokens, w_query, w_key, w_value, *vera, *shards)


def feed(xt, ct, cotangent, w_output, weights):
    width, rows = xt.shape
    hidden = weights.shape[1]
    heads = width // HEAD_DIM
    tile, step = 512, 768
    column = pl.BlockSpec((width, tile), lambda i: (0, i))
    row = pl.BlockSpec((tile, width), lambda i: (i, 0))
    return pl.pallas_call(
        feed_kernel,
        grid=(rows // tile,),
        out_shape=[
            sds((rows, width), BF16), sds((width, rows), F32), sds((width, rows), BF16),
            sds((heads, 1, rows), F32),
        ],
        in_specs=[column, column, row, VMEM, VMEM],
        out_specs=[row, column, column, pl.BlockSpec((heads, 1, tile), lambda i: (0, 0, i))],
        scratch_shapes=[
            pltpu.VMEM((width, tile), F32),
            pltpu.VMEM((width, tile), BF16),
            pltpu.VMEM((hidden, tile), F32),
            pltpu.VMEM((width, tile), F32),
            pltpu.VMEM((2, step, tile), BF16),
            pltpu.VMEM((2, step, tile), F32),
        ],
        compiler_params=PARAMS,
    )(xt, ct, cotangent, w_output, weights)


def attend_back(shift, lengths, qt, ke, ve, ls, gc, dl):
    width, rows = qt.shape
    extent = ke.shape[1]
    wide = sds((width, extent), BF16)
    return call(
        attend_back_kernel,
        [sds((width, rows), BF16), wide, wide],
        6,
        [
            pltpu.VMEM((width, TILE_Q), F32),
            pltpu.VMEM((width, extent), F32),
            pltpu.VMEM((width, extent), F32),
            pltpu.VMEM((TILE_K, TILE_Q), F32),
        ],
        2,
    )(shift, lengths, qt, ke, ve, ls, gc, dl)


def edges(dk, dv, w_key, wve):
    half = sds((dk.shape[0], SEQ_MOST), BF16)
    return call(edge_kernel, [half, half], 4)(dk, dv, w_key, wve)


def grads(dq, *rest):
    width, rows = dq.shape
    rank = rest[-5].shape[0]
    return call(
        grads_kernel,
        [
            sds((width, rows), F32), sds((1, rank), F32), sds((1, width), F32),
            sds((1, rank), F32), sds((1, width), F32),
        ],
        16,
        [pltpu.VMEM((width, width), BF16)],
    )(dq, *rest)


def body(n_seq, n_head, *arrays):
    (
        tokens, lengths, cotangent, w_query, w_key, w_value, w_output, vera_down, vera_up,
        query_scale, query_bias, value_scale, value_bias, hidden_in, hidden_out,
    ) = arrays
    rows, width = tokens.shape
    up_z = [(i, i + 1) for i in range(n_head - 1)]
    down_z = [(i + 1, i) for i in range(n_head - 1)]
    shift = (lax.axis_index("head") * rows - SEQ_MOST).astype(jnp.int32).reshape(1)
    vera = (vera_down, vera_up, query_scale[None], query_bias[None], value_scale[None], value_bias[None])
    fused = (n_seq, n_head) == (8, 4)
    shards = (hidden_in, hidden_out) if fused else ()
    ct, ls, qt, ke, ve, xt, lt, rt, wqe, wve, *full = front(
        n_head, n_seq, lengths, tokens, w_query, w_key, w_value, vera, shards
    )
    if fused:
        (weights,) = full
    else:
        weights = lax.all_gather(
            jnp.stack([hidden_in.T, hidden_out.T]), ("seq", "head"), axis=1, tiled=True
        )
    layer_out, gf, gc, dl = feed(xt, ct, cotangent, w_output, weights)
    dq, dk, dv = attend_back(shift, lengths, qt, ke, ve, ls, gc, dl)
    to_left, to_right = edges(dk, dv, w_key, wve)
    right_part = lax.ppermute(to_left, "head", down_z)
    left_part = lax.ppermute(to_right, "head", up_z)
    own, gqs, gqb, gvs, gvb = grads(dq, dk, dv, xt, lt, rt, gf, wqe, w_key, wve, *vera)
    totals = lax.psum((gqs[0], gqb[0], gvs[0], gvb[0]), ("seq", "head"))
    (token_grad,) = call(finish_kernel, [sds((rows, width), BF16)], 3)(own, left_part, right_part)
    return (layer_out, token_grad, *totals)


def solution(mesh):
    return jax.shard_map(
        functools.partial(body, mesh.shape["seq"], mesh.shape["head"]),
        mesh=mesh,
        in_specs=(
            P(("seq", "head"), None),
            P("seq", None),
            P(("seq", "head"), None),
            P(), P(), P(), P(), P(), P(), P(), P(), P(), P(),
            P(None, ("seq", "head")),
            P(None, ("seq", "head")),
        ),
        out_specs=(P(("seq", "head"), None), P(("seq", "head"), None), P(), P(), P(), P()),
        check_vma=False,
    )
```

time: 355 us -> 245 us (0.69)
  waiting for transfers between devices: 56.9 us -> 0.01 us
  Pallas kernels: 217 us -> 174 us
  between operations: 14.1 us -> 0.69 us
  blocking collectives: 42 us -> 45.6 us
    all_gather x2 -> x0, waiting for transfers between devices: 50.2 us -> none  [the longest x1 50.2 us: body(): lax.all_gather(hidden_out.T, ('seq', 'head'), axis=0, tiled=True)]
    pallas_call x6 -> x5, Pallas kernels: 213 us -> 170 us  [the longest x1 70.5 us: front(): pl.pallas_call(functools.partial(front_kernel, n_head, n_seq, gather), ou...]
    ppermute x2 -> x0, starting transfers between devices: 6.9 us -> none  [the longest x1 5.61 us: body(): from_left = lax.ppermute(tokens[rows - SEQ_MOST:], 'head', up_z)]
    ppermute x2 -> x0, waiting for transfers between devices: 5.32 us -> none  [the longest x1 4.14 us: body(): from_right = lax.ppermute(tokens[:SEQ_MOST], 'head', down_z)]
    ppermute x1, starting transfers between devices: 7.32 us -> 11.1 us  [body(): left_part = lax.ppermute(to_right, 'head', up_z)]
    psum x1, blocking collectives: 42 us -> 45.6 us  [body(): totals = lax.psum((gqs[0], gqb[0], gvs[0], gvb[0]), ('seq', 'head'))]
  transfers between devices with their start and end apart: 6 -> 2, of which waited for: 3 -> 0; matrix products, arithmetic and copies ran while one was open for 1% -> 1% of each run, Pallas kernels for 26% -> 9%
where the time goes in v2:
time: 245 us; the launch traced here: 241 us
  Pallas kernels  174 us (71%)
  blocking collectives  45.6 us (19%)
  starting transfers between devices  12.4 us (5%)
  local copies, waits for them, and re-layouts  7.13 us (3%)
    pallas_call x1, Pallas kernels, front(): pl.pallas_call(functools.partial(front_kernel, n_head, n_seq, gather), ou...  70.5 us
    psum x1, blocking collectives, body(): totals = lax.psum((gqs[0], gqb[0], gvs[0], gvb[0]), ('seq', 'head'))  45.6 us
    pallas_call x1, Pallas kernels, feed(): pl.pallas_call(feed_kernel, grid=(rows // tile,), out_shape=[sds((rows, w...  36.7 us
    pallas_call x1, Pallas kernels, attend_back(): call(attend_back_kernel, [sds((width, rows), BF16), wide, wide], 6, [pltp...  33.2 us
    pallas_call x1, Pallas kernels, grads(): call(grads_kernel, [sds((width, rows), F32), sds((1, rank), F32), sds((1,...  22.5 us
    ppermute x1, starting transfers between devices, body(): left_part = lax.ppermute(to_right, 'head', up_z)  11.1 us
    pallas_call x1, Pallas kernels, edges(): return call(edge_kernel, [half, half], 4)(dk, dv, w_key, wve)  7.32 us
  transfers between devices with their start and end apart: 2, of which 0 were waited for; matrix products, arithmetic and copies ran while one was open for 1% of the time, Pallas kernels for 9%

profile of v2, /device:TPU:0, one launch (start us, length us, event | category | flops | bytes accessed | tf_op | source)
XLA Modules:
  0.0 241.4 jit_solution(18062553119792280519)
XLA Ops:
  0.6 1.3 broadcast_in_dim.13.refs_8_.qb_ref
  1.9 1.3 broadcast_in_dim.15.refs_10_.vb_ref
  3.2 1.7 copy.21.refs_11_
  4.9 1.7 copy.22.refs_12_
  6.6 70.5 %shard_map.190 = (bf16[768,1024]{1,0:T(8,128)(2,1)}, f32[12,1,1024]{2,1,0:T(1,128)}, bf16[768,1024]{1,0:T(8,128)(2,1)}, bf16[768,2048]{1,0:T(8,128)(2,1)}, bf16[...) custom-call(s32[1,32]{1,0:T(1,128)} %len_ref.1, ...), custom_call_target="tpu_custom_call" | custom-call | tf_op jit(solution)/shard_map/pallas_call | solution.py:594
  77.1 36.7 %shard_map.191 = (bf16[1024,768]{1,0:T(8,128)(2,1)}, f32[768,1024]{1,0:T(8,128)}, bf16[768,1024]{1,0:T(8,128)(2,1)}, f32[12,1,1024]{2,1,0:T(1,128)}) custom-call(bf16[768,1024]{1,0:T(8,128)(2,1)} %get-tuple-element.31.xt_ref, bf16[768,1024]{1,0:T(8,128)(2,1)} %get-tuple-element.32.ct_ref, bf16[1024,768]{1,0:T(8,128)(2,1)} %cot_ref.1, ...), custom_call_target="tpu_custom_call" | custom-call | tf_op jit(solution)/shard_map/pallas_call | solution.py:613
  113.8 33.2 %shard_map.192 = (bf16[768,1024]{1,0:T(8,128)(2,1)}, bf16[768,2048]{1,0:T(8,128)(2,1)}, bf16[768,2048]{1,0:T(8,128)(2,1)}) custom-call(s32[1]{0:T(128)} %bitcast.2.shift_ref, s32[1,32]{1,0:T(1,128)} %len_ref.1, bf16[768,1024]{1,0:T(8,128)(2,1)} %get-tuple-element.35.qt_ref, bf16[768,2048]{1,0:T(8,128)(2,1)} %get-tuple-element.36.ke_ref, ...), custom_call_target="tpu_custom_call" | custom-call | tf_op jit(solution)/shard_map/pallas_call | solution.py:638
  147.0 7.3 %shard_map.194 = (bf16[768,512]{1,0:T(8,128)(2,1)}, bf16[768,512]{1,0:T(8,128)(2,1)}) custom-call(bf16[768,2048]{1,0:T(8,128)(2,1)} %get-tuple-element.42.dk_ref, bf16[768,2048]{1,0:T(8,128)(2,1)} %get-tuple-element.43.dv_ref, bf16[768,768]{1,0:T(8,128)(2,1)} %wk_ref.3, bf16[768,768]{1,0:T(8,128)(2,1)} %get-tuple-element.48.wve_ref), custom_call_target="tpu_custom_call" | custom-call | tf_op jit(solution)/shard_map/pallas_call | solution.py:654
  154.3 11.1 %collective-permute-start = (bf16[768,512]{1,0:T(8,128)(2,1)}, bf16[768,512]{1,0:T(8,128)(2,1)S(1)}, u32[]{:S(2)}, u32[]{:S(2)}) collective-permute-start(bf16[768,512]{1,0:T(8,128)(2,1)} %get-tuple-element.50), channel_id=1, source_target_pairs={{0,1},{1,2},{2,3},{4,5},{5,6},{6,7},{8,9},{9,10},{10,11},{12,13},{... | collective-permute-start | bytes 2359304 | tf_op jit(solution)/shard_map/ppermute | solution.py:696
  165.4 1.3 collective-permute-start.1
  166.7 22.5 %shard_map.193 = (f32[768,1024]{1,0:T(8,128)}, f32[1,1024]{1,0:T(1,128)}, f32[1,768]{1,0:T(1,128)}, f32[1,1024]{1,0:T(1,128)}, f32[1,768]{1,0:T(1,128)}) custom-call(bf16[768,1024]{1,0:T(8,128)(2,1)} %get-tuple-element.41.dq_ref, bf16[768,2048]{1,0:T(8,128)(2,1)} %get-tuple-element.42.dk_ref, bf16[768,2048]{1,0:T(8,128)(2,1)} %get-tuple-element.43.dv_ref, ...), custom_call_target="tpu_custom_call" | custom-call | tf_op jit(solution)/shard_map/pallas_call | solution.py:660
  189.2 0.7 reduce
  189.9 0.7 reduce.1
  190.6 45.6 %all-reduce = (f32[1024]{0:T(1024)}, f32[768]{0:T(1024)}, f32[1024]{0:T(1024)}, f32[768]{0:T(1024)}) all-reduce(f32[1024]{0:T(1024)} %bitcast.9, f32[768]{0:T(1024)S(1)} %reduce, f32[1024]{0:T(1024)} %bitcast.10, f32[768]{0:T(1024)S(1)} %reduce.1), channel_id=1, replica_groups=mesh['seq'=8,'head'=4] {'seq','head'}, use_global_device_ids=true, to_apply=%region_0.0 | all-reduce | flops 3584 | bytes 28672 | tf_op jit(solution)/shard_map/psum | solution.py:698
  236.2 0.0 collective-permute-done.left_ref
  236.2 0.0 copy-start
  236.2 0.0 collective-permute-done.1.right_ref
  236.2 0.0 copy-start.1
  236.3 0.9 copy-done
  237.1 0.3 copy-done.1
  237.4 4.0 %shard_map.195 = bf16[1024,768]{1,0:T(8,128)(2,1)} custom-call(f32[768,1024]{1,0:T(8,128)} %get-tuple-element.49.own_ref, bf16[768,512]{1,0:T(8,128)(2,1)} %copy-done, bf16[768,512]{1,0:T(8,128)(2,1)} %copy-done.1), custom_call_target="tpu_custom_call" | custom-call | tf_op jit(solution)/shard_map/pallas_call | solution.py:699
Async XLA Ops:
  154.3 81.9 %collective-permute-start = (bf16[768,512]{1,0:T(8,128)(2,1)}, bf16[768,512]{1,0:T(8,128)(2,1)S(1)}, u32[]{:S(2)}, u32[]{:S(2)}) collective-permute-start(bf16[768,512]{1,0:T(8,128)(2,1)} %get-tuple-element.50), channel_id=1, source_target_pairs={{0,1},{1,2},{2,3},{4,5},{5,6},{6,7},{8,9},{9,10},{10,11},{12,13},{... | collective-permute-start | bytes 2359304 | tf_op jit(solution)/shard_map/ppermute | solution.py:696
  165.4 70.8 %collective-permute-start.1 = (bf16[768,512]{1,0:T(8,128)(2,1)}, bf16[768,512]{1,0:T(8,128)(2,1)S(1)}, u32[]{:S(2)}, u32[]{:S(2)}) collective-permute-start(bf16[768,512]{1,0:T(8,128)(2,1)} %get-tuple-element.51), channel_id=1, source_target_pairs={{1,0},{2,1},{3,2},{5,4},{6,5},{7,6},{9,8},{10,9},{11,10},{13,12},{... | collective-permute-start | bytes 2359304 | tf_op jit(solution)/shard_map/ppermute | solution.py:695
  236.2 0.9 copy-start
  236.2 1.2 copy-start.1

commit v3 on v2

--- a/solution.py
+++ b/solution.py
@@ -17,6 +17,7 @@
 TILE_Q = 256
 TILE_K = 256
 LANES = 128
+PACK = 512
 NN = (((1,), (0,)), ((), ()))
 NT = (((1,), (1,)), ((), ()))
 TN = (((0,), (0,)), ((), ()))
@@ -88,56 +89,153 @@
         self.seq, self.head, self.n = seq, head, n_head
         self.shard = own.shape[1]
         self.near_x, self.near_y = other(seq, 2), other(seq, 4)
-        self.far = other(self.near_x, 4)
-
-    def rows(self, seq, k):
-        origin = (self.head + self.n - k) % self.n
+        self.groups = (seq, self.near_x, self.near_y, other(self.near_x, 4))
+
+    def origin(self, way):
+        return self.head - way if way < 4 else self.head + way - 3
+
+    def there(self, way):
+        return self.head >= way if way < 4 else self.head + way - 3 < self.n
+
+    def rows(self, seq, origin):
         return self.full.at[:, span(seq * self.n + origin, self.shard), :]
 
-    def column(self, seq):
-        return self.full.at[:, span(seq, self.n * self.shard), :]
-
-    def pair(self, kind, k):
-        return self.sems.at[2 * (4 * kind + k)], self.sems.at[2 * (4 * kind + k) + 1]
+    def source(self, way):
+        return self.own if way == 0 else self.rows(self.seq, self.origin(way))
+
+    def pair(self, kind, way):
+        return self.sems.at[2 * (7 * kind + way)], self.sems.at[2 * (7 * kind + way) + 1]
 
     def local(self):
-        return pltpu.make_async_copy(self.own, self.rows(self.seq, 0), self.sems.at[0])
-
-    def over_z(self, k):
-        return remote(self.own, self.rows(self.seq, 0), *self.pair(0, k), self.seq, (self.head + k) % self.n)
-
-    def over_x(self, k):
-        src = self.own if k == 0 else self.rows(self.seq, k)
-        return remote(src, self.rows(self.seq, k), *self.pair(1, k), self.near_x, self.head)
-
-    def over_y(self, k):
-        src = self.own if k == 0 else self.rows(self.seq, k)
-        return remote(src, self.rows(self.seq, k), *self.pair(2, k), self.near_y, self.head)
-
-    def onward(self, k):
-        src, to = (self.near_x, self.near_y) if k < 2 else (self.near_y, self.near_x)
-        return remote(self.rows(src, k), self.rows(src, k), *self.pair(3, k), to, self.head)
-
-    def across(self, group):
-        seq = (self.seq, self.near_x, self.near_y, self.far)[group]
-        return remote(
-            self.column(seq), self.column(seq), *self.pair(4, group), other(self.seq, 1), self.head
-        )
+        return pltpu.make_async_copy(self.own, self.rows(self.seq, self.head), self.sems.at[0])
+
+    def up(self, far):
+        dst = self.rows(self.seq, self.head - far)
+        return remote(self.source(far), dst, self.pair(8, far)[0], self.pair(0, far + 1)[1], self.seq, self.head + 1)
+
+    def down(self, far):
+        way = far + 3 if far else 0
+        dst = self.rows(self.seq, self.head + far)
+        return remote(self.source(way), dst, self.pair(8, far)[1], self.pair(0, far + 4)[1], self.seq, self.head - 1)
+
+    def came_z(self, way):
+        dst = self.rows(self.seq, self.origin(way))
+        return remote(dst, dst, *self.pair(0, way), self.seq, self.head)
+
+    def over_x(self, way):
+        dst = self.rows(self.seq, self.origin(way))
+        return remote(self.source(way), dst, *self.pair(1, way), self.near_x, self.head)
+
+    def over_y(self, way):
+        dst = self.rows(self.seq, self.origin(way))
+        return remote(self.source(way), dst, *self.pair(2, way), self.near_y, self.head)
+
+    def onward(self, way, half):
+        src, to = ((self.near_x, self.near_y), (self.near_y, self.near_x))[half]
+        part = self.rows(src, self.origin(way)).at[half]
+        return remote(part, part, *self.pair(3 + half, way), to, self.head)
+
+    def across(self, group, way):
+        dst = self.rows(self.groups[group], self.origin(way))
+        src = self.own if group == 0 and way == 0 else dst
+        sems = self.sems.at[126 + 2 * (7 * group + way)], self.sems.at[127 + 2 * (7 * group + way)]
+        return remote(src, dst, *sems, other(self.seq, 1), self.head)
+
+    def when(self, way, action):
+        if way == 0:
+            action()
+        else:
+            pl.when(self.there(way))(action)
+
+    def spread(self, way):
+        self.over_x(way).start()
+        self.over_y(way).start()
+        self.across(0, way).start()
+
+    def begin(self):
+        pl.when(self.head < self.n - 1)(lambda: self.up(0).start())
+        pl.when(self.head > 0)(lambda: self.down(0).start())
+        self.spread(0)
+        self.local().start()
+
+    def take_z(self, *ways):
+        for way in ways:
+
+            def action():
+                self.came_z(way).wait_recv()
+                if way in (1, 2):
+                    pl.when(self.head < self.n - 1)(lambda: self.up(way).start())
+                if way in (4, 5):
+                    pl.when(self.head > 0)(lambda: self.down(way - 3).start())
+                self.spread(way)
+
+            self.when(way, action)
+
+    def take_xy(self, *ways):
+        for way in ways:
+
+            def action():
+                self.over_x(way).wait_recv()
+                self.onward(way, 0).start()
+                self.across(1, way).start()
+                self.over_y(way).wait_recv()
+                self.onward(way, 1).start()
+                self.across(2, way).start()
+
+            self.when(way, action)
+
+    def take_far(self, *ways):
+        for way in ways:
+
+            def action():
+                self.onward(way, 0).wait_recv()
+                self.onward(way, 1).wait_recv()
+                self.across(3, way).start()
+
+            self.when(way, action)
+
+    def end(self):
+        self.local().wait()
+        for far in range(3):
+            pl.when((self.head < self.n - 1) & (self.head >= far))(lambda: self.up(far).wait_send())
+            pl.when((self.head > 0) & (self.head + far < self.n))(lambda: self.down(far).wait_send())
+        for way in range(7):
+
+            def action():
+                self.over_x(way).wait_send()
+                self.over_y(way).wait_send()
+                self.onward(way, 0).wait_send()
+                self.onward(way, 1).wait_send()
+                for group in range(4):
+                    copy = self.across(group, way)
+                    copy.wait_send()
+                    copy.wait_recv()
+
+            self.when(way, action)
 
 
 def front_kernel(n_head, n_seq, gather, *refs):
-    (
-        len_ref, x_ref, wq_ref, wk_ref, wv_ref, down_ref, up_ref, qs_ref, qb_ref, vs_ref, vb_ref,
-    ) = refs[:11]
-    refs = refs[11:]
+    big, refs = refs[:6], refs[6:]
+    len_ref, vectors, refs = refs[0], refs[1:5], refs[5:]
     if gather:
         (hi_ref, ho_ref), refs = refs[:2], refs[2:]
-    (ct_ref, ls_ref, qt_ref, ke_ref, ve_ref, xt_ref, lt_ref, rt_ref, wqe_ref, wve_ref), refs = refs[:10], refs[10:]
+    (ct_ref, ls_ref), refs = refs[:2], refs[2:]
+    stored, refs = refs[:8], refs[8:]
     if gather:
         full_ref, refs = refs[0], refs[1:]
+    held, refs = refs[:6], refs[6:]
+    kept, refs = refs[:8], refs[8:]
     (
-        xl_ref, xr_ref, acc_ref, high_ref, total_ref, low_row, high_row, bias_ref, halo_sem,
-    ), refs = refs[:9], refs[9:]
+        xl_ref, xr_ref, acc_ref, high_ref, total_ref, low_row, high_row, bias_ref,
+        load_sem, store_sem, halo_sem,
+    ), refs = refs[:11], refs[11:]
+    x_hbm = big[0]
+    loads = [pltpu.make_async_copy(src, dst, load_sem.at[n]) for n, (src, dst) in enumerate(zip(big, held))]
+    stores = [pltpu.make_async_copy(src, dst, store_sem.at[n]) for n, (src, dst) in enumerate(zip(kept, stored))]
+    for n in (1, 2, 3, 4, 0, 5):
+        loads[n].start()
+    x_ref, down_ref, up_ref, wq_ref, wv_ref, wk_ref = held
+    qt_ref, ke_ref, ve_ref, xt_ref, lt_ref, rt_ref, wqe_ref, wve_ref = kept
     rows, width = x_ref.shape
     heads = width // HEAD_DIM
     seq, head_at = lax.axis_index("seq"), lax.axis_index("head")
@@ -149,44 +247,45 @@
     if gather:
         partners += [(other(seq, bit), head_at) for bit in (1, 2, 4)]
         own_ref, gather_sem = refs
-        own_ref[0] = hi_ref[...].T
-        own_ref[1] = ho_ref[...].T
+        own_ref[0] = hi_ref[...]
+        own_ref[1] = ho_ref[...]
     for partner in partners:
         pl.semaphore_signal(barrier, inc=1, device_id=partner, device_id_type=MESH)
     pl.semaphore_wait(barrier, len(partners))
 
     to_right = remote(
-        x_ref.at[rows - SEQ_MOST :], xl_ref, halo_sem.at[0], halo_sem.at[1], seq, (head_at + 1) % n_head
+        x_hbm.at[rows - SEQ_MOST :], xl_ref, halo_sem.at[0], halo_sem.at[1], seq, (head_at + 1) % n_head
     )
     to_left = remote(
-        x_ref.at[:SEQ_MOST], xr_ref, halo_sem.at[2], halo_sem.at[3], seq, (head_at + n_head - 1) % n_head
+        x_hbm.at[:SEQ_MOST], xr_ref, halo_sem.at[2], halo_sem.at[3], seq, (head_at + n_head - 1) % n_head
     )
+
+    def send_halo():
+        pl.when(head_at < n_head - 1)(lambda: to_right.start())
+        pl.when(head_at > 0)(lambda: to_left.start())
+
     if gather:
         g = Gather(own_ref, full_ref, gather_sem, seq, head_at, n_head)
-        for k in (1, 3, 2):
-            g.over_z(k).start()
-        g.over_x(0).start()
-        g.over_y(0).start()
-        g.local().start()
-
-    @pl.when(head_at < n_head - 1)
-    def _():
-        to_right.start()
-
-    @pl.when(head_at > 0)
-    def _():
-        to_left.start()
+        g.begin()
+    else:
+        send_halo()
+    query_scale, query_bias, value_scale, value_bias = [ref[...].reshape(1, -1) for ref in vectors]
+    for n in (1, 2, 3, 4):
+        loads[n].wait()
 
     def fold(index, carry):
         part = span(index, 256)
         down = down_ref[part, :].astype(F32)
-        side_q = dot((down * qs_ref[...]).astype(BF16), up_ref[...], NN) * qb_ref[...]
+        side_q = dot((down * query_scale).astype(BF16), up_ref[...], NN) * query_bias
         wqe_ref[part, :] = ((wq_ref[part, :].astype(F32) + side_q) * QUERY_FOLD).astype(BF16)
-        side_v = dot((down * vs_ref[...]).astype(BF16), up_ref[...], NN) * vb_ref[...]
+        side_v = dot((down * value_scale).astype(BF16), up_ref[...], NN) * value_bias
         wve_ref[part, :] = (wv_ref[part, :].astype(F32) + side_v).astype(BF16)
         return carry
 
     lax.fori_loop(0, width // 256, fold, 0)
+    stores[6].start()
+    stores[7].start()
+    loads[0].wait()
 
     def flip(index, carry):
         part = span(index, 256)
@@ -194,16 +293,24 @@
         return carry
 
     lax.fori_loop(0, rows // 256, flip, 0)
+    stores[3].start()
     own = slice(SEQ_MOST, SEQ_MOST + rows)
 
-    def apply(index, carry):
-        part = span(index, 256)
-        qt_ref[part, :] = dot(wqe_ref[:, part], xt_ref[...], TN).astype(BF16)
-        ke_ref[part, own] = dot(wk_ref[:, part], xt_ref[...], TN).astype(BF16)
-        ve_ref[part, own] = dot(wve_ref[:, part], xt_ref[...], TN).astype(BF16)
-        return carry
-
-    lax.fori_loop(0, width // 256, apply, 0)
+    def apply(weight_ref, out_ref, at):
+        def piece(index, carry):
+            part = span(index, 256)
+            out_ref[part, at] = dot(weight_ref[:, part], xt_ref[...], TN).astype(BF16)
+            return carry
+
+        lax.fori_loop(0, width // 256, piece, 0)
+
+    apply(wqe_ref, qt_ref, slice(0, rows))
+    if gather:
+        g.take_z(1, 4)
+    loads[5].wait()
+    stores[0].start()
+    apply(wk_ref, ke_ref, own)
+    apply(wve_ref, ve_ref, own)
 
     low, high = bounds(len_ref, shift + SEQ_MOST, rows)
     low_row[...] = low
@@ -236,6 +343,22 @@
             acc_ref[part, q_part] = a
 
     def own_block(index, carry):
+        if gather:
+            for at, step in (
+                (1, lambda: g.take_xy(0)),
+                (2, lambda: (g.take_z(2, 5), send_halo())),
+                (3, lambda: g.take_xy(1, 4)),
+                (5, lambda: g.take_z(3, 6)),
+                (6, lambda: g.take_far(0)),
+                (8, lambda: g.take_xy(2, 5)),
+                (10, lambda: g.take_far(1, 4)),
+                (13, lambda: g.take_xy(3, 6)),
+            ):
+
+                @pl.when(index == at)
+                def _():
+                    step()
+
         tile, at = (index + 1) // 4, (index + 1) % 4
         block(tile, at + 1 + (tile + 1) // 2)
         return carry
@@ -245,32 +368,12 @@
         return carry
 
     def right_block(index, carry):
+        if gather:
+            pl.when(index == 0)(lambda: g.take_far(3, 6))
         block(2 + (index + 1) // 2, 6 + index // 2)
         return carry
 
-    if gather:
-        g.over_x(0).wait_recv()
-        g.onward(0).start()
-    lax.fori_loop(0, 3, own_block, 0)
-    if gather:
-        g.over_z(1).wait_recv()
-        g.over_x(1).start()
-        g.over_y(1).start()
-    lax.fori_loop(3, 7, own_block, 0)
-    if gather:
-        g.over_z(3).wait_recv()
-        g.over_x(3).start()
-        g.over_y(3).start()
-        g.over_x(1).wait_recv()
-        g.onward(1).start()
-    lax.fori_loop(7, 11, own_block, 0)
-    if gather:
-        g.over_z(2).wait_recv()
-        g.over_x(2).start()
-        g.over_y(2).start()
-        g.local().wait()
-        g.across(0).start()
-    lax.fori_loop(11, 14, own_block, 0)
+    lax.fori_loop(0, 14, own_block, 0)
 
     for absent, copy, side_ref, flat_ref, base in (
         (first_z, to_right, xl_ref, lt_ref, 0),
@@ -300,19 +403,11 @@
 
         lax.fori_loop(0, width // 256, edge, 0)
 
+    for n in (1, 2, 4, 5):
+        stores[n].start()
     if gather:
-        g.over_y(3).wait_recv()
-        g.onward(3).start()
+        g.take_far(2, 5)
     lax.fori_loop(0, 3, left_block, 0)
-    if gather:
-        g.over_y(2).wait_recv()
-        g.onward(2).start()
-        for k in (2, 3):
-            g.over_x(k).wait_recv()
-        g.across(1).start()
-        for k in (0, 1):
-            g.over_y(k).wait_recv()
-        g.across(2).start()
     lax.fori_loop(0, 3, right_block, 0)
 
     for head in range(heads):
@@ -321,28 +416,12 @@
         ct_ref[part, :] = (acc_ref[part, :] / total).astype(BF16)
         ls_ref[head] = high_ref[head] + jnp.log2(total)
 
-    @pl.when(head_at < n_head - 1)
-    def _():
-        to_right.wait_send()
-
-    @pl.when(head_at > 0)
-    def _():
-        to_left.wait_send()
-
+    pl.when(head_at < n_head - 1)(lambda: to_right.wait_send())
+    pl.when(head_at > 0)(lambda: to_left.wait_send())
+    for store in stores:
+        store.wait()
     if gather:
-        for k in range(4):
-            g.onward(k).wait_recv()
-        g.across(3).start()
-        for k in (1, 2, 3):
-            g.over_z(k).wait_send()
-        for k in range(4):
-            g.over_x(k).wait_send()
-            g.over_y(k).wait_send()
-            g.onward(k).wait_send()
-        for k, seq_at in enumerate((seq, g.near_x, g.near_y, g.far)):
-            g.across(k).wait_send()
-            came = g.column(other(seq_at, 1))
-            remote(came, came, *g.pair(4, k), other(seq, 1), head_at).wait_recv()
+        g.end()
 
 
 def attend_back_kernel(
@@ -470,32 +549,122 @@
         )
 
 
-def edge_kernel(dk_ref, dv_ref, wk_ref, wve_ref, left_ref, right_ref):
-    extent = dk_ref.shape[1]
-    width = wk_ref.shape[0]
-
-    def part_of(index, carry):
-        part = span(index, 256)
-        for out_ref, base in ((left_ref, 0), (right_ref, extent - SEQ_MOST)):
-            side = slice(base, base + SEQ_MOST)
-            out_ref[part, :] = (
-                dot(wk_ref[part, :], dk_ref[:, side], NN)
-                + dot(wve_ref[part, :], dv_ref[:, side], NN)
-            ).astype(BF16)
-        return carry
-
-    lax.fori_loop(0, width // 256, part_of, 0)
-
-
-def grads_kernel(
-    dq_ref, dk_ref, dv_ref, xt_ref, xl_ref, xr_ref, gf_ref, wqe_ref, wk_ref, wve_ref,
-    down_ref, up_ref, qs_ref, qb_ref, vs_ref, vb_ref,
-    own_ref, gqs_ref, gqb_ref, gvs_ref, gvb_ref,
-    sum_ref,
-):
+def pack(rows):
+    places, at = [], 0
+    for size in rows:
+        places.append([(at + n, n * PACK, min(PACK, size - n * PACK)) for n in range(-(-size // PACK))])
+        at += len(places[-1])
+    return places, at
+
+
+def tail_kernel(n_head, n_seq, *refs):
+    big, refs = refs[:12], refs[12:]
+    vectors, refs = refs[:4], refs[4:]
+    query_scale, query_bias, value_scale, value_bias = [ref[...].reshape(1, -1) for ref in vectors]
+    (out_ref, gqs_ref, gqb_ref, gvs_ref, gvb_ref), refs = refs[:5], refs[5:]
+    held, refs = refs[:12], refs[12:]
+    (
+        load_sem, own_ref, mix_ref, send_left, send_right, from_left, from_right, halo_sem,
+        z_slots, s_slots, z_sem, s_sem,
+    ) = refs
+    loads = [pltpu.make_async_copy(src, dst, load_sem.at[n]) for n, (src, dst) in enumerate(zip(big, held))]
+    for load in loads:
+        load.start()
+    dk_ref, dv_ref, wk_ref, wve_ref, xt_ref, dq_ref, lt_ref, rt_ref, down_ref, up_ref, wqe_ref, gf_ref = held
     width, rows = dq_ref.shape
     rank = up_ref.shape[0]
     own = slice(SEQ_MOST, SEQ_MOST + rows)
+    seq, head_at = lax.axis_index("seq"), lax.axis_index("head")
+
+    barrier = pltpu.get_barrier_semaphore()
+    partners = [(seq, (head_at + k) % n_head) for k in range(1, n_head)]
+    partners += [((seq + k) % n_seq, head_at) for k in range(1, n_seq)]
+    for partner in partners:
+        pl.semaphore_signal(barrier, inc=1, device_id=partner, device_id_type=MESH)
+    pl.semaphore_wait(barrier, len(partners))
+
+    for load in loads[:4]:
+        load.wait()
+
+    def edge(index, carry):
+        part = span(index, 256)
+        for side_ref, base in ((send_left, 0), (send_right, SEQ_MOST + rows)):
+            side = slice(base, base + SEQ_MOST)
+            side_ref[part, :] = (
+                dot(wk_ref[part, :], dk_ref[:, side], NN) + dot(wve_ref[part, :], dv_ref[:, side], NN)
+            ).astype(BF16)
+        return carry
+
+    lax.fori_loop(0, width // 256, edge, 0)
+    to_left = remote(
+        send_left, from_right, halo_sem.at[0], halo_sem.at[1], seq, (head_at + n_head - 1) % n_head
+    )
+    to_right = remote(send_right, from_left, halo_sem.at[2], halo_sem.at[3], seq, (head_at + 1) % n_head)
+    first_z, last_z = head_at == 0, head_at == n_head - 1
+
+    @pl.when(jnp.logical_not(first_z))
+    def _():
+        to_left.start()
+
+    @pl.when(jnp.logical_not(last_z))
+    def _():
+        to_right.start()
+
+    places, depth = pack((rank, width, rank, width))
+    z_slots[head_at] = jnp.zeros_like(z_slots[0])
+    for load in loads[4:10]:
+        load.wait()
+
+    for value in (False, True):
+        scale_row, bias = (value_scale, value_bias) if value else (query_scale, query_bias)
+        factor = 1.0 if value else QUERY_FOLD
+        scale_at, bias_at = places[2 * value], places[2 * value + 1]
+
+        def outer(index, carry):
+            part = span(index, 256)
+            if value:
+                total = dot(xt_ref[part, :], dv_ref[:, own], NT)
+                total += dot(lt_ref[part, :], dv_ref[:, :SEQ_MOST], NT)
+                total += dot(rt_ref[part, :], dv_ref[:, SEQ_MOST + rows :], NT)
+            else:
+                total = dot(xt_ref[part, :], dq_ref[...], NT)
+            mix_ref[part, :] = total.astype(BF16)
+            return carry
+
+        lax.fori_loop(0, width // 256, outer, 0)
+        bias_sum = jnp.zeros((1, width), F32)
+        for at in range(0, rank, 256):
+            part = slice(at, at + 256)
+            mixed = dot(down_ref[:, part], mix_ref[...], TN) * up_ref[part, :].astype(F32) * factor
+            scale = jnp.broadcast_to(scale_row[:, part], (LANES, 256)).T[:, :1]
+            bias_sum += jnp.sum(mixed * scale, axis=0, keepdims=True)
+            weighted = mixed * bias
+            folded = weighted[:, :LANES]
+            for lane in range(LANES, width, LANES):
+                folded = folded + weighted[:, lane : lane + LANES]
+            row, column = at // PACK, at % PACK
+            z_slots[head_at, pl.ds(scale_at[row][0], 1), pl.ds(column, 256)] = jnp.sum(
+                folded.T, axis=0, keepdims=True
+            )
+        for row, start, size in bias_at:
+            z_slots[head_at, pl.ds(row, 1), pl.ds(0, size)] = bias_sum[:, start : start + size]
+
+    def over_z(k):
+        return remote(
+            z_slots.at[head_at], z_slots.at[head_at], z_sem.at[2 * k], z_sem.at[2 * k + 1],
+            seq, (head_at + k) % n_head,
+        )
+
+    def over_seq(k):
+        return remote(
+            s_slots.at[seq], s_slots.at[seq], s_sem.at[2 * k], s_sem.at[2 * k + 1],
+            (seq + k) % n_seq, head_at,
+        )
+
+    for k in range(1, n_head):
+        over_z(k).start()
+    for load in loads[10:]:
+        load.wait()
 
     def tokens_part(index, carry):
         part = span(index, 256)
@@ -508,51 +677,57 @@
         return carry
 
     lax.fori_loop(0, width // 256, tokens_part, 0)
-
-    for value in (False, True):
-        scale_ref, bias_ref = (vs_ref, vb_ref) if value else (qs_ref, qb_ref)
-        out_scale, out_bias = (gvs_ref, gvb_ref) if value else (gqs_ref, gqb_ref)
-        factor = 1.0 if value else QUERY_FOLD
-
-        def outer(index, carry):
+    for k in range(1, n_head):
+        over_z(k).wait_recv()
+    total = z_slots[0]
+    for k in range(1, n_head):
+        total = total + z_slots[k]
+    s_slots[seq] = total
+    for k in range(1, n_seq):
+        over_seq(k).start()
+
+    for absent, copy, side_ref, base in (
+        (first_z, to_right, from_left, 0),
+        (last_z, to_left, from_right, rows - SEQ_MOST),
+    ):
+
+        @pl.when(absent)
+        def _():
+            side_ref[...] = jnp.zeros_like(side_ref)
+
+        @pl.when(jnp.logical_not(absent))
+        def _():
+            copy.wait_recv()
+
+        def finish(index, carry):
             part = span(index, 256)
-            if value:
-                total = dot(xt_ref[part, :], dv_ref[:, own], NT)
-                total += dot(xl_ref[part, :], dv_ref[:, :SEQ_MOST], NT)
-                total += dot(xr_ref[part, :], dv_ref[:, SEQ_MOST + rows :], NT)
-            else:
-                total = dot(xt_ref[part, :], dq_ref[...], NT)
-            sum_ref[part, :] = total.astype(BF16)
+            at = pl.ds(pl.multiple_of(base + index * 256, 256), 256)
+            out_ref[at, :] = (own_ref[:, at] + side_ref[:, part].astype(F32)).T.astype(BF16)
             return carry
 
-        lax.fori_loop(0, width // 256, outer, 0)
-        out_bias[...] = jnp.zeros_like(out_bias)
-
-        def inner(index, carry):
-            part = span(index, 256)
-            mixed = dot(down_ref[:, part], sum_ref[...], TN) * up_ref[part, :].astype(F32) * factor
-            out_bias[...] += dot_rows(scale_ref[:, part], mixed)
-            weighted = mixed * bias_ref[...]
-            folded = weighted[:, :LANES]
-            for at in range(LANES, width, LANES):
-                folded = folded + weighted[:, at : at + LANES]
-            out_scale[:, part] = jnp.sum(folded.T, axis=0, keepdims=True)
-            return carry
-
-        lax.fori_loop(0, rank // 256, inner, 0)
-
-
-def dot_rows(scale, mixed):
-    return jnp.sum(mixed * jnp.broadcast_to(scale, (LANES, scale.shape[1])).T[:, :1], axis=0, keepdims=True)
-
-
-def finish_kernel(own_ref, left_ref, right_ref, out_ref):
-    rows = own_ref.shape[1]
-    total = own_ref[...]
-    out_ref[:SEQ_MOST, :] = (total[:, :SEQ_MOST] + left_ref[...].astype(F32)).T.astype(BF16)
-    out_ref[rows - SEQ_MOST :, :] = (
-        total[:, rows - SEQ_MOST :] + right_ref[...].astype(F32)
-    ).T.astype(BF16)
+        lax.fori_loop(0, SEQ_MOST // 256, finish, 0)
+
+    for k in range(1, n_seq):
+        over_seq(k).wait_recv()
+    total = s_slots[0]
+    for k in range(1, n_seq):
+        total = total + s_slots[k]
+    for vector_ref, place in zip((gqs_ref, gqb_ref, gvs_ref, gvb_ref), places):
+        for row, start, size in place:
+            vector_ref[start : start + size] = total[row, :size]
+
+    @pl.when(jnp.logical_not(first_z))
+    def _():
+        to_left.wait_send()
+
+    @pl.when(jnp.logical_not(last_z))
+    def _():
+        to_right.wait_send()
+
+    for k in range(1, n_head):
+        over_z(k).wait_send()
+    for k in range(1, n_seq):
+        over_seq(k).wait_send()
 
 
 def call(kernel, outs, count, scratch=(), scalars=0):
@@ -572,8 +747,10 @@
     extent = rows + 2 * SEQ_MOST
     tall, wide = sds((width, rows), BF16), sds((width, extent), BF16)
     square, half = sds((width, width), BF16), sds((width, SEQ_MOST), BF16)
-    outs = [tall, sds((heads, 1, rows), F32), tall, wide, wide, tall, half, half, square, square]
-    scratch = [
+    kept = [tall, wide, wide, tall, half, half, square, square]
+    outs = [tall, sds((heads, 1, rows), F32)] + kept
+    big = (tokens, vera[0], vera[1], w_query, w_value, w_key)
+    scratch = [pltpu.VMEM(a.shape, a.dtype) for a in (*big, *kept)] + [
         pltpu.VMEM((SEQ_MOST, width), BF16),
         pltpu.VMEM((SEQ_MOST, width), BF16),
         pltpu.VMEM((width, rows), F32),
@@ -582,25 +759,27 @@
         pltpu.VMEM((1, rows), jnp.int32),
         pltpu.VMEM((1, rows), jnp.int32),
         pltpu.VMEM((TILE_K, TILE_Q), F32),
+        pltpu.SemaphoreType.DMA((len(big),)),
+        pltpu.SemaphoreType.DMA((len(kept),)),
         pltpu.SemaphoreType.DMA((4,)),
     ]
     gather = len(shards) > 0
-    specs = [VMEM] * len(outs)
+    specs = [VMEM] * 2 + [ANY] * len(kept)
     if gather:
-        shard = shards[0].shape[1]
+        shard = shards[0].shape[0]
         outs.append(sds((2, n_head * n_seq * shard, width), BF16))
         specs.append(ANY)
-        scratch += [pltpu.VMEM((2, shard, width), BF16), pltpu.SemaphoreType.DMA((40,))]
+        scratch += [pltpu.VMEM((2, shard, width), BF16), pltpu.SemaphoreType.DMA((182,))]
     return pl.pallas_call(
         functools.partial(front_kernel, n_head, n_seq, gather),
         out_shape=outs,
-        in_specs=[SMEM] + [VMEM] * (10 + len(shards)),
+        in_specs=[ANY] * len(big) + [SMEM] + [VMEM] * (4 + len(shards)),
         out_specs=specs,
         scratch_shapes=scratch,
         compiler_params=pltpu.CompilerParams(
             vmem_limit_bytes=58 << 20, collective_id=0, has_side_effects=True
         ),
-    )(lengths, tokens, w_query, w_key, w_value, *vera, *shards)
+    )(*big, lengths, *vera[2:], *shards)
 
 
 def feed(xt, ct, cotangent, w_output, weights):
@@ -649,23 +828,34 @@
     )(shift, lengths, qt, ke, ve, ls, gc, dl)
 
 
-def edges(dk, dv, w_key, wve):
-    half = sds((dk.shape[0], SEQ_MOST), BF16)
-    return call(edge_kernel, [half, half], 4)(dk, dv, w_key, wve)
-
-
-def grads(dq, *rest):
+def tail(n_head, n_seq, big, small):
+    dq, up = big[5], big[9]
     width, rows = dq.shape
-    rank = rest[-5].shape[0]
-    return call(
-        grads_kernel,
-        [
-            sds((width, rows), F32), sds((1, rank), F32), sds((1, width), F32),
-            sds((1, rank), F32), sds((1, width), F32),
+    rank = up.shape[0]
+    depth = -(-pack((rank, width, rank, width))[1] // 8) * 8
+    half = pltpu.VMEM((width, SEQ_MOST), BF16)
+    outs = [sds((rows, width), BF16)] + [sds((size,), F32) for size in (rank, width, rank, width)]
+    return pl.pallas_call(
+        functools.partial(tail_kernel, n_head, n_seq),
+        out_shape=outs,
+        in_specs=[ANY] * len(big) + [VMEM] * len(small),
+        out_specs=[VMEM] * len(outs),
+        scratch_shapes=[pltpu.VMEM(a.shape, a.dtype) for a in big]
+        + [
+            pltpu.SemaphoreType.DMA((len(big),)),
+            pltpu.VMEM((width, rows), F32),
+            pltpu.VMEM((width, width), BF16),
+            half, half, half, half,
+            pltpu.SemaphoreType.DMA((4,)),
+            pltpu.VMEM((n_head, depth, PACK), F32),
+            pltpu.VMEM((n_seq, depth, PACK), F32),
+            pltpu.SemaphoreType.DMA((2 * n_head,)),
+            pltpu.SemaphoreType.DMA((2 * n_seq,)),
         ],
-        16,
-        [pltpu.VMEM((width, width), BF16)],
-    )(dq, *rest)
+        compiler_params=pltpu.CompilerParams(
+            vmem_limit_bytes=58 << 20, collective_id=1, has_side_effects=True
+        ),
+    )(*big, *small)
 
 
 def body(n_seq, n_head, *arrays):
@@ -674,12 +864,10 @@
         query_scale, query_bias, value_scale, value_bias, hidden_in, hidden_out,
     ) = arrays
     rows, width = tokens.shape
-    up_z = [(i, i + 1) for i in range(n_head - 1)]
-    down_z = [(i + 1, i) for i in range(n_head - 1)]
     shift = (lax.axis_index("head") * rows - SEQ_MOST).astype(jnp.int32).reshape(1)
-    vera = (vera_down, vera_up, query_scale[None], query_bias[None], value_scale[None], value_bias[None])
+    vera = (vera_down, vera_up, query_scale, query_bias, value_scale, value_bias)
     fused = (n_seq, n_head) == (8, 4)
-    shards = (hidden_in, hidden_out) if fused else ()
+    shards = (hidden_in.T, hidden_out.T) if fused else ()
     ct, ls, qt, ke, ve, xt, lt, rt, wqe, wve, *full = front(
         n_head, n_seq, lengths, tokens, w_query, w_key, w_value, vera, shards
     )
@@ -691,12 +879,9 @@
         )
     layer_out, gf, gc, dl = feed(xt, ct, cotangent, w_output, weights)
     dq, dk, dv = attend_back(shift, lengths, qt, ke, ve, ls, gc, dl)
-    to_left, to_right = edges(dk, dv, w_key, wve)
-    right_part = lax.ppermute(to_left, "head", down_z)
-    left_part = lax.ppermute(to_right, "head", up_z)
-    own, gqs, gqb, gvs, gvb = grads(dq, dk, dv, xt, lt, rt, gf, wqe, w_key, wve, *vera)
-    totals = lax.psum((gqs[0], gqb[0], gvs[0], gvb[0]), ("seq", "head"))
-    (token_grad,) = call(finish_kernel, [sds((rows, width), BF16)], 3)(own, left_part, right_part)
+    token_grad, *totals = tail(
+        n_head, n_seq, (dk, dv, w_key, wve, xt, dq, lt, rt, vera_down, vera_up, wqe, gf), vera[2:]
+    )
     return (layer_out, token_grad, *totals)
 
 

time: 245 us -> 181 us (0.74); the launches traced: 241 us -> 181 us
  blocking collectives: 45.6 us -> 0 us
  starting transfers between devices: 12.4 us -> 0 us
    psum x1 -> x0, blocking collectives: 45.6 us -> none  [body(): totals = lax.psum((gqs[0], gqb[0], gvs[0], gvb[0]), ('seq', 'head'))]
    ppermute x2 -> x0, starting transfers between devices: 12.4 us -> none  [the longest x1 11.1 us: body(): left_part = lax.ppermute(to_right, 'head', up_z)]
    pallas_call x3 -> x1, Pallas kernels: 33.8 us -> 45.2 us  [tail(): pl.pallas_call(functools.partial(tail_kernel, n_head, n_seq), out_shape=o...]
    pallas_call x1, Pallas kernels: 70.5 us -> 60.4 us  [front(): pl.pallas_call(functools.partial(front_kernel, n_head, n_seq, gather), ou...]
    broadcast_in_dim x2 -> x0, local copies, waits for them, and re-layouts: 2.53 us -> none  [the longest x1 1.27 us: body(): query_bias[None]]
    unnamed x6 -> x13, local copies, waits for them, and re-layouts: 4.59 us -> 5.04 us
  transfers between devices with their start and end apart: 2 -> 0, of which waited for: 0 -> 0; matrix products, arithmetic and copies ran while one was open for 1% -> 0% of each run, Pallas kernels for 9% -> 0%
where the time goes in v3:
time: 181 us
  Pallas kernels  175 us (97%)
  local copies, waits for them, and re-layouts  5.04 us (3%)
    pallas_call x1, Pallas kernels, front(): pl.pallas_call(functools.partial(front_kernel, n_head, n_seq, gather), ou...  60.4 us
    pallas_call x1, Pallas kernels, tail(): pl.pallas_call(functools.partial(tail_kernel, n_head, n_seq), out_shape=o...  45.2 us
    pallas_call x1, Pallas kernels, feed(): pl.pallas_call(feed_kernel, grid=(rows // tile,), out_shape=[sds((rows, w...  36.7 us
    pallas_call x1, Pallas kernels, attend_back(): call(attend_back_kernel, [sds((width, rows), BF16), wide, wide], 6, [pltp...  33.1 us
    unnamed x13, local copies, waits for them, and re-layouts  5.04 us

profile of v3, /device:TPU:0, one launch (start us, length us, event | category | flops | bytes accessed | tf_op | source)
XLA Modules:
  0.0 181.1 jit_solution(2535369320143347884)
XLA Ops:
  0.6 60.4 %shard_map.190 = (bf16[768,1024]{1,0:T(8,128)(2,1)}, f32[12,1,1024]{2,1,0:T(1,128)}, bf16[768,1024]{1,0:T(8,128)(2,1)}, bf16[768,2048]{1,0:T(8,128)(2,1)}, bf16[...) custom-call(bf16[1024,768]{1,0:T(8,128)(2,1)} %refs_0_.1, ...), custom_call_target="tpu_custom_call" | custom-call | tf_op jit(solution)/shard_map/pallas_call | solution.py:773
  61.0 36.7 %shard_map.191 = (bf16[1024,768]{1,0:T(8,128)(2,1)}, f32[768,1024]{1,0:T(8,128)}, bf16[768,1024]{1,0:T(8,128)(2,1)}, f32[12,1,1024]{2,1,0:T(1,128)}) custom-call(bf16[768,1024]{1,0:T(8,128)(2,1)} %get-tuple-element.29.xt_ref.refs_4_, bf16[768,1024]{1,0:T(8,128)(2,1)} %get-tuple-element.30.ct_ref, bf16[1024,768]{1,0:T(8,128)(2,1)} %cot_ref.1, ...), custom_call_target="tpu_custom_call" | custom-call | tf_op jit(solution)/shard_map/pallas_call | solution.py:792
  97.7 33.1 %shard_map.192 = (bf16[768,1024]{1,0:T(8,128)(2,1)}, bf16[768,2048]{1,0:T(8,128)(2,1)}, bf16[768,2048]{1,0:T(8,128)(2,1)}) custom-call(s32[1]{0:T(128)} %bitcast.2.shift_ref, s32[1,32]{1,0:T(1,128)} %len_ref.1, bf16[768,1024]{1,0:T(8,128)(2,1)} %get-tuple-element.33.qt_ref, bf16[768,2048]{1,0:T(8,128)(2,1)} %get-tuple-element.34.ke_ref, ...), custom_call_target="tpu_custom_call" | custom-call | tf_op jit(solution)/shard_map/pallas_call | solution.py:817
  130.8 45.2 %shard_map.193 = (bf16[1024,768]{1,0:T(8,128)(2,1)}, f32[1024]{0:T(1024)}, f32[768]{0:T(1024)}, f32[1024]{0:T(1024)}, f32[768]{0:T(1024)}) custom-call(bf16[768,2048]{1,0:T(8,128)(2,1)} %get-tuple-element.39.refs_0_, bf16[768,2048]{1,0:T(8,128)(2,1)} %get-tuple-element.40.refs_1_, bf16[768,768]{1,0:T(8,128)(2,1)} %refs_2_.3, ...), custom_call_target="tpu_custom_call" | custom-call | tf_op jit(solution)/shard_map/pallas_call | solution.py:838
  176.1 0.0 copy-start.3
  176.1 0.0 copy-start.2
  176.1 0.0 copy-start.1
  176.1 0.0 copy-start
  176.1 2.7 %copy.26 = bf16[1024,768]{1,0:T(8,128)(2,1)} copy(bf16[1024,768]{1,0:T(8,128)(2,1)} %get-tuple-element.59) | data formatting | bytes 3145728
  178.7 0.0 copy-done.3
  178.8 0.6 copy.27
  179.3 0.0 copy-done.2
  179.3 0.6 copy.28
  179.9 0.0 copy-done.1
  179.9 0.6 copy.29
  180.5 0.0 copy-done
  180.5 0.6 copy.30
Async XLA Ops:
  176.1 2.7 %copy-start.3 = (f32[1024]{0:T(1024)S(1)}, f32[1024]{0:T(1024)}, u32[]{:S(2)}) copy-start(f32[1024]{0:T(1024)} %get-tuple-element.60) | copy-start | bytes 12292
  176.1 3.3 %copy-start.2 = (f32[768]{0:T(1024)S(1)}, f32[768]{0:T(1024)}, u32[]{:S(2)}) copy-start(f32[768]{0:T(1024)} %get-tuple-element.61) | copy-start | bytes 9220
  176.1 3.9 %copy-start.1 = (f32[1024]{0:T(1024)S(1)}, f32[1024]{0:T(1024)}, u32[]{:S(2)}) copy-start(f32[1024]{0:T(1024)} %get-tuple-element.62) | copy-start | bytes 12292
  176.1 4.5 %copy-start = (f32[768]{0:T(1024)S(1)}, f32[768]{0:T(1024)}, u32[]{:S(2)}) copy-start(f32[768]{0:T(1024)} %get-tuple-element.63) | copy-start | bytes 9220

commit v4 on v3

--- a/solution.py
+++ b/solution.py
@@ -141,58 +141,68 @@
         sems = self.sems.at[126 + 2 * (7 * group + way)], self.sems.at[127 + 2 * (7 * group + way)]
         return remote(src, dst, *sems, other(self.seq, 1), self.head)
 
-    def when(self, way, action):
-        if way == 0:
-            action()
-        else:
-            pl.when(self.there(way))(action)
-
-    def spread(self, way):
-        self.over_x(way).start()
-        self.over_y(way).start()
-        self.across(0, way).start()
+    def slots(self, index):
+        z = self.head
+        return (
+            ((0, None),),
+            ((1, z > 0), (4, z == 0)),
+            ((4, (z == 1) | (z == 2)), (5, z == 0), (2, z == 3)),
+            ((6, z == 0), (5, z == 1), (2, z == 2), (3, z == 3)),
+        )[index]
+
+    def each(self, index, action):
+        for way, chosen in self.slots(index):
+            if chosen is None:
+                action(way)
+            else:
+                pl.when(chosen)(functools.partial(action, way))
 
     def begin(self):
         pl.when(self.head < self.n - 1)(lambda: self.up(0).start())
         pl.when(self.head > 0)(lambda: self.down(0).start())
+        self.local().start()
         self.spread(0)
-        self.local().start()
-
-    def take_z(self, *ways):
-        for way in ways:
-
-            def action():
-                self.came_z(way).wait_recv()
-                if way in (1, 2):
-                    pl.when(self.head < self.n - 1)(lambda: self.up(way).start())
-                if way in (4, 5):
-                    pl.when(self.head > 0)(lambda: self.down(way - 3).start())
-                self.spread(way)
-
-            self.when(way, action)
-
-    def take_xy(self, *ways):
-        for way in ways:
-
-            def action():
-                self.over_x(way).wait_recv()
-                self.onward(way, 0).start()
-                self.across(1, way).start()
-                self.over_y(way).wait_recv()
-                self.onward(way, 1).start()
-                self.across(2, way).start()
-
-            self.when(way, action)
-
-    def take_far(self, *ways):
-        for way in ways:
-
-            def action():
-                self.onward(way, 0).wait_recv()
-                self.onward(way, 1).wait_recv()
-                self.across(3, way).start()
-
-            self.when(way, action)
+
+    def take_z(self, far):
+        def below():
+            self.came_z(far).wait_recv()
+            if far < self.n - 1:
+                pl.when(self.head < self.n - 1)(lambda: self.up(far).start())
+
+        def above():
+            self.came_z(far + 3).wait_recv()
+            if far < self.n - 1:
+                pl.when(self.head > 0)(lambda: self.down(far).start())
+
+        pl.when(self.there(far))(below)
+        pl.when(self.there(far + 3))(above)
+
+    def spread(self, index):
+        def action(way):
+            self.over_x(way).start()
+            self.over_y(way).start()
+            self.across(0, way).start()
+
+        self.each(index, action)
+
+    def take_xy(self, index):
+        def action(way):
+            self.over_x(way).wait_recv()
+            self.onward(way, 0).start()
+            self.over_y(way).wait_recv()
+            self.onward(way, 1).start()
+            self.across(1, way).start()
+            self.across(2, way).start()
+
+        self.each(index, action)
+
+    def take_far(self, index):
+        def action(way):
+            self.onward(way, 0).wait_recv()
+            self.onward(way, 1).wait_recv()
+            self.across(3, way).start()
+
+        self.each(index, action)
 
     def end(self):
         self.local().wait()
@@ -211,7 +221,10 @@
                     copy.wait_send()
                     copy.wait_recv()
 
-            self.when(way, action)
+            if way == 0:
+                action()
+            else:
+                pl.when(self.there(way))(action)
 
 
 def front_kernel(n_head, n_seq, gather, *refs):
@@ -306,7 +319,8 @@
 
     apply(wqe_ref, qt_ref, slice(0, rows))
     if gather:
-        g.take_z(1, 4)
+        g.take_z(1)
+        g.spread(1)
     loads[5].wait()
     stores[0].start()
     apply(wk_ref, ke_ref, own)
@@ -342,38 +356,39 @@
             total_ref[head, :, q_part] = t
             acc_ref[part, q_part] = a
 
-    def own_block(index, carry):
-        if gather:
-            for at, step in (
-                (1, lambda: g.take_xy(0)),
-                (2, lambda: (g.take_z(2, 5), send_halo())),
-                (3, lambda: g.take_xy(1, 4)),
-                (5, lambda: g.take_z(3, 6)),
-                (6, lambda: g.take_far(0)),
-                (8, lambda: g.take_xy(2, 5)),
-                (10, lambda: g.take_far(1, 4)),
-                (13, lambda: g.take_xy(3, 6)),
-            ):
-
-                @pl.when(index == at)
-                def _():
-                    step()
-
-        tile, at = (index + 1) // 4, (index + 1) % 4
-        block(tile, at + 1 + (tile + 1) // 2)
-        return carry
-
-    def left_block(index, carry):
-        block(index // 2, (index + 1) // 2)
-        return carry
-
-    def right_block(index, carry):
-        if gather:
-            pl.when(index == 0)(lambda: g.take_far(3, 6))
-        block(2 + (index + 1) // 2, 6 + index // 2)
-        return carry
-
-    lax.fori_loop(0, 14, own_block, 0)
+    steps = {}
+    if gather:
+        steps = {
+            0: lambda: (g.take_xy(0),),
+            2: lambda: (g.take_z(2), g.spread(2),),
+            4: lambda: (send_halo(), g.take_xy(1),),
+            7: lambda: (g.take_z(3), g.spread(3), g.take_far(0),),
+            10: lambda: (g.take_xy(2),),
+            12: lambda: (g.take_far(1),),
+            14: lambda: (g.take_xy(3),),
+            16: lambda: (g.take_far(2),),
+            18: lambda: (g.take_far(3),),
+        }
+
+    def blocks(first, last, place):
+        def one(index, carry):
+            for at in steps:
+                if first <= at < last:
+
+                    @pl.when(index == at)
+                    def _():
+                        steps[at]()
+
+            block(*place(index))
+            return carry
+
+        lax.fori_loop(first, last, one, 0)
+
+    def own_place(index):
+        tile = (index + 1) // 4
+        return tile, (index + 1) % 4 + 1 + (tile + 1) // 2
+
+    blocks(0, 14, own_place)
 
     for absent, copy, side_ref, flat_ref, base in (
         (first_z, to_right, xl_ref, lt_ref, 0),
@@ -405,10 +420,8 @@
 
     for n in (1, 2, 4, 5):
         stores[n].start()
-    if gather:
-        g.take_far(2, 5)
-    lax.fori_loop(0, 3, left_block, 0)
-    lax.fori_loop(0, 3, right_block, 0)
+    blocks(14, 17, lambda index: ((index - 14) // 2, (index - 13) // 2))
+    blocks(17, 20, lambda index: (2 + (index - 16) // 2, 6 + (index - 17) // 2))
 
     for head in range(heads):
         part = pl.ds(head * HEAD_DIM, HEAD_DIM)
@@ -425,14 +438,14 @@
 
 
 def attend_back_kernel(
-    shift_ref, len_ref, qt_ref, ke_ref, ve_ref, ls_ref, gt_ref, dl_ref,
+    len_ref, qt_ref, ke_ref, ve_ref, ls_ref, gt_ref, dl_ref,
     dq_ref, dk_ref, dv_ref,
     dq_acc, dk_acc, dv_acc, bias_ref,
 ):
     width, rows = qt_ref.shape
     extent = ke_ref.shape[1]
     heads = width // HEAD_DIM
-    shift = shift_ref[0]
+    shift = lax.axis_index("head") * rows - SEQ_MOST
     dk_acc[...] = jnp.zeros_like(dk_acc)
     dv_acc[...] = jnp.zeros_like(dv_acc)
 
@@ -561,19 +574,24 @@
     big, refs = refs[:12], refs[12:]
     vectors, refs = refs[:4], refs[4:]
     query_scale, query_bias, value_scale, value_bias = [ref[...].reshape(1, -1) for ref in vectors]
-    (out_ref, gqs_ref, gqb_ref, gvs_ref, gvb_ref), refs = refs[:5], refs[5:]
+    (own_hbm, from_left, from_right, sum_ref), refs = refs[:4], refs[4:]
     held, refs = refs[:12], refs[12:]
     (
-        load_sem, own_ref, mix_ref, send_left, send_right, from_left, from_right, halo_sem,
-        z_slots, s_slots, z_sem, s_sem,
+        load_sem, own_ref, mix_ref, send_left, send_right, halo_sem, z_slots, s_slots, z_sem, s_sem,
     ) = refs
-    loads = [pltpu.make_async_copy(src, dst, load_sem.at[n]) for n, (src, dst) in enumerate(zip(big, held))]
-    for load in loads:
-        load.start()
     dk_ref, dv_ref, wk_ref, wve_ref, xt_ref, dq_ref, lt_ref, rt_ref, down_ref, up_ref, wqe_ref, gf_ref = held
     width, rows = dq_ref.shape
     rank = up_ref.shape[0]
     own = slice(SEQ_MOST, SEQ_MOST + rows)
+    sides = (slice(0, SEQ_MOST), slice(SEQ_MOST + rows, 2 * SEQ_MOST + rows))
+    pieces = [(wk_ref, big[2]), (wve_ref, big[3])]
+    pieces += [(ref.at[:, side], hbm.at[:, side]) for side in sides for ref, hbm in zip(held[:2], big[:2])]
+    pieces += [(dq_ref, big[5]), (xt_ref, big[4]), (down_ref, big[8]), (up_ref, big[9])]
+    pieces += [(lt_ref, big[6]), (rt_ref, big[7]), (dv_ref.at[:, own], big[1].at[:, own])]
+    pieces += [(dk_ref.at[:, own], big[0].at[:, own]), (wqe_ref, big[10]), (gf_ref, big[11])]
+    loads = [pltpu.make_async_copy(src, dst, load_sem.at[n]) for n, (dst, src) in enumerate(pieces)]
+    for load in loads:
+        load.start()
     seq, head_at = lax.axis_index("seq"), lax.axis_index("head")
 
     barrier = pltpu.get_barrier_semaphore()
@@ -582,43 +600,42 @@
     for partner in partners:
         pl.semaphore_signal(barrier, inc=1, device_id=partner, device_id_type=MESH)
     pl.semaphore_wait(barrier, len(partners))
-
-    for load in loads[:4]:
-        load.wait()
-
-    def edge(index, carry):
-        part = span(index, 256)
-        for side_ref, base in ((send_left, 0), (send_right, SEQ_MOST + rows)):
-            side = slice(base, base + SEQ_MOST)
-            side_ref[part, :] = (
-                dot(wk_ref[part, :], dk_ref[:, side], NN) + dot(wve_ref[part, :], dv_ref[:, side], NN)
-            ).astype(BF16)
-        return carry
-
-    lax.fori_loop(0, width // 256, edge, 0)
+    first_z, last_z = head_at == 0, head_at == n_head - 1
     to_left = remote(
         send_left, from_right, halo_sem.at[0], halo_sem.at[1], seq, (head_at + n_head - 1) % n_head
     )
     to_right = remote(send_right, from_left, halo_sem.at[2], halo_sem.at[3], seq, (head_at + 1) % n_head)
-    first_z, last_z = head_at == 0, head_at == n_head - 1
-
-    @pl.when(jnp.logical_not(first_z))
-    def _():
-        to_left.start()
-
-    @pl.when(jnp.logical_not(last_z))
-    def _():
-        to_right.start()
+
+    for side_ref, side, absent, copy, waits in (
+        (send_left, sides[0], first_z, to_left, loads[:4]),
+        (send_right, sides[1], last_z, to_right, loads[4:6]),
+    ):
+        for load in waits:
+            load.wait()
+
+        def edge(index, carry):
+            part = span(index, 256)
+            side_ref[part, :] = (
+                dot(wk_ref[part, :], dk_ref[:, side], NN) + dot(wve_ref[part, :], dv_ref[:, side], NN)
+            ).astype(BF16)
+            return carry
+
+        lax.fori_loop(0, width // 256, edge, 0)
+        pl.when(jnp.logical_not(absent))(copy.start)
 
     places, depth = pack((rank, width, rank, width))
     z_slots[head_at] = jnp.zeros_like(z_slots[0])
-    for load in loads[4:10]:
+    for load in loads[6:10]:
         load.wait()
 
     for value in (False, True):
         scale_row, bias = (value_scale, value_bias) if value else (query_scale, query_bias)
         factor = 1.0 if value else QUERY_FOLD
         scale_at, bias_at = places[2 * value], places[2 * value + 1]
+
+        if value:
+            for load in loads[10:13]:
+                load.wait()
 
         def outer(index, carry):
             part = span(index, 256)
@@ -663,7 +680,7 @@
 
     for k in range(1, n_head):
         over_z(k).start()
-    for load in loads[10:]:
+    for load in loads[13:]:
         load.wait()
 
     def tokens_part(index, carry):
@@ -686,48 +703,43 @@
     for k in range(1, n_seq):
         over_seq(k).start()
 
-    for absent, copy, side_ref, base in (
-        (first_z, to_right, from_left, 0),
-        (last_z, to_left, from_right, rows - SEQ_MOST),
-    ):
-
-        @pl.when(absent)
-        def _():
-            side_ref[...] = jnp.zeros_like(side_ref)
-
-        @pl.when(jnp.logical_not(absent))
-        def _():
-            copy.wait_recv()
-
-        def finish(index, carry):
-            part = span(index, 256)
-            at = pl.ds(pl.multiple_of(base + index * 256, 256), 256)
-            out_ref[at, :] = (own_ref[:, at] + side_ref[:, part].astype(F32)).T.astype(BF16)
-            return carry
-
-        lax.fori_loop(0, SEQ_MOST // 256, finish, 0)
-
+    out = pltpu.make_async_copy(own_ref, own_hbm, load_sem.at[len(pieces)])
+    out.start()
     for k in range(1, n_seq):
         over_seq(k).wait_recv()
     total = s_slots[0]
     for k in range(1, n_seq):
         total = total + s_slots[k]
-    for vector_ref, place in zip((gqs_ref, gqb_ref, gvs_ref, gvb_ref), places):
-        for row, start, size in place:
-            vector_ref[start : start + size] = total[row, :size]
-
-    @pl.when(jnp.logical_not(first_z))
-    def _():
-        to_left.wait_send()
-
-    @pl.when(jnp.logical_not(last_z))
-    def _():
-        to_right.wait_send()
-
+    sum_ref[...] = total
+    for absent, back, copy in ((first_z, to_right, to_left), (last_z, to_left, to_right)):
+
+        @pl.when(jnp.logical_not(absent))
+        def _():
+            back.wait_recv()
+            copy.wait_send()
+
+    out.wait()
     for k in range(1, n_head):
         over_z(k).wait_send()
     for k in range(1, n_seq):
         over_seq(k).wait_send()
+
+
+def finish_kernel(n_head, own_ref, left_ref, right_ref, sum_ref, out_ref, *vector_refs):
+    tile, half = pl.program_id(0), pl.num_programs(0) // 2
+    first_z = lax.axis_index("head") == 0
+    last_z = lax.axis_index("head") == n_head - 1
+    left = jnp.where(first_z, 0.0, left_ref[...].astype(F32))
+    right = jnp.where(last_z, 0.0, right_ref[...].astype(F32))
+    total = own_ref[...] + jnp.where(tile < half, left, right)
+    out_ref[...] = total.T.astype(BF16)
+
+    @pl.when(tile == 0)
+    def _():
+        places, _ = pack([ref.shape[0] for ref in vector_refs])
+        for vector_ref, place in zip(vector_refs, places):
+            for row, start, size in place:
+                vector_ref[start : start + size] = sum_ref[row, :size]
 
 
 def call(kernel, outs, count, scratch=(), scalars=0):
@@ -810,7 +822,7 @@
     )(xt, ct, cotangent, w_output, weights)
 
 
-def attend_back(shift, lengths, qt, ke, ve, ls, gc, dl):
+def attend_back(lengths, qt, ke, ve, ls, gc, dl):
     width, rows = qt.shape
     extent = ke.shape[1]
     wide = sds((width, extent), BF16)
@@ -824,28 +836,30 @@
             pltpu.VMEM((width, extent), F32),
             pltpu.VMEM((TILE_K, TILE_Q), F32),
         ],
-        2,
-    )(shift, lengths, qt, ke, ve, ls, gc, dl)
+        1,
+    )(lengths, qt, ke, ve, ls, gc, dl)
 
 
 def tail(n_head, n_seq, big, small):
     dq, up = big[5], big[9]
     width, rows = dq.shape
     rank = up.shape[0]
-    depth = -(-pack((rank, width, rank, width))[1] // 8) * 8
-    half = pltpu.VMEM((width, SEQ_MOST), BF16)
-    outs = [sds((rows, width), BF16)] + [sds((size,), F32) for size in (rank, width, rank, width)]
-    return pl.pallas_call(
+    sizes = (rank, width, rank, width)
+    depth = -(-pack(sizes)[1] // 8) * 8
+    half = sds((width, SEQ_MOST), BF16)
+    outs = [sds((width, rows), F32), half, half, sds((depth, PACK), F32)]
+    own, left, right, total = pl.pallas_call(
         functools.partial(tail_kernel, n_head, n_seq),
         out_shape=outs,
         in_specs=[ANY] * len(big) + [VMEM] * len(small),
-        out_specs=[VMEM] * len(outs),
+        out_specs=[ANY] * 3 + [VMEM],
         scratch_shapes=[pltpu.VMEM(a.shape, a.dtype) for a in big]
         + [
-            pltpu.SemaphoreType.DMA((len(big),)),
+            pltpu.SemaphoreType.DMA((17,)),
             pltpu.VMEM((width, rows), F32),
             pltpu.VMEM((width, width), BF16),
-            half, half, half, half,
+            pltpu.VMEM(half.shape, BF16),
+            pltpu.VMEM(half.shape, BF16),
             pltpu.SemaphoreType.DMA((4,)),
             pltpu.VMEM((n_head, depth, PACK), F32),
             pltpu.VMEM((n_seq, depth, PACK), F32),
@@ -856,6 +870,22 @@
             vmem_limit_bytes=58 << 20, collective_id=1, has_side_effects=True
         ),
     )(*big, *small)
+    tile = 256
+    edge = SEQ_MOST // tile
+    away = rows // tile - edge
+    return pl.pallas_call(
+        functools.partial(finish_kernel, n_head),
+        grid=(rows // tile,),
+        out_shape=[sds((rows, width), BF16)] + [sds((size,), F32) for size in sizes],
+        in_specs=[
+            pl.BlockSpec((width, tile), lambda i: (0, i)),
+            pl.BlockSpec((width, tile), lambda i: (0, jnp.minimum(i, edge - 1))),
+            pl.BlockSpec((width, tile), lambda i: (0, jnp.maximum(i - away, 0))),
+            VMEM,
+        ],
+        out_specs=[pl.BlockSpec((tile, width), lambda i: (i, 0))] + [VMEM] * 4,
+        compiler_params=PARAMS,
+    )(own, left, right, total)
 
 
 def body(n_seq, n_head, *arrays):
@@ -864,7 +894,6 @@
         query_scale, query_bias, value_scale, value_bias, hidden_in, hidden_out,
     ) = arrays
     rows, width = tokens.shape
-    shift = (lax.axis_index("head") * rows - SEQ_MOST).astype(jnp.int32).reshape(1)
     vera = (vera_down, vera_up, query_scale, query_bias, value_scale, value_bias)
     fused = (n_seq, n_head) == (8, 4)
     shards = (hidden_in.T, hidden_out.T) if fused else ()
@@ -878,7 +907,7 @@
             jnp.stack([hidden_in.T, hidden_out.T]), ("seq", "head"), axis=1, tiled=True
         )
     layer_out, gf, gc, dl = feed(xt, ct, cotangent, w_output, weights)
-    dq, dk, dv = attend_back(shift, lengths, qt, ke, ve, ls, gc, dl)
+    dq, dk, dv = attend_back(lengths, qt, ke, ve, ls, gc, dl)
     token_grad, *totals = tail(
         n_head, n_seq, (dk, dv, w_key, wve, xt, dq, lt, rt, vera_down, vera_up, wqe, gf), vera[2:]
     )

time: 181 us -> 171 us (0.945)
  Pallas kernels: 175 us -> 169 us
  local copies, waits for them, and re-layouts: 5.04 us -> 0 us
    pallas_call x1, Pallas kernels: 45.2 us -> 33.2 us  [tail(): pl.pallas_call(functools.partial(tail_kernel, n_head, n_seq), out_shape=o...]
    unnamed x13 -> x0, local copies, waits for them, and re-layouts: 5.04 us -> none
    pallas_call x0 -> x1, Pallas kernels: none -> 4.69 us  [tail(): pl.pallas_call(functools.partial(finish_kernel, n_head), grid=(rows // ti...]
    pallas_call x1, Pallas kernels: 33.1 us -> 35.4 us  [attend_back(): call(attend_back_kernel, [sds((width, rows), BF16), wide, wide], 6, [pltp...]
where the time goes in v4:
time: 171 us; the launch traced here: 170 us
  Pallas kernels  169 us (99%)
    pallas_call x1, Pallas kernels, front(): pl.pallas_call(functools.partial(front_kernel, n_head, n_seq, gather), ou...  59.5 us
    pallas_call x1, Pallas kernels, feed(): pl.pallas_call(feed_kernel, grid=(rows // tile,), out_shape=[sds((rows, w...  36.7 us
    pallas_call x1, Pallas kernels, attend_back(): call(attend_back_kernel, [sds((width, rows), BF16), wide, wide], 6, [pltp...  35.4 us
    pallas_call x1, Pallas kernels, tail(): pl.pallas_call(functools.partial(tail_kernel, n_head, n_seq), out_shape=o...  33.2 us
    pallas_call x1, Pallas kernels, tail(): pl.pallas_call(functools.partial(finish_kernel, n_head), grid=(rows // ti...  4.69 us

profile of v4, /device:TPU:0, one launch (start us, length us, event | category | flops | bytes accessed | tf_op | source)
XLA Modules:
  0.0 170.3 jit_solution(2019958853024348534)
XLA Ops:
  0.6 59.5 %shard_map.190 = (bf16[768,1024]{1,0:T(8,128)(2,1)}, f32[12,1,1024]{2,1,0:T(1,128)}, bf16[768,1024]{1,0:T(8,128)(2,1)}, bf16[768,2048]{1,0:T(8,128)(2,1)}, bf16[...) custom-call(bf16[1024,768]{1,0:T(8,128)(2,1)} %refs_0_.1, ...), custom_call_target="tpu_custom_call" | custom-call | tf_op jit(solution)/shard_map/pallas_call | solution.py:785
  60.2 36.7 %shard_map.191 = (bf16[1024,768]{1,0:T(8,128)(2,1)}, f32[768,1024]{1,0:T(8,128)}, bf16[768,1024]{1,0:T(8,128)(2,1)}, f32[12,1,1024]{2,1,0:T(1,128)}) custom-call(bf16[768,1024]{1,0:T(8,128)(2,1)} %get-tuple-element.33.xt_ref.refs_4_, bf16[768,1024]{1,0:T(8,128)(2,1)} %get-tuple-element.34.ct_ref, bf16[1024,768]{1,0:T(8,128)(2,1)} %cot_ref.1, ...), custom_call_target="tpu_custom_call" | custom-call | tf_op jit(solution)/shard_map/pallas_call | solution.py:804
  96.9 35.4 %shard_map.192 = (bf16[768,1024]{1,0:T(8,128)(2,1)}, bf16[768,2048]{1,0:T(8,128)(2,1)}, bf16[768,2048]{1,0:T(8,128)(2,1)}) custom-call(s32[1,32]{1,0:T(1,128)} %len_ref.1, bf16[768,1024]{1,0:T(8,128)(2,1)} %get-tuple-element.37.qt_ref, bf16[768,2048]{1,0:T(8,128)(2,1)} %get-tuple-element.38.ke_ref, bf16[768,2048]{1,0:T(8,128)(2,1)} %get-tuple-element.39.ve_ref, ...), custom_call_target="tpu_custom_call" | custom-call | tf_op jit(solution)/shard_map/pallas_call | solution.py:829
  132.3 33.2 %shard_map.193 = (f32[768,1024]{1,0:T(8,128)}, bf16[768,512]{1,0:T(8,128)(2,1)}, bf16[768,512]{1,0:T(8,128)(2,1)}, f32[8,512]{1,0:T(8,128)}) custom-call(bf16[768,2048]{1,0:T(8,128)(2,1)} %get-tuple-element.43.refs_0_, bf16[768,2048]{1,0:T(8,128)(2,1)} %get-tuple-element.44.refs_1_, bf16[768,768]{1,0:T(8,128)(2,1)} %refs_2_.3, ...), custom_call_target="tpu_custom_call" | custom-call | tf_op jit(solution)/shard_map/pallas_call | solution.py:851
  165.4 4.7 %shard_map.194 = (bf16[1024,768]{1,0:T(8,128)(2,1)}, f32[1024]{0:T(1024)}, f32[768]{0:T(1024)}, f32[1024]{0:T(1024)}, f32[768]{0:T(1024)}) custom-call(f32[768,1024]{1,0:T(8,128)} %get-tuple-element.51.own_ref, bf16[768,512]{1,0:T(8,128)(2,1)} %get-tuple-element.52.left_ref, bf16[768,512]{1,0:T(8,128)(2,1)} %get-tuple-element.53.right_ref, ...), custom_call_target="tpu_custom_call" | custom-call | tf_op jit(solution)/shard_map/pallas_call | solution.py:876

commit v5 on v4

--- a/solution.py
+++ b/solution.py
@@ -11,7 +11,7 @@
 HEAD_DIM = 64
 SEQ_MOST = 512
 EPSILON = 1e-05
-HIDDEN = -1e30
+HIDDEN = -(2.0**100)
 LN2 = math.log(2.0)
 QUERY_FOLD = HEAD_DIM ** (-0.5) / LN2
 TILE_Q = 256
@@ -56,6 +56,16 @@
     return low, high
 
 
+def fill_masks(len_ref, shift, query_mask, key_mask):
+    for ref, first, within, outside in ((query_mask, shift + SEQ_MOST, HIDDEN, 0.0), (key_mask, shift, 0.0, 1.0)):
+        row = first + lax.broadcasted_iota(jnp.int32, (1, ref.shape[1]), 1)
+        end, pieces = 0, []
+        for i in range(ref.shape[0]):
+            start, end = end, end + len_ref[0, i]
+            pieces.append(jnp.where((row >= start) & (row < end), within, outside))
+        ref[...] = jnp.concatenate(pieces, axis=0).astype(BF16)
+
+
 def reach(len_ref, first, count):
     last = first + count - 1
     end, least, most = 0, 0, 1 << 30
@@ -239,9 +249,9 @@
     held, refs = refs[:6], refs[6:]
     kept, refs = refs[:8], refs[8:]
     (
-        xl_ref, xr_ref, acc_ref, high_ref, total_ref, low_row, high_row, bias_ref,
+        xl_ref, xr_ref, acc_ref, high_ref, total_ref, query_mask, key_mask,
         load_sem, store_sem, halo_sem,
-    ), refs = refs[:11], refs[11:]
+    ), refs = refs[:10], refs[10:]
     x_hbm = big[0]
     loads = [pltpu.make_async_copy(src, dst, load_sem.at[n]) for n, (src, dst) in enumerate(zip(big, held))]
     stores = [pltpu.make_async_copy(src, dst, store_sem.at[n]) for n, (src, dst) in enumerate(zip(kept, stored))]
@@ -326,23 +336,26 @@
     apply(wk_ref, ke_ref, own)
     apply(wve_ref, ve_ref, own)
 
-    low, high = bounds(len_ref, shift + SEQ_MOST, rows)
-    low_row[...] = low
-    high_row[...] = high
+    fill_masks(len_ref, shift, query_mask, key_mask)
     acc_ref[...] = jnp.zeros_like(acc_ref)
     high_ref[...] = jnp.full_like(high_ref, HIDDEN)
     total_ref[...] = jnp.zeros_like(total_ref)
 
     def block(tile, key_tile):
         q_part, k_part = span(tile, TILE_Q), span(key_tile, TILE_K)
-        key = shift + key_tile * TILE_K + lax.broadcasted_iota(jnp.int32, (TILE_K, TILE_Q), 0)
-        bias_ref[...] = jnp.where((key >= low_row[:, q_part]) & (key < high_row[:, q_part]), 0.0, HIDDEN)
-        bias = bias_ref[...]
+        q_mask, k_mask = query_mask[:, q_part], key_mask[:, k_part]
         parts = [span(head, HEAD_DIM) for head in range(heads)]
         before = [high_ref[head, :, q_part] for head in range(heads)]
         totals = [total_ref[head, :, q_part] for head in range(heads)]
         sums = [acc_ref[part, q_part] for part in parts]
-        scores = [dot(ke_ref[part, k_part], qt_ref[part, q_part], TN) + bias for part in parts]
+        scores = [
+            dot(
+                jnp.concatenate([ke_ref[part, k_part], k_mask]),
+                jnp.concatenate([qt_ref[part, q_part], q_mask]),
+                TN,
+            )
+            for part in parts
+        ]
         best = [jnp.maximum(b, jnp.max(v, axis=0, keepdims=True)) for b, v in zip(before, scores)]
         probs = [jnp.exp2(v - b) for v, b in zip(scores, best)]
         fade = [jnp.exp2(a - b) for a, b in zip(before, best)]
@@ -438,16 +451,39 @@
 
 
 def attend_back_kernel(
-    len_ref, qt_ref, ke_ref, ve_ref, ls_ref, gt_ref, dl_ref,
-    dq_ref, dk_ref, dv_ref,
-    dq_acc, dk_acc, dv_acc, bias_ref,
+    len_ref, qt_hbm, ke_hbm, ve_hbm, ls_ref, gt_hbm, dl_ref,
+    dq_hbm, dk_hbm, dv_hbm,
+    qt_ref, ke_ref, ve_ref, gt_ref, dq_ref, dk_ref, dv_ref,
+    dq_acc, dk_acc, dv_acc, bias_ref, load_sem, store_sem,
 ):
     width, rows = qt_ref.shape
     extent = ke_ref.shape[1]
     heads = width // HEAD_DIM
     shift = lax.axis_index("head") * rows - SEQ_MOST
+    loads = [
+        pltpu.make_async_copy(src, dst, load_sem.at[n])
+        for n, (src, dst) in enumerate(((ke_hbm, ke_ref), (qt_hbm, qt_ref), (ve_hbm, ve_ref), (gt_hbm, gt_ref)))
+    ]
+    for load in loads:
+        load.start()
+
+    def store(kind, tile):
+        src, dst = ((dq_ref, dq_hbm), (dk_ref, dk_hbm), (dv_ref, dv_hbm))[kind]
+        part = span(tile, TILE_Q)
+        return pltpu.make_async_copy(src.at[:, part], dst.at[:, part], store_sem.at[kind, tile])
+
+    def settle(tile, carry):
+        part = span(tile, TILE_Q)
+        dk_ref[:, part] = (dk_acc[:, part] * LN2).astype(BF16)
+        dv_ref[:, part] = dv_acc[:, part].astype(BF16)
+        store(1, tile).start()
+        store(2, tile).start()
+        return carry
+
     dk_acc[...] = jnp.zeros_like(dk_acc)
     dv_acc[...] = jnp.zeros_like(dv_acc)
+    for load in loads:
+        load.wait()
 
     def query_tile(tile, carry):
         first = shift + SEQ_MOST + tile * TILE_Q
@@ -485,11 +521,20 @@
 
         lax.fori_loop(0, tiles, key_tile, 0)
         dq_ref[:, q_part] = (dq_acc[...] * LN2).astype(BF16)
+        store(0, tile).start()
+        settle(tile, 0)
         return carry
 
+    def drain(tile, carry):
+        store(1, tile).wait()
+        store(2, tile).wait()
+        return carry
+
     lax.fori_loop(0, rows // TILE_Q, query_tile, 0)
-    dk_ref[...] = (dk_acc[...] * LN2).astype(BF16)
-    dv_ref[...] = dv_acc[...].astype(BF16)
+    lax.fori_loop(rows // TILE_Q, extent // TILE_Q, settle, 0)
+    for tile in range(rows // TILE_Q):
+        store(0, tile).wait()
+    lax.fori_loop(0, extent // TILE_Q, drain, 0)
 
 
 def norm(values):
@@ -590,7 +635,7 @@
     pieces += [(lt_ref, big[6]), (rt_ref, big[7]), (dv_ref.at[:, own], big[1].at[:, own])]
     pieces += [(dk_ref.at[:, own], big[0].at[:, own]), (wqe_ref, big[10]), (gf_ref, big[11])]
     loads = [pltpu.make_async_copy(src, dst, load_sem.at[n]) for n, (dst, src) in enumerate(pieces)]
-    for load in loads:
+    for load in loads[:6]:
         load.start()
     seq, head_at = lax.axis_index("seq"), lax.axis_index("head")
 
@@ -601,30 +646,35 @@
         pl.semaphore_signal(barrier, inc=1, device_id=partner, device_id_type=MESH)
     pl.semaphore_wait(barrier, len(partners))
     first_z, last_z = head_at == 0, head_at == n_head - 1
-    to_left = remote(
-        send_left, from_right, halo_sem.at[0], halo_sem.at[1], seq, (head_at + n_head - 1) % n_head
-    )
-    to_right = remote(send_right, from_left, halo_sem.at[2], halo_sem.at[3], seq, (head_at + 1) % n_head)
-
-    for side_ref, side, absent, copy, waits in (
-        (send_left, sides[0], first_z, to_left, loads[:4]),
-        (send_right, sides[1], last_z, to_right, loads[4:6]),
-    ):
-        for load in waits:
-            load.wait()
-
-        def edge(index, carry):
-            part = span(index, 256)
+
+    def to_left(piece):
+        part = span(piece, 256)
+        sems = halo_sem.at[2 * piece], halo_sem.at[2 * piece + 1]
+        return remote(send_left.at[part], from_right.at[part], *sems, seq, (head_at + n_head - 1) % n_head)
+
+    def to_right(piece):
+        part = span(piece, 256)
+        piece += width // 256
+        sems = halo_sem.at[2 * piece], halo_sem.at[2 * piece + 1]
+        return remote(send_right.at[part], from_left.at[part], *sems, seq, (head_at + 1) % n_head)
+
+    for load in loads[:6]:
+        load.wait()
+    for load in loads[6:]:
+        load.start()
+    for piece in range(width // 256):
+        part = span(piece, 256)
+        for side_ref, side, absent, copy in (
+            (send_left, sides[0], first_z, to_left(piece)),
+            (send_right, sides[1], last_z, to_right(piece)),
+        ):
             side_ref[part, :] = (
                 dot(wk_ref[part, :], dk_ref[:, side], NN) + dot(wve_ref[part, :], dv_ref[:, side], NN)
             ).astype(BF16)
-            return carry
-
-        lax.fori_loop(0, width // 256, edge, 0)
-        pl.when(jnp.logical_not(absent))(copy.start)
+            pl.when(jnp.logical_not(absent))(copy.start)
 
     places, depth = pack((rank, width, rank, width))
-    z_slots[head_at] = jnp.zeros_like(z_slots[0])
+    s_slots[seq] = jnp.zeros_like(s_slots[0])
     for load in loads[6:10]:
         load.wait()
 
@@ -660,11 +710,11 @@
             for lane in range(LANES, width, LANES):
                 folded = folded + weighted[:, lane : lane + LANES]
             row, column = at // PACK, at % PACK
-            z_slots[head_at, pl.ds(scale_at[row][0], 1), pl.ds(column, 256)] = jnp.sum(
+            s_slots[seq, pl.ds(scale_at[row][0], 1), pl.ds(column, 256)] = jnp.sum(
                 folded.T, axis=0, keepdims=True
             )
         for row, start, size in bias_at:
-            z_slots[head_at, pl.ds(row, 1), pl.ds(0, size)] = bias_sum[:, start : start + size]
+            s_slots[seq, pl.ds(row, 1), pl.ds(0, size)] = bias_sum[:, start : start + size]
 
     def over_z(k):
         return remote(
@@ -678,8 +728,8 @@
             (seq + k) % n_seq, head_at,
         )
 
-    for k in range(1, n_head):
-        over_z(k).start()
+    for k in range(1, n_seq):
+        over_seq(k).start()
     for load in loads[13:]:
         load.wait()
 
@@ -694,29 +744,30 @@
         return carry
 
     lax.fori_loop(0, width // 256, tokens_part, 0)
+    for k in range(1, n_seq):
+        over_seq(k).wait_recv()
+    total = s_slots[0]
+    for k in range(1, n_seq):
+        total = total + s_slots[k]
+    z_slots[head_at] = total
+    for k in range(1, n_head):
+        over_z(k).start()
+
+    out = pltpu.make_async_copy(own_ref, own_hbm, load_sem.at[len(pieces)])
+    out.start()
     for k in range(1, n_head):
         over_z(k).wait_recv()
     total = z_slots[0]
     for k in range(1, n_head):
         total = total + z_slots[k]
-    s_slots[seq] = total
-    for k in range(1, n_seq):
-        over_seq(k).start()
-
-    out = pltpu.make_async_copy(own_ref, own_hbm, load_sem.at[len(pieces)])
-    out.start()
-    for k in range(1, n_seq):
-        over_seq(k).wait_recv()
-    total = s_slots[0]
-    for k in range(1, n_seq):
-        total = total + s_slots[k]
     sum_ref[...] = total
     for absent, back, copy in ((first_z, to_right, to_left), (last_z, to_left, to_right)):
 
         @pl.when(jnp.logical_not(absent))
         def _():
-            back.wait_recv()
-            copy.wait_send()
+            for piece in range(width // 256):
+                back(piece).wait_recv()
+                copy(piece).wait_send()
 
     out.wait()
     for k in range(1, n_head):
@@ -768,9 +819,8 @@
         pltpu.VMEM((width, rows), F32),
         pltpu.VMEM((heads, 1, rows), F32),
         pltpu.VMEM((heads, 1, rows), F32),
-        pltpu.VMEM((1, rows), jnp.int32),
-        pltpu.VMEM((1, rows), jnp.int32),
-        pltpu.VMEM((TILE_K, TILE_Q), F32),
+        pltpu.VMEM((lengths.shape[1], rows), BF16),
+        pltpu.VMEM((lengths.shape[1], extent), BF16),
         pltpu.SemaphoreType.DMA((len(big),)),
         pltpu.SemaphoreType.DMA((len(kept),)),
         pltpu.SemaphoreType.DMA((4,)),
@@ -825,18 +875,22 @@
 def attend_back(lengths, qt, ke, ve, ls, gc, dl):
     width, rows = qt.shape
     extent = ke.shape[1]
-    wide = sds((width, extent), BF16)
-    return call(
+    outs = [sds((width, rows), BF16), sds(ke.shape, BF16), sds(ke.shape, BF16)]
+    return pl.pallas_call(
         attend_back_kernel,
-        [sds((width, rows), BF16), wide, wide],
-        6,
-        [
+        out_shape=outs,
+        in_specs=[SMEM, ANY, ANY, ANY, VMEM, ANY, VMEM],
+        out_specs=[ANY] * 3,
+        scratch_shapes=[pltpu.VMEM(a.shape, BF16) for a in (qt, ke, ve, gc, *outs)]
+        + [
             pltpu.VMEM((width, TILE_Q), F32),
             pltpu.VMEM((width, extent), F32),
             pltpu.VMEM((width, extent), F32),
             pltpu.VMEM((TILE_K, TILE_Q), F32),
+            pltpu.SemaphoreType.DMA((4,)),
+            pltpu.SemaphoreType.DMA((3, extent // TILE_Q)),
         ],
-        1,
+        compiler_params=PARAMS,
     )(lengths, qt, ke, ve, ls, gc, dl)
 
 
@@ -860,7 +914,7 @@
             pltpu.VMEM((width, width), BF16),
             pltpu.VMEM(half.shape, BF16),
             pltpu.VMEM(half.shape, BF16),
-            pltpu.SemaphoreType.DMA((4,)),
+            pltpu.SemaphoreType.DMA((4 * (width // 256),)),
             pltpu.VMEM((n_head, depth, PACK), F32),
             pltpu.VMEM((n_seq, depth, PACK), F32),
             pltpu.SemaphoreType.DMA((2 * n_head,)),
@@ -870,7 +924,7 @@
             vmem_limit_bytes=58 << 20, collective_id=1, has_side_effects=True
         ),
     )(*big, *small)
-    tile = 256
+    tile = 512
     edge = SEQ_MOST // tile
     away = rows // tile - edge
     return pl.pallas_call(

time: 171 us -> 163 us (0.953)
  Pallas kernels: 169 us -> 161 us
    pallas_call x1, Pallas kernels: 33.2 us -> 29.5 us  [tail(): pl.pallas_call(functools.partial(tail_kernel, n_head, n_seq), out_shape=o...]
    pallas_call x1, Pallas kernels: 35.4 us -> 32.5 us  [attend_back(): pl.pallas_call(attend_back_kernel, out_shape=outs, in_specs=[SMEM, ANY, A...]
where the time goes in v5:
time: 163 us; the launch traced here: 162 us
  Pallas kernels  161 us (99%)
    pallas_call x1, Pallas kernels, front(): pl.pallas_call(functools.partial(front_kernel, n_head, n_seq, gather), ou...  58.7 us
    pallas_call x1, Pallas kernels, feed(): pl.pallas_call(feed_kernel, grid=(rows // tile,), out_shape=[sds((rows, w...  36.7 us
    pallas_call x1, Pallas kernels, attend_back(): pl.pallas_call(attend_back_kernel, out_shape=outs, in_specs=[SMEM, ANY, A...  32.5 us
    pallas_call x1, Pallas kernels, tail(): pl.pallas_call(functools.partial(tail_kernel, n_head, n_seq), out_shape=o...  29.5 us
    pallas_call x1, Pallas kernels, tail(): pl.pallas_call(functools.partial(finish_kernel, n_head), grid=(rows // ti...  3.76 us

profile of v5, /device:TPU:0, one launch (start us, length us, event | category | flops | bytes accessed | tf_op | source)
XLA Modules:
  0.0 161.9 jit_solution(11777534451086524895)
XLA Ops:
  0.6 58.7 %shard_map.190 = (bf16[768,1024]{1,0:T(8,128)(2,1)}, f32[12,1,1024]{2,1,0:T(1,128)}, bf16[768,1024]{1,0:T(8,128)(2,1)}, bf16[768,2048]{1,0:T(8,128)(2,1)}, bf16[...) custom-call(bf16[1024,768]{1,0:T(8,128)(2,1)} %refs_0_.1, ...), custom_call_target="tpu_custom_call" | custom-call | tf_op jit(solution)/shard_map/pallas_call | solution.py:835
  59.3 36.7 %shard_map.191 = (bf16[1024,768]{1,0:T(8,128)(2,1)}, f32[768,1024]{1,0:T(8,128)}, bf16[768,1024]{1,0:T(8,128)(2,1)}, f32[12,1,1024]{2,1,0:T(1,128)}) custom-call(bf16[768,1024]{1,0:T(8,128)(2,1)} %get-tuple-element.33.xt_ref.refs_4_, bf16[768,1024]{1,0:T(8,128)(2,1)} %get-tuple-element.34.ct_ref, bf16[1024,768]{1,0:T(8,128)(2,1)} %cot_ref.1, ...), custom_call_target="tpu_custom_call" | custom-call | tf_op jit(solution)/shard_map/pallas_call | solution.py:854
  96.0 32.5 %shard_map.192 = (bf16[768,1024]{1,0:T(8,128)(2,1)}, bf16[768,2048]{1,0:T(8,128)(2,1)}, bf16[768,2048]{1,0:T(8,128)(2,1)}) custom-call(s32[1,32]{1,0:T(1,128)} %len_ref.1, bf16[768,1024]{1,0:T(8,128)(2,1)} %get-tuple-element.37.qt_hbm, bf16[768,2048]{1,0:T(8,128)(2,1)} %get-tuple-element.38.ke_hbm, bf16[768,2048]{1,0:T(8,128)(2,1)} %get-tuple-element.39.ve_hbm, ...), custom_call_target="tpu_custom_call" | custom-call | tf_op jit(solution)/shard_map/pallas_call | solution.py:879
  128.5 29.5 %shard_map.193 = (f32[768,1024]{1,0:T(8,128)}, bf16[768,512]{1,0:T(8,128)(2,1)}, bf16[768,512]{1,0:T(8,128)(2,1)}, f32[8,512]{1,0:T(8,128)}) custom-call(bf16[768,2048]{1,0:T(8,128)(2,1)} %get-tuple-element.43.refs_0_, bf16[768,2048]{1,0:T(8,128)(2,1)} %get-tuple-element.44.refs_1_, bf16[768,768]{1,0:T(8,128)(2,1)} %refs_2_.3, ...), custom_call_target="tpu_custom_call" | custom-call | tf_op jit(solution)/shard_map/pallas_call | solution.py:905
  158.0 3.8 %shard_map.194 = (bf16[1024,768]{1,0:T(8,128)(2,1)}, f32[1024]{0:T(1024)}, f32[768]{0:T(1024)}, f32[1024]{0:T(1024)}, f32[768]{0:T(1024)}) custom-call(f32[768,1024]{1,0:T(8,128)} %get-tuple-element.51.own_ref, bf16[768,512]{1,0:T(8,128)(2,1)} %get-tuple-element.52.left_ref, bf16[768,512]{1,0:T(8,128)(2,1)} %get-tuple-element.53.right_ref, ...), custom_call_target="tpu_custom_call" | custom-call | tf_op jit(solution)/shard_map/pallas_call | solution.py:930

commit v6 on v5

--- a/solution.py
+++ b/solution.py
@@ -276,22 +276,30 @@
         pl.semaphore_signal(barrier, inc=1, device_id=partner, device_id_type=MESH)
     pl.semaphore_wait(barrier, len(partners))
 
-    to_right = remote(
-        x_hbm.at[rows - SEQ_MOST :], xl_ref, halo_sem.at[0], halo_sem.at[1], seq, (head_at + 1) % n_head
-    )
-    to_left = remote(
-        x_hbm.at[:SEQ_MOST], xr_ref, halo_sem.at[2], halo_sem.at[3], seq, (head_at + n_head - 1) % n_head
-    )
-
-    def send_halo():
-        pl.when(head_at < n_head - 1)(lambda: to_right.start())
-        pl.when(head_at > 0)(lambda: to_left.start())
+    half = SEQ_MOST // 2
+
+    def to_right(far):
+        at = 0 if far else half
+        sems = halo_sem.at[4 * far], halo_sem.at[4 * far + 1]
+        src = x_hbm.at[pl.ds(rows - SEQ_MOST + at, half)]
+        return remote(src, xl_ref.at[pl.ds(at, half)], *sems, seq, (head_at + 1) % n_head)
+
+    def to_left(far):
+        at = half if far else 0
+        sems = halo_sem.at[4 * far + 2], halo_sem.at[4 * far + 3]
+        src = x_hbm.at[pl.ds(at, half)]
+        return remote(src, xr_ref.at[pl.ds(at, half)], *sems, seq, (head_at + n_head - 1) % n_head)
+
+    def send_halo(far):
+        pl.when(head_at < n_head - 1)(lambda: to_right(far).start())
+        pl.when(head_at > 0)(lambda: to_left(far).start())
 
     if gather:
         g = Gather(own_ref, full_ref, gather_sem, seq, head_at, n_head)
         g.begin()
     else:
-        send_halo()
+        send_halo(0)
+        send_halo(1)
     query_scale, query_bias, value_scale, value_bias = [ref[...].reshape(1, -1) for ref in vectors]
     for n in (1, 2, 3, 4):
         loads[n].wait()
@@ -374,13 +382,15 @@
         steps = {
             0: lambda: (g.take_xy(0),),
             2: lambda: (g.take_z(2), g.spread(2),),
-            4: lambda: (send_halo(), g.take_xy(1),),
+            3: lambda: (send_halo(0),),
+            4: lambda: (g.take_xy(1),),
             7: lambda: (g.take_z(3), g.spread(3), g.take_far(0),),
+            8: lambda: (send_halo(1),),
             10: lambda: (g.take_xy(2),),
             12: lambda: (g.take_far(1),),
-            14: lambda: (g.take_xy(3),),
+            15: lambda: (g.take_xy(3),),
             16: lambda: (g.take_far(2),),
-            18: lambda: (g.take_far(3),),
+            19: lambda: (g.take_far(3),),
         }
 
     def blocks(first, last, place):
@@ -403,38 +413,34 @@
 
     blocks(0, 14, own_place)
 
-    for absent, copy, side_ref, flat_ref, base in (
-        (first_z, to_right, xl_ref, lt_ref, 0),
-        (last_z, to_left, xr_ref, rt_ref, SEQ_MOST + rows),
-    ):
-
-        @pl.when(absent)
-        def _():
-            side_ref[...] = jnp.zeros_like(side_ref)
-
-        @pl.when(jnp.logical_not(absent))
-        def _():
-            copy.wait_recv()
-
-        def edge_flip(index, carry):
-            part = span(index, 256)
-            flat_ref[:, part] = side_ref[part, :].T
-            return carry
-
-        lax.fori_loop(0, SEQ_MOST // 256, edge_flip, 0)
-
-        def edge(index, carry):
-            part = span(index, 256)
-            ke_ref[part, base : base + SEQ_MOST] = dot(wk_ref[:, part], flat_ref[...], TN).astype(BF16)
-            ve_ref[part, base : base + SEQ_MOST] = dot(wve_ref[:, part], flat_ref[...], TN).astype(BF16)
-            return carry
-
-        lax.fori_loop(0, width // 256, edge, 0)
-
+    def take_halo(far):
+        for absent, copy, side_ref, flat_ref, base, at in (
+            (first_z, to_right(far), xl_ref, lt_ref, 0, 0 if far else half),
+            (last_z, to_left(far), xr_ref, rt_ref, SEQ_MOST + rows, half if far else 0),
+        ):
+            piece, place = slice(at, at + half), slice(base + at, base + at + half)
+
+            @pl.when(absent)
+            def _():
+                side_ref[piece, :] = jnp.zeros((half, width), BF16)
+
+            pl.when(jnp.logical_not(absent))(copy.wait_recv)
+            flat_ref[:, piece] = side_ref[piece, :].T
+
+            def edge(index, carry):
+                part = span(index, 256)
+                ke_ref[part, place] = dot(wk_ref[:, part], flat_ref[:, piece], TN).astype(BF16)
+                ve_ref[part, place] = dot(wve_ref[:, part], flat_ref[:, piece], TN).astype(BF16)
+                return carry
+
+            lax.fori_loop(0, width // 256, edge, 0)
+
+    take_halo(0)
+    blocks(14, 18, lambda index: (index - 14, 1 + 5 * ((index - 14) // 2)))
+    take_halo(1)
     for n in (1, 2, 4, 5):
         stores[n].start()
-    blocks(14, 17, lambda index: ((index - 14) // 2, (index - 13) // 2))
-    blocks(17, 20, lambda index: (2 + (index - 16) // 2, 6 + (index - 17) // 2))
+    blocks(18, 20, lambda index: (3 * (index - 18), 7 * (index - 18)))
 
     for head in range(heads):
         part = pl.ds(head * HEAD_DIM, HEAD_DIM)
@@ -442,8 +448,9 @@
         ct_ref[part, :] = (acc_ref[part, :] / total).astype(BF16)
         ls_ref[head] = high_ref[head] + jnp.log2(total)
 
-    pl.when(head_at < n_head - 1)(lambda: to_right.wait_send())
-    pl.when(head_at > 0)(lambda: to_left.wait_send())
+    for far in range(2):
+        pl.when(head_at < n_head - 1)(to_right(far).wait_send)
+        pl.when(head_at > 0)(to_left(far).wait_send)
     for store in stores:
         store.wait()
     if gather:
@@ -650,13 +657,15 @@
     def to_left(piece):
         part = span(piece, 256)
         sems = halo_sem.at[2 * piece], halo_sem.at[2 * piece + 1]
-        return remote(send_left.at[part], from_right.at[part], *sems, seq, (head_at + n_head - 1) % n_head)
+        return remote(
+            send_left.at[:, part], from_right.at[:, part], *sems, seq, (head_at + n_head - 1) % n_head
+        )
 
     def to_right(piece):
         part = span(piece, 256)
         piece += width // 256
         sems = halo_sem.at[2 * piece], halo_sem.at[2 * piece + 1]
-        return remote(send_right.at[part], from_left.at[part], *sems, seq, (head_at + 1) % n_head)
+        return remote(send_right.at[:, part], from_left.at[:, part], *sems, seq, (head_at + 1) % n_head)
 
     for load in loads[:6]:
         load.wait()
@@ -668,9 +677,8 @@
             (send_left, sides[0], first_z, to_left(piece)),
             (send_right, sides[1], last_z, to_right(piece)),
         ):
-            side_ref[part, :] = (
-                dot(wk_ref[part, :], dk_ref[:, side], NN) + dot(wve_ref[part, :], dv_ref[:, side], NN)
-            ).astype(BF16)
+            partial = dot(wk_ref[part, :], dk_ref[:, side], NN) + dot(wve_ref[part, :], dv_ref[:, side], NN)
+            side_ref[:, part] = partial.astype(BF16).T
             pl.when(jnp.logical_not(absent))(copy.start)
 
     places, depth = pack((rank, width, rank, width))
@@ -735,12 +743,13 @@
 
     def tokens_part(index, carry):
         part = span(index, 256)
-        own_ref[part, :] = (
+        total = (
             gf_ref[part, :]
             + dot(wqe_ref[part, :], dq_ref[...], NN)
             + dot(wk_ref[part, :], dk_ref[:, own], NN)
             + dot(wve_ref[part, :], dv_ref[:, own], NN)
         )
+        own_ref[:, part] = total.astype(BF16).T
         return carry
 
     lax.fori_loop(0, width // 256, tokens_part, 0)
@@ -777,13 +786,11 @@
 
 
 def finish_kernel(n_head, own_ref, left_ref, right_ref, sum_ref, out_ref, *vector_refs):
-    tile, half = pl.program_id(0), pl.num_programs(0) // 2
-    first_z = lax.axis_index("head") == 0
-    last_z = lax.axis_index("head") == n_head - 1
-    left = jnp.where(first_z, 0.0, left_ref[...].astype(F32))
-    right = jnp.where(last_z, 0.0, right_ref[...].astype(F32))
-    total = own_ref[...] + jnp.where(tile < half, left, right)
-    out_ref[...] = total.T.astype(BF16)
+    tile, last = pl.program_id(0), pl.num_programs(0) - 1
+    to_first = (tile == 0) & (lax.axis_index("head") > 0)
+    to_last = (tile == last) & (lax.axis_index("head") < n_head - 1)
+    total = own_ref[...].astype(F32) + jnp.where(to_first, left_ref[...].astype(F32), 0.0)
+    out_ref[...] = (total + jnp.where(to_last, right_ref[...].astype(F32), 0.0)).astype(BF16)
 
     @pl.when(tile == 0)
     def _():
@@ -823,7 +830,7 @@
         pltpu.VMEM((lengths.shape[1], extent), BF16),
         pltpu.SemaphoreType.DMA((len(big),)),
         pltpu.SemaphoreType.DMA((len(kept),)),
-        pltpu.SemaphoreType.DMA((4,)),
+        pltpu.SemaphoreType.DMA((8,)),
     ]
     gather = len(shards) > 0
     specs = [VMEM] * 2 + [ANY] * len(kept)
@@ -900,8 +907,8 @@
     rank = up.shape[0]
     sizes = (rank, width, rank, width)
     depth = -(-pack(sizes)[1] // 8) * 8
-    half = sds((width, SEQ_MOST), BF16)
-    outs = [sds((width, rows), F32), half, half, sds((depth, PACK), F32)]
+    half = sds((SEQ_MOST, width), BF16)
+    outs = [sds((rows, width), BF16), half, half, sds((depth, PACK), F32)]
     own, left, right, total = pl.pallas_call(
         functools.partial(tail_kernel, n_head, n_seq),
         out_shape=outs,
@@ -910,7 +917,7 @@
         scratch_shapes=[pltpu.VMEM(a.shape, a.dtype) for a in big]
         + [
             pltpu.SemaphoreType.DMA((17,)),
-            pltpu.VMEM((width, rows), F32),
+            pltpu.VMEM((rows, width), BF16),
             pltpu.VMEM((width, width), BF16),
             pltpu.VMEM(half.shape, BF16),
             pltpu.VMEM(half.shape, BF16),
@@ -924,20 +931,13 @@
             vmem_limit_bytes=58 << 20, collective_id=1, has_side_effects=True
         ),
     )(*big, *small)
-    tile = 512
-    edge = SEQ_MOST // tile
-    away = rows // tile - edge
+    piece = pl.BlockSpec((SEQ_MOST, width), lambda i: (i, 0))
     return pl.pallas_call(
         functools.partial(finish_kernel, n_head),
-        grid=(rows // tile,),
+        grid=(rows // SEQ_MOST,),
         out_shape=[sds((rows, width), BF16)] + [sds((size,), F32) for size in sizes],
-        in_specs=[
-            pl.BlockSpec((width, tile), lambda i: (0, i)),
-            pl.BlockSpec((width, tile), lambda i: (0, jnp.minimum(i, edge - 1))),
-            pl.BlockSpec((width, tile), lambda i: (0, jnp.maximum(i - away, 0))),
-            VMEM,
-        ],
-        out_specs=[pl.BlockSpec((tile, width), lambda i: (i, 0))] + [VMEM] * 4,
+        in_specs=[piece, VMEM, VMEM, VMEM],
+        out_specs=[piece] + [VMEM] * 4,
         compiler_params=PARAMS,
     )(own, left, right, total)
 

time: 163 us -> 160 us (0.982)
  Pallas kernels: 161 us -> 159 us
    pallas_call x1, Pallas kernels: 32.5 us -> 34.8 us  [attend_back(): pl.pallas_call(attend_back_kernel, out_shape=outs, in_specs=[SMEM, ANY, A...]
    pallas_call x1, Pallas kernels: 29.5 us -> 27.3 us  [tail(): pl.pallas_call(functools.partial(tail_kernel, n_head, n_seq), out_shape=o...]
where the time goes in v6:
time: 160 us
  Pallas kernels  159 us (99%)
    pallas_call x1, Pallas kernels, front(): pl.pallas_call(functools.partial(front_kernel, n_head, n_seq, gather), ou...  57.3 us
    pallas_call x1, Pallas kernels, feed(): pl.pallas_call(feed_kernel, grid=(rows // tile,), out_shape=[sds((rows, w...  36.7 us
    pallas_call x1, Pallas kernels, attend_back(): pl.pallas_call(attend_back_kernel, out_shape=outs, in_specs=[SMEM, ANY, A...  34.8 us
    pallas_call x1, Pallas kernels, tail(): pl.pallas_call(functools.partial(tail_kernel, n_head, n_seq), out_shape=o...  27.3 us
    pallas_call x1, Pallas kernels, tail(): pl.pallas_call(functools.partial(finish_kernel, n_head), grid=(rows // SE...  3.33 us

profile of v6, /device:TPU:0, one launch (start us, length us, event | category | flops | bytes accessed | tf_op | source)
XLA Modules:
  0.0 160.2 jit_solution(4222634080337044288)
XLA Ops:
  0.6 57.3 %shard_map.190 = (bf16[768,1024]{1,0:T(8,128)(2,1)}, f32[12,1,1024]{2,1,0:T(1,128)}, bf16[768,1024]{1,0:T(8,128)(2,1)}, bf16[768,2048]{1,0:T(8,128)(2,1)}, bf16[...) custom-call(bf16[1024,768]{1,0:T(8,128)(2,1)} %refs_0_.1, ...), custom_call_target="tpu_custom_call" | custom-call | tf_op jit(solution)/shard_map/pallas_call | solution.py:842
  57.9 36.7 %shard_map.191 = (bf16[1024,768]{1,0:T(8,128)(2,1)}, f32[768,1024]{1,0:T(8,128)}, bf16[768,1024]{1,0:T(8,128)(2,1)}, f32[12,1,1024]{2,1,0:T(1,128)}) custom-call(bf16[768,1024]{1,0:T(8,128)(2,1)} %get-tuple-element.33.xt_ref.refs_4_, bf16[768,1024]{1,0:T(8,128)(2,1)} %get-tuple-element.34.ct_ref, bf16[1024,768]{1,0:T(8,128)(2,1)} %cot_ref.1, ...), custom_call_target="tpu_custom_call" | custom-call | tf_op jit(solution)/shard_map/pallas_call | solution.py:861
  94.6 34.8 %shard_map.192 = (bf16[768,1024]{1,0:T(8,128)(2,1)}, bf16[768,2048]{1,0:T(8,128)(2,1)}, bf16[768,2048]{1,0:T(8,128)(2,1)}) custom-call(s32[1,32]{1,0:T(1,128)} %len_ref.1, bf16[768,1024]{1,0:T(8,128)(2,1)} %get-tuple-element.37.qt_hbm, bf16[768,2048]{1,0:T(8,128)(2,1)} %get-tuple-element.38.ke_hbm, bf16[768,2048]{1,0:T(8,128)(2,1)} %get-tuple-element.39.ve_hbm, ...), custom_call_target="tpu_custom_call" | custom-call | tf_op jit(solution)/shard_map/pallas_call | solution.py:886
  129.4 27.3 %shard_map.193 = (bf16[1024,768]{1,0:T(8,128)(2,1)}, bf16[512,768]{1,0:T(8,128)(2,1)}, bf16[512,768]{1,0:T(8,128)(2,1)}, f32[8,512]{1,0:T(8,128)}) custom-call(bf16[768,2048]{1,0:T(8,128)(2,1)} %get-tuple-element.43.refs_0_, bf16[768,2048]{1,0:T(8,128)(2,1)} %get-tuple-element.44.refs_1_, bf16[768,768]{1,0:T(8,128)(2,1)} %refs_2_.3, ...), custom_call_target="tpu_custom_call" | custom-call | tf_op jit(solution)/shard_map/pallas_call | solution.py:912
  156.7 3.3 %shard_map.194 = (bf16[1024,768]{1,0:T(8,128)(2,1)}, f32[1024]{0:T(1024)}, f32[768]{0:T(1024)}, f32[1024]{0:T(1024)}, f32[768]{0:T(1024)}) custom-call(bf16[1024,768]{1,0:T(8,128)(2,1)} %get-tuple-element.51.own_ref, bf16[512,768]{1,0:T(8,128)(2,1)} %get-tuple-element.52.left_ref, bf16[512,768]{1,0:T(8,128)(2,1)} %get-tuple-element.53.right_ref, ...), custom_call_target="tpu_custom_call" | custom-call | tf_op jit(solution)/shard_map/pallas_call | solution.py:935
